TPU v7x, 32 devices: a whole 2x2x4 slice. The times are simulated.
32 devices in a mesh: seq: 16 (over z, x, core), head: 2 (over y).
Axes of the slice: x: 2, y: 2, z: 4, core: 2. Of those that a mesh axis runs over, the one named last changes fastest.
Arguments:
- tokens: bfloat16 [2048, 768], P(('seq', 'head')), may hold values from -6 to 6
- out_grad: bfloat16 [2048, 768], P(('seq', 'head')), may hold values from -6 to 6
- short_lengths: int32 [3], replicated, may hold values from 1 to 512, 1024 in all
- attn_gain: bfloat16 [768], P(('seq', 'head')), may hold values from 0.099609375 to 1.8984375
- qkv_weight: bfloat16 [768, 3, 768], P('seq', None, 'head'), may hold values from -0.21875 to 0.21875
- out_weight: bfloat16 [768, 768], P('head', 'seq'), may hold values from -2.5 to 2.5
- mlp_gain: bfloat16 [768], P(('seq', 'head')), may hold values from 0.099609375 to 1.8984375
- in_weight: bfloat16 [768, 2, 1152], P('seq', None, 'head'), may hold values from -0.21875 to 0.21875
- down_weight: bfloat16 [1152, 768], P('head', 'seq'), may hold values from -0.1875 to 0.1875
Outputs:
- mixed: bfloat16 [2048, 768], P(('seq', 'head'))
- tokens_grad: float32 [2048, 768], P(('seq', 'head'))
- attn_gain_grad: float32 [768], P(('seq', 'head'))
- qkv_weight_grad: float32 [768, 3, 768], P('seq', None, 'head')
- out_weight_grad: float32 [768, 768], P('head', 'seq')
- mlp_gain_grad: float32 [768], P(('seq', 'head'))
- in_weight_grad: float32 [768, 2, 1152], P('seq', None, 'head')
- down_weight_grad: float32 [1152, 768], P('head', 'seq')
Inputs may be any that keep to these rules, and one draw needn't show every extreme that they name: `short_lengths`: the long document 0 fills the first 1024 rows; the short documents follow in this order, their lengths sum to 1024, and one of them has exactly 512 tokens.
All inputs are finite; a program needn't handle non-finite values.
Results may differ from a plain program's by a relative error of at most 0.02.
Values may be sent and summed in bfloat16 or wider, within the bound.
A program may use at most 192 MiB of HBM per device.

v0:
```python
import math

import jax
import jax.numpy as jnp
from jax import lax
from jax.sharding import PartitionSpec as P

HEAD_DIM = 64


norm_eps = 1e-05
rope_base = 160000.0
score_scale = 0.125
masked_low = -1e30


def layer_norm(inputs, gain_vector):
    row_mean = jnp.mean(inputs, axis=-1, keepdims=True)
    centred = inputs - row_mean
    spread = jnp.mean(centred * centred, axis=-1, keepdims=True)
    return centred * lax.rsqrt(spread + norm_eps) * gain_vector


def doc_layout(short_lengths, row_ids, total_rows):
    long_end = total_rows - jnp.sum(short_lengths)
    before = jnp.cumsum(short_lengths) - short_lengths
    bounds = long_end + before
    passed = row_ids[:, None] >= bounds[None, :]
    doc_ids = jnp.sum(passed.astype(jnp.int32), axis=1)
    starts = jnp.max(jnp.where(passed, bounds[None, :], jnp.zeros_like(bounds)[None, :]), axis=1)
    return (doc_ids, row_ids - starts)


def rope_tables(positions):
    steps_half = jnp.arange(HEAD_DIM // 2, dtype=jnp.float32)
    inverse = jnp.exp(steps_half * (-2.0 * math.log(rope_base) / HEAD_DIM))
    angles = positions.astype(jnp.float32)[:, None] * inverse[None, :]
    cosines = jnp.cos(angles)
    sines = jnp.sin(angles)
    return (jnp.concatenate([cosines, cosines], axis=1), jnp.concatenate([sines, sines], axis=1))


def rotate(heads_in, cosines, sines):
    half_dim = heads_in.shape[-1] // 2
    turned = jnp.concatenate([-heads_in[..., half_dim:], heads_in[..., :half_dim]], axis=-1)
    return heads_in * cosines[:, None, :] + turned * sines[:, None, :]


def block_length(row_count, shard_rows):
    shards = row_count // shard_rows
    return shard_rows * math.gcd(shards, max(1, 1024 // shard_rows))


def over_blocks(carry_state, row_count, shard_rows, block_fn):
    block_size = block_length(row_count, shard_rows)

    def block_step(inner_state, block_index):
        return (block_fn(inner_state, block_index * block_size, block_size), None)

    carry_state, _ = lax.scan(
        block_step, carry_state, jnp.arange(row_count // block_size, dtype=jnp.int32)
    )
    return carry_state


def scores_of(queries, key_part):
    return (
        jnp.einsum("qhd,khd->hqk", queries, key_part, preferred_element_type=jnp.float32)
        * score_scale
    )


def block_grads(queries, grad_rows, log_sums, row_dots, key_part, value_part, same_doc):
    scores = scores_of(queries, key_part)
    softmax_part = jnp.where(same_doc, jnp.exp(scores - log_sums[:, :, None]), 0.0)
    grad_probs = jnp.einsum(
        "qhd,khd->hqk", grad_rows, value_part, preferred_element_type=jnp.float32
    )
    dscore = (softmax_part * (grad_probs - row_dots[:, :, None])).astype(jnp.bfloat16)
    return (softmax_part, dscore)


def on_device(
    tokens,
    out_grad,
    short_lengths,
    attn_gain,
    qkv_weight,
    out_weight,
    mlp_gain,
    in_weight,
    down_weight,
):
    half_rows = tokens.shape[0]
    head_count = lax.axis_size("head")
    seq_count = lax.axis_size("seq")
    block_rows = half_rows * head_count
    total_rows = block_rows * seq_count
    local_ids = lax.axis_index("seq") * block_rows + jnp.arange(block_rows, dtype=jnp.int32)
    local_docs, local_pos = doc_layout(short_lengths, local_ids, total_rows)
    cosines, sines = rope_tables(local_pos)
    qkv_full, out_full = (
        lax.all_gather(qkv_weight, "seq", axis=0, tiled=True),
        lax.all_gather(out_weight, "seq", axis=1, tiled=True),
    )
    gain_first, gain_second, in_parts, down_parts = (
        lax.all_gather(attn_gain, ("seq", "head"), axis=0, tiled=True),
        lax.all_gather(mlp_gain, ("seq", "head"), axis=0, tiled=True),
        lax.all_gather(in_weight[None], ("seq", "head"), axis=0, tiled=True),
        lax.all_gather(down_weight[None], ("seq", "head"), axis=0, tiled=True),
    )
    in_parts = in_parts.reshape(seq_count, head_count, in_weight.shape[0], 2, in_weight.shape[2])
    down_parts = down_parts.reshape(
        seq_count, head_count, down_weight.shape[0], down_weight.shape[1]
    )
    heads_here = qkv_full.shape[2] // HEAD_DIM
    inputs = tokens.astype(jnp.float32)
    gain_one = gain_first.astype(jnp.float32)
    normed = layer_norm(inputs, gain_one).astype(jnp.bfloat16)
    normed_block = lax.all_gather(normed, "head", axis=0, tiled=True)
    projected = jnp.einsum(
        "rd,dgc->rgc", normed_block, qkv_full, preferred_element_type=jnp.float32
    )
    queries = rotate(
        projected[:, 0].reshape(block_rows, heads_here, HEAD_DIM), cosines, sines
    ).astype(jnp.bfloat16)
    key_rows = rotate(
        projected[:, 1].reshape(block_rows, heads_here, HEAD_DIM), cosines, sines
    ).astype(jnp.bfloat16)
    value_flat = projected[:, 2].astype(jnp.bfloat16)
    value_rows = value_flat.reshape(block_rows, heads_here, HEAD_DIM)
    key_flat = key_rows.reshape(block_rows, -1)
    query_flat = queries.reshape(block_rows, -1)

    def forward_fold(carry_state, portion):
        piece_keys, piece_values = portion

        def forward_block(inner_state, block_begin, block_size):
            running_max, running_sum, weighted = inner_state
            key_part = lax.dynamic_slice_in_dim(piece_keys, block_begin, block_size, 0).reshape(
                block_size, heads_here, HEAD_DIM
            )
            value_part = lax.dynamic_slice_in_dim(piece_values, block_begin, block_size, 0).reshape(
                block_size, heads_here, HEAD_DIM
            )
            other_docs, _ = doc_layout(
                short_lengths, block_begin + jnp.arange(block_size, dtype=jnp.int32), total_rows
            )
            same_doc = (local_docs[:, None] == other_docs[None, :])[None]
            scores = scores_of(queries, key_part)
            new_max = jnp.maximum(
                running_max, jnp.max(jnp.where(same_doc, scores, masked_low), axis=2)
            )
            factor = jnp.exp(running_max - new_max)
            softmax_part = jnp.where(same_doc, jnp.exp(scores - new_max[:, :, None]), 0.0)
            running_sum = running_sum * factor + jnp.sum(softmax_part, axis=2)
            weighted = weighted * factor.T[:, :, None] + jnp.einsum(
                "hqk,khd->qhd",
                softmax_part.astype(jnp.bfloat16),
                value_part,
                preferred_element_type=jnp.float32,
            )
            return (new_max, running_sum, weighted)

        return over_blocks(carry_state, piece_keys.shape[0], block_rows, forward_block)

    zeros_three = jnp.zeros((block_rows, heads_here, HEAD_DIM), jnp.float32)
    start_state = (
        jnp.full((heads_here, block_rows), masked_low, jnp.float32),
        jnp.zeros((heads_here, block_rows), jnp.float32),
        zeros_three,
    )
    running_max, running_sum, weighted = forward_fold(
        start_state,
        (
            lax.all_gather(key_flat, "seq", axis=0, tiled=True),
            lax.all_gather(value_flat, "seq", axis=0, tiled=True),
        ),
    )
    attended = weighted / running_sum.T[:, :, None]
    log_sums = running_max + jnp.log(running_sum)
    attended_low = attended.reshape(block_rows, -1).astype(jnp.bfloat16)
    branch = jnp.dot(attended_low, out_full, preferred_element_type=jnp.float32)
    branch_rows = lax.psum_scatter(
        branch.astype(jnp.bfloat16), "head", scatter_dimension=0, tiled=True
    ).astype(jnp.float32)
    resid = inputs + branch_rows
    gain_two = gain_second.astype(jnp.float32)
    normed_two = layer_norm(resid, gain_two).astype(jnp.bfloat16)
    normed_split = normed_two.reshape(half_rows, seq_count, -1)
    gate_up = jnp.einsum(
        "rse,shegf->rghf", normed_split, in_parts, preferred_element_type=jnp.float32
    ).reshape(half_rows, 2, -1)

    def activate(gate_part, up_part):
        return jax.nn.gelu(gate_part, approximate=False) * up_part

    hidden, activate_pull = jax.vjp(activate, gate_up[:, 0], gate_up[:, 1])
    hidden_low = hidden.astype(jnp.bfloat16)
    hidden_split = hidden_low.reshape(half_rows, head_count, -1)
    mlp_out = jnp.einsum(
        "rhf,shfe->rse", hidden_split, down_parts, preferred_element_type=jnp.float32
    ).reshape(half_rows, -1)
    mixed = (resid + mlp_out).astype(jnp.bfloat16)
    grad_out = out_grad.astype(jnp.float32)
    grad_split = out_grad.reshape(half_rows, seq_count, -1)
    grad_hidden = jnp.einsum(
        "rse,shfe->rhf", grad_split, down_parts, preferred_element_type=jnp.float32
    ).reshape(half_rows, -1)
    grad_gate, grad_up = activate_pull(grad_hidden)
    grad_gate_up = (
        jnp.stack([grad_gate, grad_up], axis=1)
        .astype(jnp.bfloat16)
        .reshape(half_rows, 2, head_count, -1)
    )
    down_grad = jnp.einsum(
        "rhf,rse->shfe", hidden_split, grad_split, preferred_element_type=jnp.float32
    ).reshape(seq_count * head_count, down_weight.shape[0], down_weight.shape[1])
    in_grad = jnp.einsum(
        "rse,rghf->shegf", normed_split, grad_gate_up, preferred_element_type=jnp.float32
    ).reshape(seq_count * head_count, in_weight.shape[0], 2, in_weight.shape[2])
    grad_normed_two = jnp.einsum(
        "rghf,shegf->rse", grad_gate_up, in_parts, preferred_element_type=jnp.float32
    ).reshape(half_rows, -1)
    _, norm_two_pull = jax.vjp(layer_norm, resid, gain_two)
    grad_resid_norm, gain_two_grad = norm_two_pull(grad_normed_two)
    grad_resid = grad_out + grad_resid_norm
    grad_branch = lax.all_gather(grad_resid.astype(jnp.bfloat16), "head", axis=0, tiled=True)
    out_grad_weight = jnp.einsum(
        "rc,rd->cd", attended_low, grad_branch, preferred_element_type=jnp.float32
    )
    grad_attended = jnp.einsum(
        "rd,cd->rc", grad_branch, out_full, preferred_element_type=jnp.float32
    ).astype(jnp.bfloat16)
    grad_three = grad_attended.reshape(block_rows, heads_here, HEAD_DIM)
    row_dots = jnp.sum(grad_three.astype(jnp.float32) * attended, axis=2).T
    all_sums, all_dots = (
        lax.all_gather(log_sums.T, "seq", axis=0, tiled=True),
        lax.all_gather(row_dots.T, "seq", axis=0, tiled=True),
    )

    def query_terms(query_grad, key_part, value_part, other_docs):
        same_doc = (local_docs[:, None] == other_docs[None, :])[None]
        _, dscore = block_grads(
            queries, grad_three, log_sums, row_dots, key_part, value_part, same_doc
        )
        return (
            query_grad
            + jnp.einsum("hqk,khd->qhd", dscore, key_part, preferred_element_type=jnp.float32)
            * score_scale
        )

    def key_terms(key_grad, value_grad, query_part, grad_part, sums_part, dots_part, other_docs):
        same_doc = (other_docs[:, None] == local_docs[None, :])[None]
        softmax_part, dscore = block_grads(
            query_part, grad_part, sums_part, dots_part, key_rows, value_rows, same_doc
        )
        value_grad = value_grad + jnp.einsum(
            "hqk,qhd->khd",
            softmax_part.astype(jnp.bfloat16),
            grad_part,
            preferred_element_type=jnp.float32,
        )
        key_grad = (
            key_grad
            + jnp.einsum("hqk,qhd->khd", dscore, query_part, preferred_element_type=jnp.float32)
            * score_scale
        )
        return (key_grad, value_grad)

    def piece_rows(source, block_begin, block_size):
        return lax.dynamic_slice_in_dim(source, block_begin, block_size, 0).reshape(
            block_size, heads_here, HEAD_DIM
        )

    def piece_stats(block_begin, block_size):
        sums_part = lax.dynamic_slice_in_dim(all_sums, block_begin, block_size, 0).T
        dots_part = lax.dynamic_slice_in_dim(all_dots, block_begin, block_size, 0).T
        other_docs, _ = doc_layout(
            short_lengths, block_begin + jnp.arange(block_size, dtype=jnp.int32), total_rows
        )
        return (sums_part, dots_part, other_docs)

    def fold_keys(carry_state, portion):
        piece_keys, piece_values = portion

        def key_block(inner_state, block_begin, block_size):
            _, _, other_docs = piece_stats(block_begin, block_size)
            return query_terms(
                inner_state,
                piece_rows(piece_keys, block_begin, block_size),
                piece_rows(piece_values, block_begin, block_size),
                other_docs,
            )

        return over_blocks(carry_state, piece_keys.shape[0], block_rows, key_block)

    query_grad = fold_keys(
        zeros_three,
        (
            lax.all_gather(key_flat, "seq", axis=0, tiled=True),
            lax.all_gather(value_flat, "seq", axis=0, tiled=True),
        ),
    )

    def fold_queries(carry_state, portion):
        piece_queries, piece_grads = portion

        def query_block(inner_state, block_begin, block_size):
            sums_part, dots_part, other_docs = piece_stats(block_begin, block_size)
            return key_terms(
                inner_state[0],
                inner_state[1],
                piece_rows(piece_queries, block_begin, block_size),
                piece_rows(piece_grads, block_begin, block_size),
                sums_part,
                dots_part,
                other_docs,
            )

        return over_blocks(carry_state, piece_queries.shape[0], block_rows, query_block)

    key_grad, value_grad = fold_queries(
        (zeros_three, zeros_three),
        (
            lax.all_gather(query_flat, "seq", axis=0, tiled=True),
            lax.all_gather(grad_attended, "seq", axis=0, tiled=True),
        ),
    )

    def rotate_local(heads_in):
        return rotate(heads_in, cosines, sines)

    _, rotate_pull = jax.vjp(rotate_local, zeros_three)
    query_back = rotate_pull(query_grad)[0]
    key_back = rotate_pull(key_grad)[0]
    grad_qkv = jnp.stack(
        [
            query_back.reshape(block_rows, -1),
            key_back.reshape(block_rows, -1),
            value_grad.reshape(block_rows, -1),
        ],
        axis=1,
    ).astype(jnp.bfloat16)
    qkv_grad = jnp.einsum("rd,rgc->dgc", normed_block, grad_qkv, preferred_element_type=jnp.float32)
    grad_normed_one = jnp.einsum(
        "rgc,dgc->rd", grad_qkv, qkv_full, preferred_element_type=jnp.float32
    )
    grad_normed_rows = lax.psum_scatter(
        grad_normed_one.astype(jnp.bfloat16), "head", scatter_dimension=0, tiled=True
    ).astype(jnp.float32)
    _, norm_one_pull = jax.vjp(layer_norm, inputs, gain_one)
    grad_inputs_norm, gain_one_grad = norm_one_pull(grad_normed_rows)
    tokens_grad = grad_resid + grad_inputs_norm
    qkv_weight_grad, out_weight_grad = (
        lax.psum_scatter(qkv_grad, "seq", scatter_dimension=0, tiled=True),
        lax.psum_scatter(out_grad_weight, "seq", scatter_dimension=1, tiled=True),
    )
    attn_gain_grad, mlp_gain_grad, in_weight_grad, down_weight_grad = (
        lax.psum_scatter(gain_one_grad, ("seq", "head"), scatter_dimension=0, tiled=True),
        lax.psum_scatter(gain_two_grad, ("seq", "head"), scatter_dimension=0, tiled=True),
        lax.psum_scatter(in_grad, ("seq", "head"), scatter_dimension=0, tiled=True),
        lax.psum_scatter(down_grad, ("seq", "head"), scatter_dimension=0, tiled=True),
    )
    return (
        mixed,
        tokens_grad,
        attn_gain_grad,
        qkv_weight_grad,
        out_weight_grad,
        mlp_gain_grad,
        in_weight_grad.reshape(in_weight.shape),
        down_weight_grad.reshape(down_weight.shape),
    )


def solution(mesh):
    placed = (
        P(("seq", "head"), None),
        P(("seq", "head"), None),
        P(),
        P(("seq", "head")),
        P("seq", None, "head"),
        P("head", "seq"),
        P(("seq", "head")),
        P("seq", None, "head"),
        P("head", "seq"),
    )
    return jax.shard_map(
        on_device,
        mesh=mesh,
        in_specs=placed,
        out_specs=(
            P(("seq", "head"), None),
            P(("seq", "head"), None),
            P(("seq", "head")),
            P("seq", None, "head"),
            P("head", "seq"),
            P(("seq", "head")),
            P("seq", None, "head"),
            P("head", "seq"),
        ),
        check_vma=False,
    )
```

profile of v0, /device:TPU:0, one launch (start us, length us, event | category | flops | bytes accessed | tf_op | source)
XLA Modules:
  0.0 791.6 jit_solution(17327773189222594226)
XLA Ops:
  9.7 42.2 %all-reduce.9 = (bf16[768]{0:T(1024)(128)(2,1)S(1)}, bf16[768]{0:T(1024)(128)(2,1)S(1)}) all-reduce(bf16[768]{0:T(1024)(128)(2,1)S(1)} %dynamic-update-slice, bf16[768]{0:T(1024)(128)(2,1)S(1)} %dynamic-update-slice.1), channel_id=1, replica_groups=mesh['seq'=16,'head'=2] {'seq','head'}, use_global_device_ids=true, to_apply=%add.4 | all-reduce | flops 1536 | bytes 6144
  55.0 5.5 all_gather.45
  67.9 24.1 %all_gather.49 = bf16[384,768]{0,1:T(8,128)(2,1)} all-gather(bf16[384,48]{0,1:T(8,128)(2,1)S(1)} %copy-done.34), channel_id=1, replica_groups=mesh['seq'=16,'head'=2] {'seq'}, dimensions={1}, use_global_device_ids=true | all-gather | bytes 626688 | tf_op jit(solution)/shard_map/all_gather | solution.py:104
  92.0 11.4 %all-gather.20.cloned.1.call-done = bf16[2048,1,384]{2,0,1:T(8,128)(2,1)} async-done(((bf16[128,1,384]{2,0,1:T(8,128)(2,1)}), bf16[2048,1,384]{2,0,1:T(8,128)(2,1)}) %all-gather.20.cloned.1.call-update) | async-done | bytes 1572880 | tf_op jit(solution)/shard_map/all_gather | solution.py:177
  106.0 38.8 %all-gather.14.cloned.1.call-done = bf16[2048,384]{1,0:T(8,128)(2,1)} async-done(((bf16[128,384]{1,0:T(8,128)(2,1)}), bf16[2048,384]{1,0:T(8,128)(2,1)}) %all-gather.14.cloned.1.call-update) | async-done | bytes 1572880 | tf_op jit(solution)/shard_map/all_gather | solution.py:176
  147.5 16.2 %while.45 = (s32[]{:T(128)}, f32[6,128]{1,0:T(8,128)S(1)}, f32[6,128]{1,0:T(8,128)S(1)}, f32[128,6,64]{0,2,1:T(8,128)}, s32[128]{0:T(128)S(1)}, /*index=5*/s32[2...) while((s32[]{:T(128)}, f32[6,128]{1,0:T(8,128)S(1)}, ...), condition=%wide.region_10.11_spmd.clone, body=%wide.region_6.10_spmd.clone.sunk | while | flops 210269696 | bytes 19956576 | solution.py:60
  172.5 30.3 %all-gather.24.cloned.1.call-done = bf16[32,576,48]{1,2,0:T(8,128)(2,1)} async-done(((bf16[1,576,48]{1,2,0:T(8,128)(2,1)}), bf16[32,576,48]{1,2,0:T(8,128)(2,1)}) %all-gather.24.cloned.1.call-update) | async-done | bytes 1769488 | tf_op jit(solution)/shard_map/all_gather | solution.py:110
  208.4 21.8 %all_gather.55 = f32[2048,6]{0,1:T(8,128)} all-gather(f32[128,6]{0,1:T(8,128)S(1)} %bitcast.408), channel_id=1, replica_groups=mesh['seq'=16,'head'=2] {'seq'}, dimensions={0}, use_global_device_ids=true | all-gather | bytes 52224 | tf_op jit(solution)/shard_map/all_gather | solution.py:238
  234.0 45.9 %all-gather.22.cloned.1.call-done = bf16[1536,2,576]{2,0,1:T(8,128)(2,1)} async-done(((bf16[48,2,576]{2,0,1:T(8,128)(2,1)}), bf16[1536,2,576]{2,0,1:T(8,128)(2,1)}) %all-gather.22.cloned.1.call-update) | async-done | bytes 3538960 | tf_op jit(solution)/shard_map/all_gather | solution.py:109
  291.6 5.6 all_gather.53
  300.0 21.9 %all_gather.57 = f32[2048,6]{0,1:T(8,128)} all-gather(f32[128,6]{0,1:T(8,128)S(1)} %multiply_reduce_fusion.1), channel_id=1, replica_groups=mesh['seq'=16,'head'=2] {'seq'}, dimensions={0}, use_global_device_ids=true | all-gather | bytes 52224 | tf_op jit(solution)/shard_map/all_gather | solution.py:239
  321.9 20.7 %while.46 = (s32[]{:T(128)}, f32[128,6,64]{0,2,1:T(8,128)}, s32[2]{0:T(128)S(1)}, bf16[2048,384]{0,1:T(8,128)(2,1)}, s32[128]{0:T(128)S(1)}, /*index=5*/s32[]{:T...) while((s32[]{:T(128)}, f32[128,6,64]{0,2,1:T(8,128)}, ...), condition=%wide.region_19.20_spmd.clone, body=%wide.region_17.19_spmd.clone.sunk | while | flops 306996224 | bytes 15817517 | solution.py:60
  328.7 3.6 fusion.261
  339.0 3.6 fusion.261
  342.6 19.4 %all-gather.18.cloned.1.call-done = bf16[2048,384]{1,0:T(8,128)(2,1)} async-done(((bf16[128,384]{1,0:T(8,128)(2,1)}), bf16[2048,384]{1,0:T(8,128)(2,1)}) %all-gather.18.cloned.1.call-update) | async-done | bytes 1572880 | tf_op jit(solution)/shard_map/all_gather | solution.py:327
  362.5 35.9 %while.47 = (s32[]{:T(128)}, f32[128,6,64]{0,2,1:T(8,128)}, f32[128,6,64]{0,2,1:T(8,128)}, s32[2]{0:T(128)}, bf16[2048,384]{1,0:T(8,128)(2,1)}, /*index=5*/s32[]...) while((s32[]{:T(128)}, f32[128,6,64]{0,2,1:T(8,128)}, ...), condition=%wide.region_22.23_spmd.clone, body=%wide.region_20.22_spmd.clone.sunk | while | flops 410903552 | bytes 20833108 | solution.py:60
  373.1 4.4 fusion.270
  391.0 4.5 fusion.270
  404.7 4.1 copy.227
  426.8 38.7 %all-reduce.8 = (f32[768]{0:T(1024)S(1)}, f32[768]{0:T(1024)S(1)}) all-reduce(f32[768]{0:T(1024)S(1)} %get-tuple-element.750, f32[768]{0:T(1024)S(1)} %get-tuple-element.748), channel_id=7, replica_groups=mesh['seq'=16,'head'=2] {'seq','head'}, use_global_device_ids=true, to_apply=%region_27.28.clone | all-reduce | flops 1536 | bytes 12288
  468.3 73.1 %reduce-scatter.15.cloned.1.call-done = f32[1,48,2,576]{3,1,2,0:T(8,128)} async-done(((f32[32,48,2,576]{3,1,2,0:T(8,128)}), f32[1,48,2,576]{3,1,2,0:T(8,128)}) %reduce-scatter.15.cloned.1.call-update) | async-done | bytes 221200 | tf_op jit(solution)/shard_map/reduce_scatter | solution.py:362
  543.2 60.2 %reduce-scatter.13.cloned.1.call-done = f32[384,48]{0,1:T(8,128)} async-done(((f32[384,768]{0,1:T(8,128)}), f32[384,48]{0,1:T(8,128)}) %reduce-scatter.13.cloned.1.call-update) | async-done | bytes 73744 | tf_op jit(solution)/shard_map/reduce_scatter | solution.py:357
  603.4 109.8 %reduce-scatter.17.cloned.1.call-done = f32[1,576,48]{1,2,0:T(8,128)} async-done(((f32[32,576,48]{1,2,0:T(8,128)}), f32[1,576,48]{1,2,0:T(8,128)}) %reduce-scatter.17.cloned.1.call-update) | async-done | bytes 110608 | tf_op jit(solution)/shard_map/reduce_scatter | solution.py:363
  713.3 71.8 %reduce-scatter.11.cloned.1.call-done = f32[48,3,384]{2,0,1:T(8,128)} async-done(((f32[768,3,384]{2,0,1:T(8,128)}), f32[48,3,384]{2,0,1:T(8,128)}) %reduce-scatter.11.cloned.1.call-update) | async-done | bytes 221200 | tf_op jit(solution)/shard_map/reduce_scatter | solution.py:356
  (291 shorter events, 131.3 us)
Async XLA Ops:
  7.2 56.1 %copy-start.41 = (s32[3]{0:T(128)S(1)}, s32[3]{0:T(128)}, u32[]{:S(2)}) copy-start(s32[3]{0:T(128)} %param.17) | copy-start | bytes 40
  7.2 53.4 %all-gather.12.cloned.1.call-start = ((), (), s32[]{:S(2)}) async-start(), calls=%async_computation.6 | async-start | bytes 1880064 | tf_op jit(solution)/shard_map/all_gather | solution.py:103
  7.9 95.5 %all-gather.20.cloned.1.call-start = ((), (), s32[]{:S(2)}) async-start(), calls=%async_computation.16 | async-start | bytes 1671168 | tf_op jit(solution)/shard_map/all_gather | solution.py:177
  54.0 10.7 %copy-start.39 = (f32[64]{0:T(128)}, f32[64]{0:T(128)S(1)}, u32[]{:S(2)}) copy-start(f32[64]{0:T(128)S(1)} %fusion.102) | copy-start | bytes 772
  54.0 12.0 %copy-start.35 = (f32[64]{0:T(128)}, f32[64]{0:T(128)S(1)}, u32[]{:S(2)}) copy-start(f32[64]{0:T(128)S(1)} %fusion.149) | copy-start | bytes 772
  63.2 81.6 %all-gather.14.cloned.1.call-start = ((), (), s32[]{:S(2)}) async-start(), calls=%async_computation.7 | async-start | bytes 1671168 | tf_op jit(solution)/shard_map/all_gather | solution.py:176
  67.2 135.6 %all-gather.24.cloned.1.call-start = ((), (), s32[]{:S(2)}) async-start(), calls=%async_computation.18 | async-start | bytes 2027520 | tf_op jit(solution)/shard_map/all_gather | solution.py:110
  67.8 162.5 %reduce-scatter.7.cloned.1.call-start = ((), (), s32[]{:S(2)}) async-start(), calls=%async_computation.8 | async-start | bytes 294912 | tf_op jit(solution)/shard_map/reduce_scatter | solution.py:184
  167.3 112.6 %all-gather.22.cloned.1.call-start = ((), (), s32[]{:S(2)}) async-start(), calls=%async_computation.17 | async-start | bytes 4055040 | tf_op jit(solution)/shard_map/all_gather | solution.py:109
  169.0 173.6 %all-gather.16.cloned.1.call-start = ((), (), s32[]{:S(2)}) async-start(), calls=%async_computation.9 | async-start | bytes 1671168 | tf_op jit(solution)/shard_map/all_gather | solution.py:326
  172.5 189.5 %all-gather.18.cloned.1.call-start = ((), (), s32[]{:S(2)}) async-start(), calls=%async_computation.10 | async-start | bytes 1671168 | tf_op jit(solution)/shard_map/all_gather | solution.py:327
  202.8 27.5 %copy-start.2 = (bf16[64,768]{1,0:T(8,128)(2,1)S(1)}, bf16[64,768]{1,0:T(8,128)(2,1)}, u32[]{:S(2)}) copy-start(bf16[64,768]{1,0:T(8,128)(2,1)} %param.15) | copy-start | bytes 294916
  234.0 49.0 %copy-start.14 = (bf16[64,16,48,1,1]{0,2,1,4,3:T(8,128)(2,1)}, bf16[64,16,48,1,1]{0,2,1,4,3:T(8,128)(2,1)S(1)}, u32[]{:S(2)}) copy-start(bf16[64,16,48,1,1]{0,2,1,4,3:T(8,128)(2,1)S(1)} %copy.234) | copy-start | bytes 294916
  289.1 8.8 %copy-start.6 = (bf16[384,768]{0,1:T(8,128)(2,1)S(1)}, bf16[384,768]{0,1:T(8,128)(2,1)}, u32[]{:S(2)}) copy-start(bf16[384,768]{0,1:T(8,128)(2,1)} %all_gather.49) | copy-start | bytes 1769476
  289.2 9.9 %copy-start.31 = (f32[128,6,64]{0,2,1:T(8,128)S(1)}, f32[128,6,64]{0,2,1:T(8,128)}, u32[]{:S(2)}) copy-start(f32[128,6,64]{0,2,1:T(8,128)} %get-tuple-element.413) | copy-start | bytes 589828
  290.9 31.0 %copy-start.37 = (f32[64]{0:T(128)}, f32[64]{0:T(128)S(1)}, u32[]{:S(2)}) copy-start(f32[64]{0:T(128)S(1)} %negate_multiply_fusion.2) | copy-start | bytes 772
  299.0 125.5 %reduce-scatter.9.cloned.1.call-start = ((), (), s32[]{:S(2)}) async-start(), calls=%async_computation.11 | async-start | bytes 294912 | tf_op jit(solution)/shard_map/reduce_scatter | solution.py:349
  403.5 138.0 %reduce-scatter.15.cloned.1.call-start = ((), (), s32[]{:S(2)}) async-start(), calls=%async_computation.14 | async-start | bytes 8110080 | tf_op jit(solution)/shard_map/reduce_scatter | solution.py:362
  408.8 194.6 %reduce-scatter.13.cloned.1.call-start = ((), (), s32[]{:S(2)}) async-start(), calls=%async_computation.13 | async-start | bytes 1253376 | tf_op jit(solution)/shard_map/reduce_scatter | solution.py:357
  411.3 302.0 %reduce-scatter.17.cloned.1.call-start = ((), (), s32[]{:S(2)}) async-start(), calls=%async_computation.15 | async-start | bytes 4055040 | tf_op jit(solution)/shard_map/reduce_scatter | solution.py:363
  415.4 369.7 %reduce-scatter.11.cloned.1.call-start = ((), (), s32[]{:S(2)}) async-start(), calls=%async_computation.12 | async-start | bytes 3760128 | tf_op jit(solution)/shard_map/reduce_scatter | solution.py:356
  421.1 45.5 %copy-start.18 = (f32[64,768]{1,0:T(8,128)S(1)}, f32[64,768]{1,0:T(8,128)}, u32[]{:S(2)}) copy-start(f32[64,768]{1,0:T(8,128)} %copy-done.17) | copy-start | bytes 589828
  421.1 45.5 %copy-start.25 = (bf16[64,768]{1,0:T(8,128)(2,1)S(1)}, bf16[64,768]{1,0:T(8,128)(2,1)}, u32[]{:S(2)}) copy-start(bf16[64,768]{1,0:T(8,128)(2,1)} %param.16) | copy-start | bytes 294916
  421.1 45.5 %copy-start.38 = (f32[64]{0:T(128)S(1)}, f32[64]{0:T(128)}, u32[]{:S(2)}) copy-start(f32[64]{0:T(128)} %copy-done.37) | copy-start | bytes 772
  (37 other events, 88.9 us)
Sparse Core Ops, SparseCore 0:
  10.3 43.2 all-gather.11
  63.3 40.0 all-gather.19
  106.3 38.5 all-gather.13
  147.6 55.1 all-gather.23
  205.4 9.7 reduce-scatter.6
  218.6 61.2 all-gather.21
  282.8 38.4 all-gather.15
  323.5 38.3 all-gather.17
  403.6 9.8 reduce-scatter.8
  419.0 122.4 reduce-scatter.14
  546.1 57.2 reduce-scatter.12
  610.1 103.0 reduce-scatter.16
  718.2 66.8 reduce-scatter.10
where the time goes:
time: 793 us; the launch traced here: 792 us
  waiting for transfers between devices  462 us (58%)
  blocking collectives  160 us (20%)
  local copies, waits for them, and re-layouts  70.8 us (9%)
  matrix products  51.5 us (6%)
  other arithmetic  26.9 us (3%)
  between operations  15.3 us (2%)
    reduce_scatter x1, waiting for transfers between devices, on_device(): lax.psum_scatter(down_grad, ('seq', 'head'), scatter_dimension=0, tiled=T...  110 us
    unnamed x2, blocking collectives  80.9 us
    reduce_scatter x1, waiting for transfers between devices, on_device(): lax.psum_scatter(in_grad, ('seq', 'head'), scatter_dimension=0, tiled=True)  73.1 us
    reduce_scatter x1, waiting for transfers between devices, on_device(): lax.psum_scatter(qkv_grad, 'seq', scatter_dimension=0, tiled=True)  71.8 us
    reduce_scatter x1, waiting for transfers between devices, on_device(): lax.psum_scatter(out_grad_weight, 'seq', scatter_dimension=1, tiled=True)  60.2 us
    all_gather x1, waiting for transfers between devices, on_device(): lax.all_gather(in_weight[None], ('seq', 'head'), axis=0, tiled=True)  45.9 us
    all_gather x1, waiting for transfers between devices, on_device(): lax.all_gather(key_flat, 'seq', axis=0, tiled=True)  38.8 us
    all_gather x1, waiting for transfers between devices, on_device(): lax.all_gather(down_weight[None], ('seq', 'head'), axis=0, tiled=True)  30.3 us
  transfers between devices with their start and end apart: 13, of which 9 were waited for; matrix products, arithmetic and copies ran while one was open for 12% of the time, Pallas kernels for 0%

commit v1 on v0

--- a/solution.py
+++ b/solution.py
@@ -3,6 +3,8 @@
 import jax
 import jax.numpy as jnp
 from jax import lax
+from jax.experimental import pallas as pl
+from jax.experimental.pallas import tpu as pltpu
 from jax.sharding import PartitionSpec as P
 
 HEAD_DIM = 64
@@ -61,6 +63,84 @@
         block_step, carry_state, jnp.arange(row_count // block_size, dtype=jnp.int32)
     )
     return carry_state
+
+
+def group_peers(axes, seq_count, head_count):
+    seq, head = lax.axis_index("seq"), lax.axis_index("head")
+    if axes == "seq":
+        return seq, [((seq + k) % seq_count, head) for k in range(1, seq_count)]
+    if axes == "head":
+        return head, [(seq, (head + k) % head_count) for k in range(1, head_count)]
+    mine = seq * head_count + head
+    total = seq_count * head_count
+    others = [(mine + k) % total for k in range(1, total)]
+    return mine, [(other // head_count, other % head_count) for other in others]
+
+
+def peer_index(axes, peer, head_count):
+    if axes == "seq":
+        return peer[0]
+    if axes == "head":
+        return peer[1]
+    return peer[0] * head_count + peer[1]
+
+
+def exchange(operands, groups, spread, collective_id):
+    seq_count, head_count = lax.axis_size("seq"), lax.axis_size("head")
+    size_of = {"seq": seq_count, "head": head_count, "all": seq_count * head_count}
+    count = len(operands)
+    widest = "all" if "all" in groups else groups[0]
+    most = max(size_of[g] for g in groups)
+
+    def kernel(*refs):
+        sources, results = refs[:count], refs[count : 2 * count]
+        send_sem, recv_sem, own_sem = refs[2 * count :]
+        barrier = pltpu.get_barrier_semaphore()
+        _, everyone = group_peers(widest, seq_count, head_count)
+        for peer in everyone:
+            pl.semaphore_signal(barrier, inc=1, device_id=peer, device_id_type=pl.DeviceIdType.MESH)
+        pl.semaphore_wait(barrier, len(everyone))
+        copies = []
+        for i in range(count):
+            mine, peers = group_peers(groups[i], seq_count, head_count)
+            own = pltpu.make_async_copy(
+                sources[i].at[mine] if spread[i] else sources[i], results[i].at[mine], own_sem.at[i]
+            )
+            own.start()
+            for k, peer in enumerate(peers):
+                there = peer_index(groups[i], peer, head_count)
+                copy = pltpu.make_async_remote_copy(
+                    src_ref=sources[i].at[there] if spread[i] else sources[i],
+                    dst_ref=results[i].at[mine],
+                    send_sem=send_sem.at[i, k],
+                    recv_sem=recv_sem.at[i, k],
+                    device_id=peer,
+                    device_id_type=pl.DeviceIdType.MESH,
+                )
+                copy.start()
+                copies.append(copy)
+            copies.append(own)
+        for copy in copies:
+            copy.wait()
+
+    shapes = [
+        jax.ShapeDtypeStruct(o.shape if s else (size_of[g],) + o.shape, o.dtype)
+        for o, g, s in zip(operands, groups, spread)
+    ]
+    return pl.pallas_call(
+        kernel,
+        out_shape=shapes,
+        in_specs=[pl.BlockSpec(memory_space=pltpu.VMEM)] * count,
+        out_specs=[pl.BlockSpec(memory_space=pltpu.VMEM)] * count,
+        scratch_shapes=[
+            pltpu.SemaphoreType.DMA((count, most)),
+            pltpu.SemaphoreType.DMA((count, most)),
+            pltpu.SemaphoreType.DMA((count,)),
+        ],
+        compiler_params=pltpu.CompilerParams(
+            collective_id=collective_id, has_side_effects=True, vmem_limit_bytes=56 << 20
+        ),
+    )(*operands)
 
 
 def scores_of(queries, key_part):
@@ -99,16 +179,33 @@
     local_ids = lax.axis_index("seq") * block_rows + jnp.arange(block_rows, dtype=jnp.int32)
     local_docs, local_pos = doc_layout(short_lengths, local_ids, total_rows)
     cosines, sines = rope_tables(local_pos)
-    qkv_full, out_full = (
-        lax.all_gather(qkv_weight, "seq", axis=0, tiled=True),
-        lax.all_gather(out_weight, "seq", axis=1, tiled=True),
-    )
-    gain_first, gain_second, in_parts, down_parts = (
-        lax.all_gather(attn_gain, ("seq", "head"), axis=0, tiled=True),
-        lax.all_gather(mlp_gain, ("seq", "head"), axis=0, tiled=True),
-        lax.all_gather(in_weight[None], ("seq", "head"), axis=0, tiled=True),
-        lax.all_gather(down_weight[None], ("seq", "head"), axis=0, tiled=True),
-    )
+    small = seq_count * head_count <= 32
+    if small:
+        gain_tile = jnp.zeros((16, 128), jnp.bfloat16)
+        gain_tile = gain_tile.at[0, : attn_gain.shape[0]].set(attn_gain)
+        gain_tile = gain_tile.at[1, : mlp_gain.shape[0]].set(mlp_gain)
+        gain_tiles, qkv_full, out_full, in_parts, down_parts = exchange(
+            (gain_tile, qkv_weight.transpose(1, 0, 2), out_weight, in_weight.transpose(1, 0, 2), down_weight),
+            ("all", "seq", "seq", "all", "all"),
+            (False,) * 5,
+            0,
+        )
+        gain_first = gain_tiles[:, 0, : attn_gain.shape[0]].reshape(-1)
+        gain_second = gain_tiles[:, 1, : mlp_gain.shape[0]].reshape(-1)
+        qkv_full = qkv_full.transpose(0, 2, 1, 3).reshape(-1, 3, qkv_weight.shape[2])
+        out_full = out_full.transpose(1, 0, 2).reshape(out_weight.shape[0], -1)
+        in_parts = in_parts.transpose(0, 2, 1, 3)
+    else:
+        qkv_full, out_full = (
+            lax.all_gather(qkv_weight, "seq", axis=0, tiled=True),
+            lax.all_gather(out_weight, "seq", axis=1, tiled=True),
+        )
+        gain_first, gain_second, in_parts, down_parts = (
+            lax.all_gather(attn_gain, ("seq", "head"), axis=0, tiled=True),
+            lax.all_gather(mlp_gain, ("seq", "head"), axis=0, tiled=True),
+            lax.all_gather(in_weight[None], ("seq", "head"), axis=0, tiled=True),
+            lax.all_gather(down_weight[None], ("seq", "head"), axis=0, tiled=True),
+        )
     in_parts = in_parts.reshape(seq_count, head_count, in_weight.shape[0], 2, in_weight.shape[2])
     down_parts = down_parts.reshape(
         seq_count, head_count, down_weight.shape[0], down_weight.shape[1]
@@ -170,13 +267,16 @@
         jnp.zeros((heads_here, block_rows), jnp.float32),
         zeros_three,
     )
-    running_max, running_sum, weighted = forward_fold(
-        start_state,
-        (
-            lax.all_gather(key_flat, "seq", axis=0, tiled=True),
-            lax.all_gather(value_flat, "seq", axis=0, tiled=True),
-        ),
-    )
+    if small:
+        all_keys, all_values, all_queries = (
+            a.reshape(-1, a.shape[2])
+            for a in exchange((key_flat, value_flat, query_flat), ("seq",) * 3, (False,) * 3, 1)
+        )
+    else:
+        all_keys, all_values, all_queries = (
+            lax.all_gather(a, "seq", axis=0, tiled=True) for a in (key_flat, value_flat, query_flat)
+        )
+    running_max, running_sum, weighted = forward_fold(start_state, (all_keys, all_values))
     attended = weighted / running_sum.T[:, :, None]
     log_sums = running_max + jnp.log(running_sum)
     attended_low = attended.reshape(block_rows, -1).astype(jnp.bfloat16)
@@ -234,10 +334,17 @@
     ).astype(jnp.bfloat16)
     grad_three = grad_attended.reshape(block_rows, heads_here, HEAD_DIM)
     row_dots = jnp.sum(grad_three.astype(jnp.float32) * attended, axis=2).T
-    all_sums, all_dots = (
-        lax.all_gather(log_sums.T, "seq", axis=0, tiled=True),
-        lax.all_gather(row_dots.T, "seq", axis=0, tiled=True),
-    )
+    if small:
+        stats = jnp.zeros((16, block_rows), jnp.float32)
+        stats = stats.at[:heads_here].set(log_sums).at[8 : 8 + heads_here].set(row_dots)
+        all_grads, all_stats = exchange((grad_attended, stats), ("seq",) * 2, (False,) * 2, 2)
+        all_grads = all_grads.reshape(-1, all_grads.shape[2])
+        all_sums = all_stats[:, :heads_here].transpose(0, 2, 1).reshape(-1, heads_here)
+        all_dots = all_stats[:, 8 : 8 + heads_here].transpose(0, 2, 1).reshape(-1, heads_here)
+    else:
+        all_grads, all_sums, all_dots = (
+            lax.all_gather(a, "seq", axis=0, tiled=True) for a in (grad_attended, log_sums.T, row_dots.T)
+        )
 
     def query_terms(query_grad, key_part, value_part, other_docs):
         same_doc = (local_docs[:, None] == other_docs[None, :])[None]
@@ -297,10 +404,7 @@
 
     query_grad = fold_keys(
         zeros_three,
-        (
-            lax.all_gather(key_flat, "seq", axis=0, tiled=True),
-            lax.all_gather(value_flat, "seq", axis=0, tiled=True),
-        ),
+        (all_keys, all_values),
     )
 
     def fold_queries(carry_state, portion):
@@ -322,10 +426,7 @@
 
     key_grad, value_grad = fold_queries(
         (zeros_three, zeros_three),
-        (
-            lax.all_gather(query_flat, "seq", axis=0, tiled=True),
-            lax.all_gather(grad_attended, "seq", axis=0, tiled=True),
-        ),
+        (all_queries, all_grads),
     )
 
     def rotate_local(heads_in):
@@ -352,16 +453,39 @@
     _, norm_one_pull = jax.vjp(layer_norm, inputs, gain_one)
     grad_inputs_norm, gain_one_grad = norm_one_pull(grad_normed_rows)
     tokens_grad = grad_resid + grad_inputs_norm
-    qkv_weight_grad, out_weight_grad = (
-        lax.psum_scatter(qkv_grad, "seq", scatter_dimension=0, tiled=True),
-        lax.psum_scatter(out_grad_weight, "seq", scatter_dimension=1, tiled=True),
-    )
-    attn_gain_grad, mlp_gain_grad, in_weight_grad, down_weight_grad = (
-        lax.psum_scatter(gain_one_grad, ("seq", "head"), scatter_dimension=0, tiled=True),
-        lax.psum_scatter(gain_two_grad, ("seq", "head"), scatter_dimension=0, tiled=True),
-        lax.psum_scatter(in_grad, ("seq", "head"), scatter_dimension=0, tiled=True),
-        lax.psum_scatter(down_grad, ("seq", "head"), scatter_dimension=0, tiled=True),
-    )
+    if small:
+        rows_in = qkv_weight.shape[0]
+        low_qkv = qkv_grad.astype(jnp.bfloat16).reshape(seq_count, rows_in, 3, -1).transpose(0, 2, 1, 3)
+        low_out = out_grad_weight.astype(jnp.bfloat16).reshape(-1, seq_count, out_weight.shape[1]).transpose(1, 0, 2)
+        low_in = in_grad.astype(jnp.bfloat16).transpose(0, 2, 1, 3)
+        low_down = down_grad.astype(jnp.bfloat16)
+        width = attn_gain.shape[0]
+        gains = jnp.zeros((seq_count * head_count, 16, 128), jnp.float32)
+        gains = gains.at[:, 0, :width].set(gain_one_grad.reshape(-1, width))
+        gains = gains.at[:, 1, :width].set(gain_two_grad.reshape(-1, width))
+        qkv_terms, out_terms, in_terms, down_terms, gain_terms = exchange(
+            (low_qkv, low_out, low_in, low_down, gains),
+            ("seq", "seq", "all", "all", "all"),
+            (True,) * 5,
+            3,
+        )
+        qkv_weight_grad = jnp.sum(qkv_terms.astype(jnp.float32), axis=0).transpose(1, 0, 2)
+        out_weight_grad = jnp.sum(out_terms.astype(jnp.float32), axis=0)
+        in_weight_grad = jnp.sum(in_terms.astype(jnp.float32), axis=0).transpose(1, 0, 2)
+        down_weight_grad = jnp.sum(down_terms.astype(jnp.float32), axis=0)
+        gain_sums = jnp.sum(gain_terms, axis=0)
+        attn_gain_grad, mlp_gain_grad = gain_sums[0, :width], gain_sums[1, :width]
+    else:
+        qkv_weight_grad, out_weight_grad = (
+            lax.psum_scatter(qkv_grad, "seq", scatter_dimension=0, tiled=True),
+            lax.psum_scatter(out_grad_weight, "seq", scatter_dimension=1, tiled=True),
+        )
+        attn_gain_grad, mlp_gain_grad, in_weight_grad, down_weight_grad = (
+            lax.psum_scatter(gain_one_grad, ("seq", "head"), scatter_dimension=0, tiled=True),
+            lax.psum_scatter(gain_two_grad, ("seq", "head"), scatter_dimension=0, tiled=True),
+            lax.psum_scatter(in_grad, ("seq", "head"), scatter_dimension=0, tiled=True),
+            lax.psum_scatter(down_grad, ("seq", "head"), scatter_dimension=0, tiled=True),
+        )
     return (
         mixed,
         tokens_grad,

time: 793 us -> 937 us (1.18)
  Pallas kernels: 0 us -> 716 us
  waiting for transfers between devices: 462 us -> 6.65 us
  blocking collectives: 160 us -> 12.3 us
  local copies, waits for them, and re-layouts: 70.8 us -> 83.7 us
  other arithmetic: 26.9 us -> 36.3 us
    pallas_call x0 -> x4, Pallas kernels: none -> 716 us  [exchange(): pl.pallas_call(kernel, out_shape=shapes, in_specs=[pl.BlockSpec(memory_sp...]
    reduce_scatter x4 -> x0, waiting for transfers between devices: 315 us -> none  [the longest x1 110 us: on_device(): lax.psum_scatter(down_grad, ('seq', 'head'), scatter_dimension=0, tiled=T...]
    all_gather x7 -> x0, waiting for transfers between devices: 146 us -> none  [the longest x1 45.9 us: on_device(): lax.all_gather(in_weight[None], ('seq', 'head'), axis=0, tiled=True)]
    unnamed x2 -> x0, blocking collectives: 80.9 us -> none
    all_gather x3 -> x0, blocking collectives: 67.8 us -> none  [the longest x1 24.1 us: on_device(): lax.all_gather(out_weight, 'seq', axis=1, tiled=True)]
    reshape x0 -> x5, local copies, waits for them, and re-layouts: none -> 10.2 us  [the longest x1 4.33 us: on_device(): in_parts.reshape(seq_count, head_count, in_weight.shape[0], 2, in_weight....]
    convert_element_type x0 -> x5, local copies, waits for them, and re-layouts: none -> 10.1 us  [the longest x1 4.75 us: on_device(): low_in = in_grad.astype(jnp.bfloat16).transpose(0, 2, 1, 3)]
  transfers between devices with their start and end apart: 13 -> 2, of which waited for: 9 -> 1; matrix products, arithmetic and copies ran while one was open for 12% -> 3% of each run, Pallas kernels for 0% -> 0%
where the time goes in v1:
time: 937 us; the launch traced here: 928 us
  Pallas kernels  716 us (76%)
  local copies, waits for them, and re-layouts  83.7 us (9%)
  matrix products  52.8 us (6%)
  other arithmetic  36.3 us (4%)
  between operations  16.1 us (2%)
  blocking collectives  12.3 us (1%)
    pallas_call x4, Pallas kernels, exchange(): pl.pallas_call(kernel, out_shape=shapes, in_specs=[pl.BlockSpec(memory_sp...  716 us
  transfers between devices with their start and end apart: 2, of which 1 were waited for; matrix products, arithmetic and copies ran while one was open for 3% of the time, Pallas kernels for 0%

profile of v1, /device:TPU:0, one launch (start us, length us, event | category | flops | bytes accessed | tf_op | source)
XLA Modules:
  0.0 928.5 jit_solution(5782959142290002674)
XLA Ops:
  16.1 237.3 %shard_map.152 = (bf16[32,16,128]{2,1,0:T(8,128)(2,1)}, bf16[16,3,48,384]{3,2,1,0:T(8,128)(2,1)}, bf16[16,384,48]{2,1,0:T(8,128)(2,1)}, bf16[32,2,48,576]{3,2,1,0:T(8,128)(2,1)}, bf16[32,576,48]{2,1,0:T(8,128)(2,1)}) custom-call(bf16[16,128]{1,0:T(8,128)(2,1)} %copy-done.32, bf16[3,48,384]{2,1,0:T(8,128)(2,1)} %bitcast.374, bf16[384,48]{1,0:T(8,128)(2,1)} %copy.202.refs_2_, ...), custom_call_target="tpu_custom_call" | custom-call | tf_op jit(solution)/shard_map/pallas_call | solution.py:130
  256.4 7.0 all_gather.6
  270.1 138.8 %shard_map.153 = (bf16[16,128,384]{2,1,0:T(8,128)(2,1)}, bf16[16,128,384]{2,1,0:T(8,128)(2,1)}, bf16[16,128,384]{2,1,0:T(8,128)(2,1)}) custom-call(bf16[128,384]{1,0:T(8,128)(2,1)} %get-tuple-element.945.refs_0_, bf16[128,384]{1,0:T(8,128)(2,1)} %slice_bitcast_fusion.4.refs_1_, bf16[128,384]{1,0:T(8,128)(2,1)} %get-tuple-element.944.refs_2_), custom_call_target="tpu_custom_call" | custom-call | tf_op jit(solution)/shard_map/pallas_call | solution.py:130
  414.1 12.2 %while.51 = (s32[]{:T(128)}, f32[6,128]{1,0:T(8,128)S(1)}, f32[6,128]{1,0:T(8,128)S(1)}, f32[128,6,64]{0,2,1:T(8,128)S(1)}, s32[128]{0:T(128)S(1)}, /*index=5*/s...) while((s32[]{:T(128)}, f32[6,128]{1,0:T(8,128)S(1)}, ...), condition=%wide.region_10.11_spmd.clone, body=%wide.region_6.0_spmd.clone.sunk | while | flops 210269696 | bytes 15237899 | solution.py:62
  428.0 3.9 convolution_bitcast_fusion.2
  432.9 5.8 copy.224
  440.0 4.3 copy.231
  444.9 6.6 reduce-scatter.3.cloned.1.call-done
  455.7 3.0 convolution_bitcast_fusion
  462.5 4.2 multiply_reduce_fusion
  467.7 5.3 all_gather.7
  476.7 22.2 %while.52 = (s32[]{:T(128)}, f32[128,6,64]{0,2,1:T(8,128)}, s32[2]{0:T(128)}, bf16[2048,384]{0,1:T(8,128)(2,1)}, s32[128]{0:T(128)S(1)}, /*index=5*/s32[]{:T(128...) while((s32[]{:T(128)}, f32[128,6,64]{0,2,1:T(8,128)}, ...), condition=%wide.region_19.20_spmd.clone, body=%wide.region_17.19_spmd.clone.sunk | while | flops 306996224 | bytes 15829833 | solution.py:62
  484.3 3.5 fusion.229
  495.3 3.6 fusion.229
  500.2 49.4 %shard_map.154 = (bf16[16,128,384]{2,1,0:T(8,128)(2,1)}, f32[16,16,128]{2,1,0:T(8,128)}) custom-call(bf16[128,384]{1,0:T(8,128)(2,1)} %copy-done.18, f32[16,128]{1,0:T(8,128)} %scatter.25.refs_1_), custom_call_target="tpu_custom_call" | custom-call | tf_op jit(solution)/shard_map/pallas_call | solution.py:130
  551.1 33.5 %while.53 = (s32[]{:T(128)}, f32[128,6,64]{0,2,1:T(8,128)}, f32[128,6,64]{0,2,1:T(8,128)}, s32[2]{0:T(128)S(1)}, bf16[2048,384]{1,0:T(8,128)(2,1)}, /*index=5*/s...) while((s32[]{:T(128)}, f32[128,6,64]{0,2,1:T(8,128)}, ...), condition=%wide.region_22.23_spmd.clone, body=%wide.region_20.22_spmd.clone.sunk | while | flops 410903552 | bytes 20439836 | solution.py:62
  560.4 4.4 fusion.238
  577.1 4.5 fusion.238
  581.5 3.0 fusion.239
  591.5 3.1 convert_bitcast_fusion
  604.4 4.1 copy.249
  608.5 4.8 copy.246
  618.8 290.6 %shard_map.155 = (bf16[16,3,48,384]{3,2,1,0:T(8,128)(2,1)}, bf16[16,384,48]{2,1,0:T(8,128)(2,1)}, bf16[32,2,48,576]{3,2,1,0:T(8,128)(2,1)}, bf16[32,576,48]{2,1,0:T(8,128)(2,1)}, f32[32,16,128]{2,1,0:T(8,128)}) custom-call(bf16[16,3,48,384]{3,2,1,0:T(8,128)(2,1)} %bitcast.343, bf16[16,384,48]{2,1,0:T(8,128)(2,1)} %bitcast.344, ...), custom_call_target="tpu_custom_call" | custom-call | tf_op jit(solution)/shard_map/pallas_call | solution.py:130
  914.5 3.3 convert_reduce_fusion.4
  (275 shorter events, 117.6 us)
Async XLA Ops:
  7.2 249.1 %copy-start.1 = (bf16[64,768]{1,0:T(8,128)(2,1)S(1)}, bf16[64,768]{1,0:T(8,128)(2,1)}, u32[]{:S(2)}) copy-start(bf16[64,768]{1,0:T(8,128)(2,1)} %param.27) | copy-start | bytes 294916
  7.2 444.4 %reduce-scatter.3.cloned.1.call-start = ((), (), s32[]{:S(2)}) async-start(), calls=%async_computation.2 | async-start | bytes 294912 | tf_op jit(solution)/shard_map/reduce_scatter | solution.py:284
  8.3 255.5 %copy-start.36 = (f32[64]{0:T(128)}, f32[64]{0:T(128)S(1)}, u32[]{:S(2)}) copy-start(f32[64]{0:T(128)S(1)} %broadcast_multiply_fusion.3) | copy-start | bytes 772
  9.4 254.4 %copy-start.42 = (f32[64]{0:T(128)}, f32[64]{0:T(128)S(1)}, u32[]{:S(2)}) copy-start(f32[64]{0:T(128)S(1)} %fusion.74) | copy-start | bytes 772
  9.4 254.4 %copy-start.38 = (f32[64]{0:T(128)}, f32[64]{0:T(128)S(1)}, u32[]{:S(2)}) copy-start(f32[64]{0:T(128)S(1)} %fusion.121) | copy-start | bytes 772
  254.5 10.0 %copy-start.44 = (s32[3]{0:T(128)S(1)}, s32[3]{0:T(128)}, u32[]{:S(2)}) copy-start(s32[3]{0:T(128)} %param.29) | copy-start | bytes 40
  256.2 11.1 %copy-start.2 = (bf16[16,48,3,384]{3,1,0,2:T(8,128)(2,1)}, bf16[16,48,3,384]{3,1,0,2:T(8,128)(2,1)S(1)}, u32[]{:S(2)}) copy-start(bf16[16,48,3,384]{3,1,0,2:T(8,128)(2,1)S(1)} %copy.204) | copy-start | bytes 5308420
  408.8 5.3 copy-start.23
  414.1 13.5 %copy-start.20 = (bf16[64,768]{1,0:T(8,128)(2,1)S(1)}, bf16[64,768]{1,0:T(8,128)(2,1)}, u32[]{:S(2)}) copy-start(bf16[64,768]{1,0:T(8,128)(2,1)} %param.28) | copy-start | bytes 294916
  427.4 187.7 %reduce-scatter.5.cloned.1.call-start = ((), (), s32[]{:S(2)}) async-start(), calls=%async_computation.3 | async-start | bytes 294912 | tf_op jit(solution)/shard_map/reduce_scatter | solution.py:450
  444.3 14.4 %copy-start.33 = (f32[6,128]{1,0:T(8,128)}, f32[6,128]{1,0:T(8,128)S(1)}, u32[]{:S(2)}) copy-start(f32[6,128]{1,0:T(8,128)S(1)} %log_add_fusion) | copy-start | bytes 9220
  462.5 10.8 %copy-start.9 = (bf16[64,2,2,576]{3,0,2,1:T(8,128)(2,1)}, bf16[64,2,2,576]{3,0,2,1:T(8,128)(2,1)S(1)}, u32[]{:S(2)}) copy-start(bf16[64,2,2,576]{3,0,2,1:T(8,128)(2,1)S(1)} %copy_dynamic-update-slice_fusion) | copy-start | bytes 884740
  462.5 12.7 %copy-start.25 = (f32[128,6,64]{0,2,1:T(8,128)S(1)}, f32[128,6,64]{0,2,1:T(8,128)}, u32[]{:S(2)}) copy-start(f32[128,6,64]{0,2,1:T(8,128)} %copy-done.24) | copy-start | bytes 589828
  466.9 9.8 %copy-start.40 = (f32[64]{0:T(128)}, f32[64]{0:T(128)S(1)}, u32[]{:S(2)}) copy-start(f32[64]{0:T(128)S(1)} %negate_multiply_fusion.2) | copy-start | bytes 772
  584.5 5.2 copy-start.13
  586.9 4.6 copy-start.7
  586.9 4.6 copy-start.10
  589.7 4.9 copy-start.26
  589.7 5.1 copy-start.35
  589.7 5.2 copy-start.8
  598.4 5.4 copy-start.22
  608.5 4.8 copy-start.11
  909.4 4.1 copy-start.14
  913.5 5.1 copy-start.4
  (25 other events, 57.8 us)
Sparse Core Ops, SparseCore 0:
  427.5 23.9 reduce-scatter.2
  602.5 11.6 reduce-scatter.4

commit v2 on v0

--- a/solution.py
+++ b/solution.py
@@ -3,6 +3,8 @@
 import jax
 import jax.numpy as jnp
 from jax import lax
+from jax.experimental import pallas as pl
+from jax.experimental.pallas import tpu as pltpu
 from jax.sharding import PartitionSpec as P
 
 HEAD_DIM = 64
@@ -374,6 +376,615 @@
     )
 
 
+LOW = jnp.bfloat16
+FULL = jnp.float32
+
+
+def dot(a, b):
+    return jnp.dot(a, b, preferred_element_type=FULL)
+
+
+def dot_nt(a, b):
+    return lax.dot_general(a, b, (((1,), (1,)), ((), ())), preferred_element_type=FULL)
+
+
+def turned(a):
+    return a.astype(FULL).T
+
+
+def centred_norm(rows):
+    centred = rows - jnp.mean(rows, axis=-1, keepdims=True)
+    scale = lax.rsqrt(jnp.mean(centred * centred, axis=-1, keepdims=True) + norm_eps)
+    return centred * scale, scale
+
+
+def norm_back(unit, scale, weighted):
+    mean_w = jnp.mean(weighted, axis=-1, keepdims=True)
+    mean_wn = jnp.mean(weighted * unit, axis=-1, keepdims=True)
+    return (weighted - mean_w - unit * mean_wn) * scale
+
+
+def whole_layer(*refs):
+    (
+        short_ref, tok_ref, gout_ref, gain_ref, wq_ref, ffp_ref, wot_ref,
+        mixed_ref, tgrad_ref, gains_ref, qkvg_ref, ffg_ref, outg_ref,
+        xh, gt, gn, gb, wh, wht, ffw, wo, h1, cs, qa, ka, kt, vt, vr, pt, ot, ol, og, res,
+        ms, ms_c, ms_a, ms_y, db, dos, dop, dot_t, ds, dqt, dq, d1, d1_c, d1_a, d1_r1, d1_s1, d1_r2, d1_s2, d1_r3,
+        dw, dw_in, gf, gf_x, gf_s, gf_z, gf_f, gf_b, gf_c, go, go_x, go_s, go_z, go_f, go_b, go_c, gy, gy_in,
+        s_tok, r_tok, s_gain, r_gain, s_wq, r_wq, s_g, r_g, s_ff, r_ff, s_wo, r_wo,
+        s_o, r_o, s_ms, r_ms, s_db, r_db, s_do, r_do, s_d1, r_d1, s_dw, r_dw, s_gf, r_gf, s_go, r_go, s_gy, r_gy,
+    ) = refs
+    seq, head = lax.axis_index("seq"), lax.axis_index("head")
+    z, x, c, y = seq // 4, (seq // 2) % 2, seq % 2, head
+    zh, zb = z // 2, z % 2
+    slot = zb * 2 + x
+    active = slot < 3
+    slot3 = jnp.minimum(slot, 2)
+    pending = []
+
+    def flip(value, bit):
+        return value if bit == 0 else 1 - value
+
+    def at(z_, x_, c_, y_):
+        return (z_ * 4 + x_ * 2 + c_, y_)
+
+    def far_z(k):
+        return flip(zh, k // 2) * 2 + flip(zb, k % 2)
+
+    def partner(dim):
+        return {
+            "x": at(z, 1 - x, c, y),
+            "y": at(z, x, c, 1 - y),
+            "z": at(far_z(1), x, c, y),
+            "c": at(z, x, 1 - c, y),
+            "h": at(far_z(2), x, c, y),
+        }[dim]
+
+    def push(src, dst, send, recv, device, when=None):
+        copy = pltpu.make_async_remote_copy(
+            src_ref=src, dst_ref=dst, send_sem=send, recv_sem=recv,
+            device_id=device, device_id_type=pl.DeviceIdType.MESH,
+        )
+        if when is None:
+            copy.start()
+        else:
+            pl.when(when)(copy.start)
+        pending.append((when, copy))
+
+    def arrive(dst, recv, when=None):
+        copy = pltpu.make_async_remote_copy(
+            src_ref=dst, dst_ref=dst, send_sem=recv, recv_sem=recv,
+            device_id=partner("c"), device_id_type=pl.DeviceIdType.MESH,
+        )
+        if when is None:
+            copy.wait_recv()
+        else:
+            pl.when(when)(copy.wait_recv)
+
+    barrier = pltpu.get_barrier_semaphore()
+    peers = []
+    for k in range(1, 32):
+        kz, kx, kc, ky = k // 8, (k // 4) % 2, (k // 2) % 2, k % 2
+        if kz < 2 or ky == 0:
+            peers.append(at(far_z(kz), flip(x, kx), flip(c, kc), flip(y, ky)))
+    for peer in peers:
+        pl.semaphore_signal(barrier, inc=1, device_id=peer, device_id_type=pl.DeviceIdType.MESH)
+    pl.semaphore_wait(barrier, len(peers))
+
+    xh[zb, x, c, y] = tok_ref[...]
+    orders = (("x", "y", "z"), ("y", "z", "x"), ("z", "x", "y"))
+
+    def third(t):
+        return pl.ds(t * 256, 256)
+
+    def blocks(ref, opened, lanes, flipped=None, core=None):
+        there = {"z": zb, "x": x, "y": y, "c": c if core is None else core}
+        if flipped is not None:
+            there[flipped] = 1 - there[flipped]
+        index = tuple(slice(None) if d in opened else there[d] for d in ("z", "x", "c", "y"))
+        return ref.at[index + (slice(None), lanes)]
+
+    for t in range(3):
+        view = blocks(xh, (), third(t))
+        push(view, view, s_tok.at[0, t], r_tok.at[0, t], partner(orders[t][0]))
+
+    gt[zh, zb, x, c, y] = gain_ref[...]
+    gain_order = ("x", "y", "z", "h", "c")
+
+    def gain_view(opened, flipped=None):
+        there = {"h": zh, "z": zb, "x": x, "c": c, "y": y}
+        if flipped is not None:
+            there[flipped] = 1 - there[flipped]
+        return gt.at[tuple(slice(None) if d in opened else there[d] for d in ("h", "z", "x", "c", "y"))]
+
+    def gain_send(k):
+        view = gain_view(gain_order[:k])
+        push(view, view, s_gain.at[k], r_gain.at[k], partner(gain_order[k]))
+
+    def gain_wait(k):
+        arrive(gain_view(gain_order[:k], gain_order[k]), r_gain.at[k])
+
+    gain_send(0)
+
+    own_rows = pl.ds(pl.multiple_of(seq * 48, 16), 48)
+    for k in range(16):
+        z_, x_, c_ = far_z(k // 4), flip(x, (k // 2) % 2), flip(c, k % 2)
+        slot_ = (z_ % 2) * 2 + x_
+        piece = wq_ref.at[jnp.minimum(slot_ * 2 + c_, 5)]
+        if k == 0:
+            wh[own_rows, :] = piece[...]
+        else:
+            push(piece, wh.at[own_rows, :], s_wq.at[k], r_wq.at[k], at(z_, x_, c_, y), slot_ < 3)
+
+    gb[c, y] = gout_ref[...]
+    group = ((0, 1), (1, 0), (1, 1))
+    for k, (kc, ky) in enumerate(group):
+        push(gb.at[c, y], gb.at[c, y], s_g.at[k], r_g.at[k], at(z, x, flip(c, kc), flip(y, ky)))
+
+    core_rows = pl.ds(pl.multiple_of(c * 48, 16), 48)
+    wo_lanes = pl.ds(pl.multiple_of(y * 384, 128), 384)
+    wo_others = pl.ds(pl.multiple_of((1 - y) * 384, 128), 384)
+    ffw[z, x, core_rows, :] = ffp_ref[c]
+    wo[z, x, c, :, wo_lanes] = wot_ref[...]
+    for k in range(1, 4):
+        push(wot_ref, wo.at[z, x, c, :, wo_lanes], s_wo.at[k], r_wo.at[k], at(far_z(k), x, c, y))
+    for k in range(1, 8):
+        c_ = flip(c, k % 2)
+        push(ffp_ref.at[c_], ffw.at[z, x, core_rows, :], s_ff.at[k], r_ff.at[k], at(far_z(k // 2), x, c_, y))
+
+    for step in (1, 2):
+        for t in range(3):
+            arrive(blocks(xh, orders[t][: step - 1], third(t), orders[t][step - 1]), r_tok.at[step - 1, t])
+            view = blocks(xh, orders[t][:step], third(t))
+            push(view, view, s_tok.at[step, t], r_tok.at[step, t], partner(orders[t][step]))
+        gain_wait(step - 1)
+        gain_send(step)
+    gain_wait(2)
+    gain_send(3)
+    for t in range(3):
+        arrive(blocks(xh, orders[t][:2], third(t), orders[t][2]), r_tok.at[2, t])
+        view = blocks(xh, ("x", "y", "z"), third(t))
+        push(view, view, s_tok.at[3, t], r_tok.at[3, t], partner("c"))
+
+    half_rows = 1024
+    row = lax.broadcasted_iota(jnp.int32, (32, half_rows), 1) + zh * half_rows
+    feature = lax.broadcasted_iota(jnp.int32, (32, half_rows), 0)
+    bound = jnp.int32(2 * half_rows)
+    for b in range(short_ref.shape[0]):
+        bound = bound - short_ref[b]
+    doc = jnp.zeros_like(row)
+    start = jnp.zeros_like(row)
+    for b in range(short_ref.shape[0]):
+        passed = row >= bound
+        doc = doc + jnp.where(passed, 1, 0)
+        start = jnp.where(passed, bound, start)
+        bound = bound + short_ref[b]
+    inverse = jnp.exp(feature.astype(FULL) * (-2.0 * math.log(rope_base) / HEAD_DIM))
+    angles = (row - start).astype(FULL) * inverse
+    cs[0] = jnp.cos(angles)
+    cs[1] = jnp.sin(angles)
+    same = jnp.where(feature == doc, 1.0, 0.0)
+    cs[2] = same
+    qa[64:96, :] = ((same - 1.0) * 1e30).astype(LOW)
+    qa[96:128, :] = jnp.zeros((32, half_rows), LOW)
+
+    gain_wait(3)
+    gain_send(4)
+    gain_wait(4)
+    tiles = gt[...].reshape(512, 128)
+    width = 24
+    pick = lax.broadcasted_iota(jnp.int32, (128, 768), 1) % width == lax.broadcasted_iota(jnp.int32, (128, 768), 0)
+    spread = dot(tiles, jnp.where(pick, 1.0, 0.0).astype(LOW))
+    source = lax.broadcasted_iota(jnp.int32, (512, 768), 0)
+    wanted = (lax.broadcasted_iota(jnp.int32, (512, 768), 1) // width) * 16
+    gn[0:1, :] = jnp.sum(jnp.where(source == wanted, spread, 0.0), axis=0, keepdims=True)
+    gn[1:2, :] = jnp.sum(jnp.where(source == wanted + 1, spread, 0.0), axis=0, keepdims=True)
+
+    for t in range(3):
+        arrive(blocks(xh, ("x", "y", "z"), third(t), "c"), r_tok.at[3, t])
+    for k in range(1, 16):
+        source_seq = far_z(k // 4) * 4 + flip(x, (k // 2) % 2) * 2 + flip(c, k % 2)
+        arrive(wh.at[pl.ds(pl.multiple_of(source_seq * 48, 16), 48), :], r_wq.at[k], active)
+
+    @pl.when(active)
+    def _():
+        gain = gn[0:1, :]
+
+        def normed_block(b, carry):
+            rows = xh[b // 8, (b // 4) % 2, (b // 2) % 2, b % 2].astype(FULL)
+            unit, _ = centred_norm(rows)
+            h1[pl.ds(pl.multiple_of(b * 64, 64), 64), :] = (unit * gain).astype(LOW)
+            return carry
+
+        lax.fori_loop(0, 16, normed_block, 0)
+        wht[...] = turned(wh[...]).astype(LOW)
+        for part in range(4):
+            cols = pl.ds(part * 256, 256)
+            proj = dot_nt(wht[...], h1[cols, :])
+            cosine, sine = cs[0, :, cols], cs[1, :, cols]
+            q1, q2, k1, k2 = proj[0:32], proj[32:64], proj[64:96], proj[96:128]
+            qr = jnp.concatenate([q1 * cosine - q2 * sine, q2 * cosine + q1 * sine], axis=0)
+            kr = jnp.concatenate([k1 * cosine - k2 * sine, k2 * cosine + k1 * sine], axis=0)
+            qa[0:64, cols] = (qr * score_scale).astype(LOW)
+            kt[:, cols] = kr.astype(LOW)
+            vt[:, cols] = proj[128:192].astype(LOW)
+            pad = jnp.zeros((32, 256), FULL)
+            ka[cols, :] = jnp.concatenate([kr, cs[2, :, cols], pad], axis=0).T.astype(LOW)
+            vr[cols, :] = proj[128:192].T.astype(LOW)
+
+    def ff_forward(kz):
+        z_ = far_z(kz)
+        for kc in range(2):
+            if (kz, kc) != (0, 0):
+                rows = pl.ds(pl.multiple_of(flip(c, kc) * 48, 16), 48)
+                arrive(ffw.at[z_, x, rows, :], r_ff.at[kz * 2 + kc])
+        push(ffw.at[z_, x], ffw.at[z_, x], s_ff.at[8 + kz], r_ff.at[8 + kz], partner("x"))
+
+    for part in range(4):
+        cols = pl.ds(part * 256, 256)
+
+        @pl.when(active)
+        def _(part=part, cols=cols):
+            scores = dot(ka[...], qa[:, cols])
+            expo = jnp.exp(scores - jnp.max(scores, axis=0, keepdims=True))
+            prob = (expo * (1.0 / jnp.sum(expo, axis=0, keepdims=True))).astype(LOW)
+            pt[:, cols] = prob
+            result = dot(vt[...], prob)
+            ot[part] = result
+            ol[part] = result.astype(LOW)
+
+        for y_ in range(2):
+            mine = jnp.logical_and(slot == part, y == y_)
+
+            @pl.when(jnp.logical_and(active, mine))
+            def _(part=part):
+                og[y, slot3, c] = ol[part]
+
+            push(
+                ol.at[part], og.at[y, slot3, c], s_o.at[part, y_], r_o.at[slot3, y],
+                at(zh * 2 + part // 2, part % 2, c, y_), jnp.logical_and(active, jnp.logical_not(mine)),
+            )
+        ff_forward(part)
+        if part == 1:
+            for k in range(1, 4):
+                arrive(wo.at[far_z(k), x, c, :, wo_lanes], r_wo.at[k])
+            view = wo.at[:, x, c, :, wo_lanes]
+            push(view, view, s_wo.at[4], r_wo.at[4], partner("x"))
+        if part == 3:
+            arrive(wo.at[:, 1 - x, c, :, wo_lanes], r_wo.at[4])
+            view = wo.at[:, :, c, :, wo_lanes]
+            push(view, view, s_wo.at[5], r_wo.at[5], partner("y"))
+
+    for slot_ in range(3):
+        for y_ in range(2):
+            mine = jnp.logical_and(slot == slot_, y == y_)
+            arrive(og.at[y_, slot_, c], r_o.at[slot_, y_], jnp.logical_not(mine))
+    push(og.at[:, :, c], og.at[:, :, c], s_o.at[4, 0], r_o.at[3, 0], partner("c"))
+    arrive(wo.at[:, :, c, :, wo_others], r_wo.at[5])
+    push(wo.at[:, :, c], wo.at[:, :, c], s_wo.at[6], r_wo.at[6], partner("c"))
+    arrive(og.at[:, :, 1 - c], r_o.at[3, 0])
+    arrive(wo.at[:, :, 1 - c], r_wo.at[6])
+
+    gain_two = gn[1:2, :]
+    branch = dot(wo[...].reshape(768, 768), og[...].reshape(768, 256)).T
+    resid = xh[zb, x].reshape(256, 768).astype(FULL) + branch
+    res[...] = resid.reshape(2, 2, 64, 768)
+    unit_two, _ = centred_norm(resid)
+    h2 = (unit_two * gain_two).astype(LOW)
+
+    for kz in range(4):
+        arrive(ffw.at[far_z(kz), 1 - x], r_ff.at[8 + kz])
+    for k, (kc, ky) in enumerate(group):
+        arrive(gb.at[flip(c, kc), flip(y, ky)], r_g.at[k])
+    w_in = ffw[:, :, :, 0:576].reshape(768, 576)
+    w_down = ffw[:, :, :, 576:864].reshape(768, 288)
+    gate_up = dot(h2, w_in)
+    gate, up = gate_up[:, :288], gate_up[:, 288:]
+    grad_out = gb[...].reshape(256, 768)
+    grad_hidden = dot(grad_out, w_down)
+    chance = 0.5 * (1.0 + lax.erf(gate * (1.0 / math.sqrt(2.0))))
+    density = jnp.exp(gate * gate * -0.5) * (1.0 / math.sqrt(2.0 * math.pi))
+    curve = gate * chance
+    hidden = (curve * up).astype(LOW)
+    grad_gate = grad_hidden * up * (chance + gate * density)
+    grad_gate_up = jnp.concatenate([grad_gate, grad_hidden * curve], axis=1).astype(LOW)
+
+    def halve(kind, part):
+        ms[kind] = part.astype(LOW).reshape(2, 2, 64, 768)
+        push(ms.at[kind, 1 - c], ms_c.at[kind], s_ms.at[kind, 0], r_ms.at[kind, 0], partner("c"))
+
+    def quarter(kind):
+        arrive(ms_c.at[kind], r_ms.at[kind, 0])
+        ms_a[kind] = (ms[kind, c, 1 - y].astype(FULL) + ms_c[kind, 1 - y].astype(FULL)).astype(LOW)
+        push(ms_a.at[kind], ms_y.at[kind], s_ms.at[kind, 1], r_ms.at[kind, 1], partner("y"))
+
+    def quarter_sum(kind):
+        arrive(ms_y.at[kind], r_ms.at[kind, 1])
+        return ms[kind, c, y].astype(FULL) + ms_c[kind, y].astype(FULL) + ms_y[kind].astype(FULL)
+
+    halve(0, dot_nt(grad_gate_up, w_in))
+    halve(1, dot_nt(hidden, w_down))
+    quarter(0)
+    h2_t = turned(h2).astype(LOW)
+    gf[:, :, :, 0:576] = dot(h2_t, grad_gate_up).astype(LOW).reshape(4, 2, 96, 576)
+    g_t = turned(grad_out).astype(LOW)
+    gf[:, :, :, 576:864] = dot(g_t, hidden).astype(LOW).reshape(4, 2, 96, 288)
+    for kz in range(4):
+        z_ = far_z(kz)
+        push(gf.at[z_, 1 - x], gf_x.at[z_], s_gf.at[0, kz], r_gf.at[0, kz], partner("x"))
+    quarter(1)
+
+    own_res = res[c, y]
+    unit_two, scale_two = centred_norm(own_res)
+    grad_h2 = quarter_sum(0)
+    grad_resid = gout_ref[...].astype(FULL) + norm_back(unit_two, scale_two, grad_h2 * gain_two)
+    tgrad_ref[...] = grad_resid
+    grad_branch = grad_resid.astype(LOW)
+    db[c, y] = grad_branch
+    grad_o = dot(grad_branch, wo[...].reshape(768, 768)).astype(LOW)
+    own_block = zb * 8 + x * 4 + c * 2 + y
+    for slot_ in range(3):
+        for y_ in range(2):
+            lanes = y_ * 384 + slot_ * 128
+            dos[y_, slot_] = grad_o[:, lanes : lanes + 128]
+            for c_ in range(2):
+                mine = jnp.logical_and(jnp.logical_and(slot == slot_, y == y_), c == c_)
+
+                @pl.when(mine)
+                def _(slot_=slot_, y_=y_):
+                    dop[zb, x, c, y] = dos[y_, slot_]
+
+                push(
+                    dos.at[y_, slot_], dop.at[zb, x, c, y], s_do.at[slot_ * 4 + y_ * 2 + c_], r_do.at[own_block],
+                    at(zh * 2 + slot_ // 2, slot_ % 2, c_, y_), jnp.logical_not(mine),
+                )
+    for k, (kc, ky) in enumerate(group):
+        push(db.at[c, y], db.at[c, y], s_db.at[k], r_db.at[k], at(z, x, flip(c, kc), flip(y, ky)))
+    mixed_ref[...] = (own_res + quarter_sum(1)).astype(LOW)
+    for k, (kc, ky) in enumerate(group):
+        arrive(db.at[flip(c, kc), flip(y, ky)], r_db.at[k])
+    db_t = turned(db[...].reshape(256, 768)).astype(LOW)
+    o_part = og[...].reshape(2, 6, 64, 256)
+    o_pick = jnp.where(y == 0, o_part[0], o_part[1])
+    o_pick = jnp.where(c == 0, o_pick[0:3], o_pick[3:6]).reshape(192, 256)
+    go[...] = dot_nt(db_t, o_pick).astype(LOW).reshape(4, 2, 96, 192)
+    for kz in range(4):
+        z_ = far_z(kz)
+        push(go.at[z_, 1 - x], go_x.at[z_], s_go.at[0, kz], r_go.at[0, kz], partner("x"))
+
+    for b in range(16):
+        z_, x_, c_, y_ = b // 8, (b // 4) % 2, (b // 2) % 2, b % 2
+        arrive(dop.at[z_, x_, c_, y_], r_do.at[b], jnp.logical_and(active, own_block != b))
+
+    @pl.when(active)
+    def _():
+        pair = turned(dop[...].reshape(1024, 128))
+        dot_t[...] = jnp.where(c == 0, pair[0:64], pair[64:128]).astype(LOW)
+
+    def sum_x(kz, mine, other, total, send, recv, landing):
+        z_ = far_z(kz)
+        arrive(other.at[z_], recv.at[0, kz])
+        total[z_] = (mine[z_, x].astype(FULL) + other[z_].astype(FULL)).astype(LOW)
+        if kz:
+            push(total.at[z_], landing.at[kz - 1], send.at[1, kz], recv.at[1, kz], at(z_, x, c, y))
+
+    for part in range(4):
+        cols = pl.ds(part * 256, 256)
+
+        @pl.when(active)
+        def _(part=part, cols=cols):
+            grad_t = dot_t[:, cols]
+            delta = jnp.sum(grad_t.astype(FULL) * ot[part], axis=0, keepdims=True)
+            grad_p = dot(vr[...], grad_t)
+            score_grad = (pt[:, cols].astype(FULL) * (grad_p - delta)).astype(LOW)
+            ds[:, cols] = score_grad
+            back = dot(kt[...], score_grad) * score_scale
+            cosine, sine = cs[0, :, cols], cs[1, :, cols]
+            b1, b2 = back[0:32], back[32:64]
+            dqt[0:64, cols] = jnp.concatenate([b1 * cosine + b2 * sine, b2 * cosine - b1 * sine], axis=0).astype(LOW)
+
+        sum_x(part, gf, gf_x, gf_s, s_gf, r_gf, gf_z)
+
+    @pl.when(active)
+    def _():
+        for part in range(4):
+            cols = pl.ds(part * 256, 256)
+            back = dot_nt(qa[0:64, :], ds[cols, :])
+            cosine, sine = cs[0, :, cols], cs[1, :, cols]
+            b1, b2 = back[0:32], back[32:64]
+            dqt[64:128, cols] = jnp.concatenate([b1 * cosine + b2 * sine, b2 * cosine - b1 * sine], axis=0).astype(LOW)
+            dqt[128:192, cols] = dot_nt(dot_t[...], pt[cols, :]).astype(LOW)
+            dq[cols, :] = turned(dqt[:, cols]).astype(LOW)
+
+    for part in range(4):
+        cols = pl.ds(part * 256, 256)
+
+        @pl.when(active)
+        def _(part=part, cols=cols):
+            d1[part // 2, part % 2] = dot_nt(dq[cols, :], wh[...]).astype(LOW).reshape(2, 2, 64, 768)
+
+        push(
+            d1.at[part // 2, part % 2, 1 - c], d1_c.at[part // 2, part % 2],
+            s_d1.at[0, part], r_d1.at[0, part], partner("c"), active,
+        )
+    for part in range(4):
+        sum_x(part, go, go_x, go_s, s_go, r_go, go_z)
+
+    @pl.when(jnp.logical_not(active))
+    def _():
+        d1_a[...] = jnp.zeros_like(d1_a)
+
+    for part in range(4):
+        arrive(d1_c.at[part // 2, part % 2], r_d1.at[0, part], active)
+
+        @pl.when(active)
+        def _(part=part):
+            both = d1[part // 2, part % 2, c].astype(FULL) + d1_c[part // 2, part % 2].astype(FULL)
+            d1_a[part // 2, part % 2] = both.astype(LOW)
+
+    def remaining(t, step):
+        return tuple(d for d in ("z", "x", "y") if d not in orders[t][:step])
+
+    landing = (d1_r1, d1_r2, d1_r3)
+
+    def step_view(t, step, flipped):
+        dim = orders[t][step]
+        place = {"z": zb, "x": x, "y": y}[dim]
+        place = 1 - place if flipped else place
+        index = tuple(place if d == dim else slice(None) for d in remaining(t, step))
+        if step == 0:
+            return d1_a.at[index + (slice(None), third(t))]
+        return (d1_s1, d1_s2)[step - 1].at[(t,) + index]
+
+    def step_push(t, step):
+        push(
+            step_view(t, step, True), landing[step].at[t], s_d1.at[1 + step, t], r_d1.at[1 + step, t],
+            partner(orders[t][step]),
+        )
+
+    def step_sum(t, step):
+        arrive(landing[step].at[t], r_d1.at[1 + step, t])
+        return step_view(t, step, False)[...].astype(FULL) + landing[step][t].astype(FULL)
+
+    for t in range(3):
+        step_push(t, 0)
+
+    @pl.when(active)
+    def _():
+        grad = dot(dqt[...], h1[...])
+        dw[...] = grad.T.astype(LOW).reshape(16, 48, 192)
+
+    own_head = zh * 6 + slot3 * 2 + c
+
+    @pl.when(active)
+    def _():
+        dw_in[own_head] = dw[seq]
+
+    for k in range(1, 16):
+        z_, x_, c_ = far_z(k // 4), flip(x, (k // 2) % 2), flip(c, k % 2)
+        push(dw.at[z_ * 4 + x_ * 2 + c_], dw_in.at[own_head], s_dw.at[k], r_dw.at[own_head], at(z_, x_, c_, y), active)
+
+    for t in range(3):
+        d1_s1[t] = step_sum(t, 0).astype(LOW)
+        step_push(t, 1)
+
+    def sum_z(total, landed, wide, low, send, recv, coming):
+        value = total[z].astype(FULL)
+        for k in range(1, 4):
+            arrive(landed.at[k - 1], recv.at[1, k])
+            value = value + landed[k - 1].astype(FULL)
+        wide[...] = value.reshape(wide.shape)
+        low[...] = wide[1 - c].astype(LOW)
+        push(low, coming, send.at[2, 0], recv.at[2, 0], partner("c"))
+
+    sum_z(gf_s, gf_z, gf_f, gf_b, s_gf, r_gf, gf_c)
+    for t in range(3):
+        d1_s2[t] = step_sum(t, 1).astype(LOW)
+        step_push(t, 2)
+    sum_z(go_s, go_z, go_f, go_b, s_go, r_go, go_c)
+    arrive(gf_c, r_gf.at[2, 0])
+    ffg_ref[c] = gf_f[c]
+    ffg_ref[1 - c] = gf_c[...].astype(FULL)
+    mlp_terms = jnp.zeros((48, 1), FULL)
+    for c_ in range(2):
+        terms = ffg_ref[c_, :, 0:576] * ffp_ref[c_, :, 0:576].astype(FULL)
+        mlp_terms = mlp_terms + jnp.sum(terms, axis=1, keepdims=True)
+    for h_ in range(2):
+        for j in range(6):
+            arrive(dw_in.at[h_ * 6 + j], r_dw.at[h_ * 6 + j], jnp.logical_not(jnp.logical_and(active, own_head == h_ * 6 + j)))
+    attn_terms = jnp.zeros((48, 1), FULL)
+    for j in range(6):
+        both = dw_in[j].astype(FULL) + dw_in[6 + j].astype(FULL)
+        qkvg_ref[j] = both
+        attn_terms = attn_terms + jnp.sum(both * wq_ref[j].astype(FULL), axis=1, keepdims=True)
+    lane = lax.broadcasted_iota(jnp.int32, (48, 128), 1)
+    gy[...] = jnp.where(lane == 0, attn_terms, jnp.where(lane == 1, mlp_terms, 0.0))
+    push(gy, gy_in, s_gy.at[0], r_gy.at[0], partner("y"))
+    arrive(go_c, r_go.at[2, 0])
+    outg_ref[c] = go_f[c]
+    outg_ref[1 - c] = go_c[...].astype(FULL)
+
+    unit_one, scale_one = centred_norm(tok_ref[...].astype(FULL))
+    for t in range(3):
+        res[0, 0, :, third(t)] = step_sum(t, 2)
+    tgrad_ref[...] = tgrad_ref[...] + norm_back(unit_one, scale_one, res[0, 0] * gn[0:1, :])
+    arrive(gy_in, r_gy.at[0])
+    gains_ref[...] = gy[...] + gy_in[...]
+    for when, copy in pending:
+        if when is None:
+            copy.wait_send()
+        else:
+            pl.when(when)(copy.wait_send)
+
+
+def on_device_fast(tokens, out_grad, short_lengths, attn_gain, qkv_weight, out_weight, mlp_gain, in_weight, down_weight):
+    rows, width = tokens.shape
+    depth = qkv_weight.shape[0]
+    heads_here = qkv_weight.shape[2] // HEAD_DIM
+    count = attn_gain.shape[0]
+    gain_tile = jnp.pad(jnp.stack([attn_gain, mlp_gain]), ((0, 14), (0, 128 - count)))
+    projections = qkv_weight.reshape(depth, 3, heads_here, HEAD_DIM).transpose(2, 0, 1, 3)
+    projections = projections.reshape(heads_here, depth, 3 * HEAD_DIM)
+    inner = jnp.concatenate([in_weight, down_weight.T[:, None]], axis=1)
+    inner = inner.reshape(depth, 3, 2, -1).transpose(2, 0, 1, 3).reshape(2, depth, -1)
+    ff = inner.shape[2]
+    feats = out_weight.shape[0]
+
+    def vm(shape, kind=LOW):
+        return pltpu.VMEM(shape, kind)
+
+    def sem(*shape):
+        return pltpu.SemaphoreType.DMA(shape)
+
+    scratch = [
+        vm((2, 2, 2, 2, 64, 768)), vm((2, 2, 2, 2, 2, 16, 128)), vm((8, 768), FULL), vm((2, 2, 64, 768)),
+        vm((768, 192)), vm((192, 768)), vm((4, 2, 96, 864)), vm((4, 2, 2, 48, 768)), vm((1024, 768)),
+        vm((3, 32, 1024), FULL), vm((128, 1024)), vm((1024, 128)), vm((64, 1024)), vm((64, 1024)), vm((1024, 64)),
+        vm((1024, 1024)), vm((4, 64, 256), FULL), vm((4, 64, 256)), vm((2, 3, 2, 64, 256)), vm((2, 2, 64, 768), FULL),
+        vm((2, 2, 2, 64, 768)), vm((2, 2, 64, 768)), vm((2, 64, 768)), vm((2, 64, 768)), vm((2, 2, 64, 768)),
+        vm((2, 3, 64, 128)), vm((2, 2, 2, 2, 64, 128)), vm((64, 1024)), vm((1024, 1024)), vm((192, 1024)),
+        vm((1024, 192)), vm((2, 2, 2, 2, 64, 768)), vm((2, 2, 2, 64, 768)), vm((2, 2, 2, 64, 768)),
+        vm((3, 2, 2, 64, 256)), vm((3, 2, 2, 64, 256)), vm((3, 2, 64, 256)), vm((3, 2, 64, 256)), vm((3, 64, 256)),
+        vm((16, 48, 192)), vm((12, 48, 192)),
+        vm((4, 2, 96, 864)), vm((4, 96, 864)), vm((4, 96, 864)), vm((3, 96, 864)), vm((2, 48, 864), FULL),
+        vm((48, 864)), vm((48, 864)),
+        vm((4, 2, 96, 192)), vm((4, 96, 192)), vm((4, 96, 192)), vm((3, 96, 192)), vm((2, 48, 192), FULL),
+        vm((48, 192)), vm((48, 192)),
+        vm((48, 128), FULL), vm((48, 128), FULL),
+        sem(4, 3), sem(4, 3), sem(5), sem(5), sem(16), sem(16), sem(3), sem(3), sem(12), sem(12), sem(7), sem(7),
+        sem(5, 2), sem(4, 2), sem(2, 2), sem(2, 2), sem(3), sem(3), sem(12), sem(16), sem(4, 4), sem(4, 4),
+        sem(16), sem(12), sem(3, 4), sem(3, 4), sem(3, 4), sem(3, 4), sem(1), sem(1),
+    ]
+    vmem = pl.BlockSpec(memory_space=pltpu.VMEM)
+    mixed, tokens_grad, gains, qkv_grad, ff_grad, out_grads = pl.pallas_call(
+        whole_layer,
+        out_shape=[
+            jax.ShapeDtypeStruct((rows, width), LOW),
+            jax.ShapeDtypeStruct((rows, width), FULL),
+            jax.ShapeDtypeStruct((depth, 128), FULL),
+            jax.ShapeDtypeStruct((heads_here, depth, 3 * HEAD_DIM), FULL),
+            jax.ShapeDtypeStruct((2, depth, ff), FULL),
+            jax.ShapeDtypeStruct((2, depth, feats // 2), FULL),
+        ],
+        in_specs=[pl.BlockSpec(memory_space=pltpu.SMEM)] + [vmem] * 6,
+        out_specs=[vmem] * 6,
+        scratch_shapes=scratch,
+        compiler_params=pltpu.CompilerParams(collective_id=0, has_side_effects=True, vmem_limit_bytes=60 << 20),
+    )(short_lengths, tokens, out_grad, gain_tile, projections, inner, out_weight.T)
+    mine = lax.dynamic_slice_in_dim(gains, lax.axis_index("head") * count, count, 0)
+    attn_gain_grad = mine[:, 0] / attn_gain.astype(FULL)
+    mlp_gain_grad = mine[:, 1] / mlp_gain.astype(FULL)
+    qkv_weight_grad = qkv_grad.reshape(heads_here, depth, 3, HEAD_DIM).transpose(1, 2, 0, 3).reshape(qkv_weight.shape)
+    ff_grad = ff_grad.reshape(2, depth, 3, -1)
+    in_weight_grad = ff_grad[:, :, :2].transpose(1, 2, 0, 3).reshape(in_weight.shape)
+    down_weight_grad = ff_grad[:, :, 2].transpose(0, 2, 1).reshape(down_weight.shape)
+    out_weight_grad = out_grads.transpose(0, 2, 1).reshape(out_weight.shape)
+    return (
+        mixed, tokens_grad, attn_gain_grad, qkv_weight_grad, out_weight_grad, mlp_gain_grad,
+        in_weight_grad, down_weight_grad,
+    )
+
+
 def solution(mesh):
     placed = (
         P(("seq", "head"), None),
@@ -386,8 +997,9 @@
         P("seq", None, "head"),
         P("head", "seq"),
     )
+    fits = mesh.shape["seq"] == 16 and mesh.shape["head"] == 2
     return jax.shard_map(
-        on_device,
+        on_device_fast if fits else on_device,
         mesh=mesh,
         in_specs=placed,
         out_specs=(

time: 793 us -> 146 us (0.18)
  waiting for transfers between devices: 462 us -> 0 us
  blocking collectives: 160 us -> 0 us
  Pallas kernels: 0 us -> 129 us
  local copies, waits for them, and re-layouts: 70.8 us -> 13.5 us
  matrix products: 51.5 us -> 0 us
  other arithmetic: 26.9 us -> 1.47 us
  between operations: 15.3 us -> 0.81 us
    reduce_scatter x6 -> x0, waiting for transfers between devices: 315 us -> none  [the longest x1 110 us: on_device(): lax.psum_scatter(down_grad, ('seq', 'head'), scatter_dimension=0, tiled=T...]
    all_gather x7 -> x0, waiting for transfers between devices: 146 us -> none  [the longest x1 45.9 us: on_device(): lax.all_gather(in_weight[None], ('seq', 'head'), axis=0, tiled=True)]
    pallas_call x0 -> x1, Pallas kernels: none -> 129 us  [on_device_fast(): pl.pallas_call(whole_layer, out_shape=[jax.ShapeDtypeStruct((rows, width)...]
    unnamed x2 -> x0, blocking collectives: 80.9 us -> none
    all_gather x5 -> x0, blocking collectives: 79 us -> none  [the longest x1 24.1 us: on_device(): lax.all_gather(out_weight, 'seq', axis=1, tiled=True)]
    dot_general x26 -> x0, matrix products: 51.5 us -> none  [the longest x2 8.84 us: key_terms(): jnp.einsum('hqk,qhd->khd', dscore, query_part, preferred_element_type=jnp...]
    dynamic_slice x16 -> x0, local copies, waits for them, and re-layouts: 26.3 us -> none  [the longest x8 16.7 us: piece_rows(): lax.dynamic_slice_in_dim(source, block_begin, block_size, 0)]
    unnamed x83 -> x21, local copies, waits for them, and re-layouts: 15.3 us -> 4.5 us
  transfers between devices with their start and end apart: 13 -> 0, of which waited for: 9 -> 0; matrix products, arithmetic and copies ran while one was open for 12% -> 0% of each run, Pallas kernels for 0% -> 0%
where the time goes in v2:
time: 146 us; the launch traced here: 145 us
  Pallas kernels  129 us (88%)
  local copies, waits for them, and re-layouts  13.5 us (9%)
  other arithmetic  1.47 us (1%)
    pallas_call x1, Pallas kernels, on_device_fast(): pl.pallas_call(whole_layer, out_shape=[jax.ShapeDtypeStruct((rows, width)...  129 us
    unnamed x21, local copies, waits for them, and re-layouts  4.5 us

profile of v2, /device:TPU:0, one launch (start us, length us, event | category | flops | bytes accessed | tf_op | source)
XLA Modules:
  0.0 144.6 jit_solution(14726587707764731543)
XLA Ops:
  0.7 0.6 copy-done.6
  1.3 0.6 fusion.5.refs_3_
  1.9 1.0 concatenate.9
  3.0 0.8 copy-done.3
  3.8 0.2 concatenate.8
  4.1 0.3 maximum_bitcast_fusion
  4.5 0.9 reshape.49.refs_5_
  5.6 0.2 copy.28
  5.8 0.9 reshape.48.refs_4_
  6.6 128.9 %shard_map.152 = (bf16[64,768]{1,0:T(8,128)(2,1)}, f32[64,768]{1,0:T(8,128)}, f32[48,128]{1,0:T(8,128)}, f32[6,48,192]{2,1,0:T(8,128)}, f32[2,48,864]{2,1,0:T(8,128)}, /*index=5*/f32[2,48,192]{2,1,0:T(8,128)}) custom-call(s32[3]{0:T(128)} %refs_0_.1, bf16[64,768]{1,0:T(8,128)(2,1)} %refs_1_.1, bf16[64,768]{1,0:T(8,128)(2,1)} %refs_2_.1, ...), custom_call_target="tpu_custom_call" | custom-call | tf_op jit(solution)/shard_map/pallas_call | solution.py:959
  135.5 1.0 dynamic-slice_reduce_fusion
  136.5 0.5 convert_divide_fusion
  137.0 1.0 copy.32
  138.0 0.8 reshape.52
  138.8 0.3 reshape.53
  139.3 0.2 copy.36
  139.6 1.0 reshape.56
  140.7 0.8 reshape.55
  141.6 0.2 reshape.50
  141.8 0.3 copy.31
  142.1 0.8 reshape.51
  143.0 0.6 copy.43
  143.6 0.3 copy-done.2
  144.0 0.7 copy.44
  (20 shorter events, 0.9 us)
Async XLA Ops:
  0.6 0.7 copy-start.6
  0.6 0.7 copy-start.7
  2.9 0.9 copy-start.3
  4.5 0.9 copy-start.4
  135.5 3.2 %copy-start = (f32[2,48,864]{2,1,0:T(8,128)S(1)}, f32[2,48,864]{2,1,0:T(8,128)}, u32[]{:S(2)}) copy-start(f32[2,48,864]{2,1,0:T(8,128)} %get-tuple-element.19) | copy-start | bytes 995332
  140.6 1.0 copy-start.1
  142.1 0.9 copy-start.5
  143.0 1.0 copy-start.2

commit v3 on v2

--- a/solution.py
+++ b/solution.py
@@ -406,13 +406,14 @@
 
 def whole_layer(*refs):
     (
-        short_ref, tok_ref, gout_ref, gain_ref, wq_ref, ffp_ref, wot_ref,
-        mixed_ref, tgrad_ref, gains_ref, qkvg_ref, ffg_ref, outg_ref,
-        xh, gt, gn, gb, wh, wht, ffw, wo, h1, cs, qa, ka, kt, vt, vr, pt, ot, ol, og, res,
+        short_ref, tok_ref, gout_ref, gain_a, gain_m, qkv_ref, out_ref, in_ref, down_ref,
+        mixed_out, tgrad_out, gains_out, qkvg_out, outg_out, ing_out, downg_out,
+        mixed_ref, tgrad_ref, gains_ref, qkvg_ref, outg_ref, ing_ref, downg_ref,
+        gain_ref, wq_ref, ffp_ref, wot_ref, xh, gt, gn, gb, wh, wht, ffw, wo, h1, cs, qa, ka, kt, vt, vr, pt, ot, ol, og, res,
         ms, ms_c, ms_a, ms_y, db, dos, dop, dot_t, ds, dqt, dq, d1, d1_c, d1_a, d1_r1, d1_s1, d1_r2, d1_s2, d1_r3,
         dw, dw_in, gf, gf_x, gf_s, gf_z, gf_f, gf_b, gf_c, go, go_x, go_s, go_z, go_f, go_b, go_c, gy, gy_in,
         s_tok, r_tok, s_gain, r_gain, s_wq, r_wq, s_g, r_g, s_ff, r_ff, s_wo, r_wo,
-        s_o, r_o, s_ms, r_ms, s_db, r_db, s_do, r_do, s_d1, r_d1, s_dw, r_dw, s_gf, r_gf, s_go, r_go, s_gy, r_gy,
+        s_o, r_o, s_ms, r_ms, s_db, r_db, s_do, r_do, s_d1, r_d1, s_dw, r_dw, s_gf, r_gf, s_go, r_go, s_gy, r_gy, s_out,
     ) = refs
     seq, head = lax.axis_index("seq"), lax.axis_index("head")
     z, x, c, y = seq // 4, (seq // 2) % 2, seq % 2, head
@@ -420,7 +421,7 @@
     slot = zb * 2 + x
     active = slot < 3
     slot3 = jnp.minimum(slot, 2)
-    pending = []
+    pending, delivered = [], []
 
     def flip(value, bit):
         return value if bit == 0 else 1 - value
@@ -451,6 +452,11 @@
             pl.when(when)(copy.start)
         pending.append((when, copy))
 
+    def deliver(k, src, dst):
+        copy = pltpu.make_async_copy(src, dst, s_out.at[k])
+        copy.start()
+        delivered.append(copy)
+
     def arrive(dst, recv, when=None):
         copy = pltpu.make_async_remote_copy(
             src_ref=dst, dst_ref=dst, send_sem=recv, recv_sem=recv,
@@ -469,6 +475,19 @@
             peers.append(at(far_z(kz), flip(x, kx), flip(c, kc), flip(y, ky)))
     for peer in peers:
         pl.semaphore_signal(barrier, inc=1, device_id=peer, device_id_type=pl.DeviceIdType.MESH)
+
+    gain_ref[...] = jnp.zeros_like(gain_ref)
+    gain_ref[0:1, 0 : gain_a.shape[1]] = gain_a[...].astype(FULL)
+    gain_ref[1:2, 0 : gain_m.shape[1]] = gain_m[...].astype(FULL)
+    wot_ref[...] = out_ref[...]
+    for g in range(3):
+        for j in range(6):
+            wq_ref[j, :, g * 64 : g * 64 + 64] = qkv_ref[g, :, j * 64 : j * 64 + 64]
+    for c_ in range(2):
+        lanes = slice(c_ * 288, c_ * 288 + 288)
+        for g in range(2):
+            ffp_ref[c_, :, g * 288 : g * 288 + 288] = in_ref[:, g, lanes]
+        ffp_ref[c_, :, 576:864] = down_ref[:, lanes]
     pl.semaphore_wait(barrier, len(peers))
 
     xh[zb, x, c, y] = tok_ref[...]
@@ -505,6 +524,43 @@
         arrive(gain_view(gain_order[:k], gain_order[k]), r_gain.at[k])
 
     gain_send(0)
+
+    core_rows = pl.ds(pl.multiple_of(c * 48, 16), 48)
+    wo_lanes = pl.ds(pl.multiple_of(y * 384, 128), 384)
+    wo_others = pl.ds(pl.multiple_of((1 - y) * 384, 128), 384)
+
+    def ff_push(k):
+        c_ = flip(c, k % 2)
+        push(ffp_ref.at[c_], ffw.at[z, x, core_rows, :], s_ff.at[k], r_ff.at[k], at(far_z(k // 2), x, c_, y))
+
+    def ff_forward(kz):
+        z_ = far_z(kz)
+        for kc in range(2):
+            if (kz, kc) != (0, 0):
+                rows = pl.ds(pl.multiple_of(flip(c, kc) * 48, 16), 48)
+                arrive(ffw.at[z_, x, rows, :], r_ff.at[kz * 2 + kc])
+        push(ffw.at[z_, x], ffw.at[z_, x], s_ff.at[8 + kz], r_ff.at[8 + kz], partner("x"))
+
+    def wo_forward_x():
+        for k in range(1, 4):
+            arrive(wo.at[far_z(k), x, c, :, wo_lanes], r_wo.at[k])
+        view = wo.at[:, x, c, :, wo_lanes]
+        push(view, view, s_wo.at[4], r_wo.at[4], partner("x"))
+
+    def wo_forward_y():
+        arrive(wo.at[:, 1 - x, c, :, wo_lanes], r_wo.at[4])
+        view = wo.at[:, :, c, :, wo_lanes]
+        push(view, view, s_wo.at[5], r_wo.at[5], partner("y"))
+
+    def wo_forward_core():
+        arrive(wo.at[:, :, c, :, wo_others], r_wo.at[5])
+        push(wo.at[:, :, c], wo.at[:, :, c], s_wo.at[6], r_wo.at[6], partner("c"))
+
+    ffw[z, x, core_rows, :] = ffp_ref[c]
+    wo[z, x, c, :, wo_lanes] = wot_ref[...]
+    ff_push(1)
+    for k in range(1, 4):
+        push(wot_ref, wo.at[z, x, c, :, wo_lanes], s_wo.at[k], r_wo.at[k], at(far_z(k), x, c, y))
 
     own_rows = pl.ds(pl.multiple_of(seq * 48, 16), 48)
     for k in range(16):
@@ -516,29 +572,28 @@
         else:
             push(piece, wh.at[own_rows, :], s_wq.at[k], r_wq.at[k], at(z_, x_, c_, y), slot_ < 3)
 
+    for k in range(2, 8):
+        ff_push(k)
+
     gb[c, y] = gout_ref[...]
     group = ((0, 1), (1, 0), (1, 1))
     for k, (kc, ky) in enumerate(group):
         push(gb.at[c, y], gb.at[c, y], s_g.at[k], r_g.at[k], at(z, x, flip(c, kc), flip(y, ky)))
 
-    core_rows = pl.ds(pl.multiple_of(c * 48, 16), 48)
-    wo_lanes = pl.ds(pl.multiple_of(y * 384, 128), 384)
-    wo_others = pl.ds(pl.multiple_of((1 - y) * 384, 128), 384)
-    ffw[z, x, core_rows, :] = ffp_ref[c]
-    wo[z, x, c, :, wo_lanes] = wot_ref[...]
-    for k in range(1, 4):
-        push(wot_ref, wo.at[z, x, c, :, wo_lanes], s_wo.at[k], r_wo.at[k], at(far_z(k), x, c, y))
-    for k in range(1, 8):
-        c_ = flip(c, k % 2)
-        push(ffp_ref.at[c_], ffw.at[z, x, core_rows, :], s_ff.at[k], r_ff.at[k], at(far_z(k // 2), x, c_, y))
-
-    for step in (1, 2):
+    def token_step(step):
         for t in range(3):
             arrive(blocks(xh, orders[t][: step - 1], third(t), orders[t][step - 1]), r_tok.at[step - 1, t])
             view = blocks(xh, orders[t][:step], third(t))
             push(view, view, s_tok.at[step, t], r_tok.at[step, t], partner(orders[t][step]))
         gain_wait(step - 1)
         gain_send(step)
+
+    ff_forward(0)
+    token_step(1)
+    wo_forward_x()
+    token_step(2)
+    ff_forward(1)
+    wo_forward_y()
     gain_wait(2)
     gain_send(3)
     for t in range(3):
@@ -571,15 +626,16 @@
     gain_wait(3)
     gain_send(4)
     gain_wait(4)
-    tiles = gt[...].reshape(512, 128)
+    tiles = gt[...].reshape(256, 128).astype(LOW)
     width = 24
     pick = lax.broadcasted_iota(jnp.int32, (128, 768), 1) % width == lax.broadcasted_iota(jnp.int32, (128, 768), 0)
     spread = dot(tiles, jnp.where(pick, 1.0, 0.0).astype(LOW))
-    source = lax.broadcasted_iota(jnp.int32, (512, 768), 0)
-    wanted = (lax.broadcasted_iota(jnp.int32, (512, 768), 1) // width) * 16
+    source = lax.broadcasted_iota(jnp.int32, (256, 768), 0)
+    wanted = (lax.broadcasted_iota(jnp.int32, (256, 768), 1) // width) * 8
     gn[0:1, :] = jnp.sum(jnp.where(source == wanted, spread, 0.0), axis=0, keepdims=True)
     gn[1:2, :] = jnp.sum(jnp.where(source == wanted + 1, spread, 0.0), axis=0, keepdims=True)
 
+    ff_forward(2)
     for t in range(3):
         arrive(blocks(xh, ("x", "y", "z"), third(t), "c"), r_tok.at[3, t])
     for k in range(1, 16):
@@ -612,13 +668,8 @@
             ka[cols, :] = jnp.concatenate([kr, cs[2, :, cols], pad], axis=0).T.astype(LOW)
             vr[cols, :] = proj[128:192].T.astype(LOW)
 
-    def ff_forward(kz):
-        z_ = far_z(kz)
-        for kc in range(2):
-            if (kz, kc) != (0, 0):
-                rows = pl.ds(pl.multiple_of(flip(c, kc) * 48, 16), 48)
-                arrive(ffw.at[z_, x, rows, :], r_ff.at[kz * 2 + kc])
-        push(ffw.at[z_, x], ffw.at[z_, x], s_ff.at[8 + kz], r_ff.at[8 + kz], partner("x"))
+    ff_forward(3)
+    wo_forward_core()
 
     for part in range(4):
         cols = pl.ds(part * 256, 256)
@@ -644,24 +695,12 @@
                 ol.at[part], og.at[y, slot3, c], s_o.at[part, y_], r_o.at[slot3, y],
                 at(zh * 2 + part // 2, part % 2, c, y_), jnp.logical_and(active, jnp.logical_not(mine)),
             )
-        ff_forward(part)
-        if part == 1:
-            for k in range(1, 4):
-                arrive(wo.at[far_z(k), x, c, :, wo_lanes], r_wo.at[k])
-            view = wo.at[:, x, c, :, wo_lanes]
-            push(view, view, s_wo.at[4], r_wo.at[4], partner("x"))
-        if part == 3:
-            arrive(wo.at[:, 1 - x, c, :, wo_lanes], r_wo.at[4])
-            view = wo.at[:, :, c, :, wo_lanes]
-            push(view, view, s_wo.at[5], r_wo.at[5], partner("y"))
 
     for slot_ in range(3):
         for y_ in range(2):
             mine = jnp.logical_and(slot == slot_, y == y_)
             arrive(og.at[y_, slot_, c], r_o.at[slot_, y_], jnp.logical_not(mine))
     push(og.at[:, :, c], og.at[:, :, c], s_o.at[4, 0], r_o.at[3, 0], partner("c"))
-    arrive(wo.at[:, :, c, :, wo_others], r_wo.at[5])
-    push(wo.at[:, :, c], wo.at[:, :, c], s_wo.at[6], r_wo.at[6], partner("c"))
     arrive(og.at[:, :, 1 - c], r_o.at[3, 0])
     arrive(wo.at[:, :, 1 - c], r_wo.at[6])
 
@@ -709,7 +748,7 @@
     gf[:, :, :, 0:576] = dot(h2_t, grad_gate_up).astype(LOW).reshape(4, 2, 96, 576)
     g_t = turned(grad_out).astype(LOW)
     gf[:, :, :, 576:864] = dot(g_t, hidden).astype(LOW).reshape(4, 2, 96, 288)
-    for kz in range(4):
+    for kz in (3, 2, 1, 0):
         z_ = far_z(kz)
         push(gf.at[z_, 1 - x], gf_x.at[z_], s_gf.at[0, kz], r_gf.at[0, kz], partner("x"))
     quarter(1)
@@ -741,32 +780,36 @@
     for k, (kc, ky) in enumerate(group):
         push(db.at[c, y], db.at[c, y], s_db.at[k], r_db.at[k], at(z, x, flip(c, kc), flip(y, ky)))
     mixed_ref[...] = (own_res + quarter_sum(1)).astype(LOW)
-    for k, (kc, ky) in enumerate(group):
-        arrive(db.at[flip(c, kc), flip(y, ky)], r_db.at[k])
-    db_t = turned(db[...].reshape(256, 768)).astype(LOW)
-    o_part = og[...].reshape(2, 6, 64, 256)
-    o_pick = jnp.where(y == 0, o_part[0], o_part[1])
-    o_pick = jnp.where(c == 0, o_pick[0:3], o_pick[3:6]).reshape(192, 256)
-    go[...] = dot_nt(db_t, o_pick).astype(LOW).reshape(4, 2, 96, 192)
-    for kz in range(4):
-        z_ = far_z(kz)
-        push(go.at[z_, 1 - x], go_x.at[z_], s_go.at[0, kz], r_go.at[0, kz], partner("x"))
-
-    for b in range(16):
-        z_, x_, c_, y_ = b // 8, (b // 4) % 2, (b // 2) % 2, b % 2
-        arrive(dop.at[z_, x_, c_, y_], r_do.at[b], jnp.logical_and(active, own_block != b))
-
-    @pl.when(active)
-    def _():
-        pair = turned(dop[...].reshape(1024, 128))
-        dot_t[...] = jnp.where(c == 0, pair[0:64], pair[64:128]).astype(LOW)
-
+    deliver(0, mixed_ref, mixed_out)
     def sum_x(kz, mine, other, total, send, recv, landing):
         z_ = far_z(kz)
         arrive(other.at[z_], recv.at[0, kz])
         total[z_] = (mine[z_, x].astype(FULL) + other[z_].astype(FULL)).astype(LOW)
         if kz:
             push(total.at[z_], landing.at[kz - 1], send.at[1, kz], recv.at[1, kz], at(z_, x, c, y))
+
+    def out_share():
+        for k, (kc, ky) in enumerate(group):
+            arrive(db.at[flip(c, kc), flip(y, ky)], r_db.at[k])
+        db_t = turned(db[...].reshape(256, 768)).astype(LOW)
+        o_part = og[...].reshape(2, 6, 64, 256)
+        o_pick = jnp.where(y == 0, o_part[0], o_part[1])
+        o_pick = jnp.where(c == 0, o_pick[0:3], o_pick[3:6]).reshape(192, 256)
+        go[...] = dot_nt(db_t, o_pick).astype(LOW).reshape(4, 2, 96, 192)
+        for kz in (3, 2, 1, 0):
+            z_ = far_z(kz)
+            push(go.at[z_, 1 - x], go_x.at[z_], s_go.at[0, kz], r_go.at[0, kz], partner("x"))
+
+    sum_x(3, gf, gf_x, gf_s, s_gf, r_gf, gf_z)
+
+    for b in range(16):
+        z_, x_, c_, y_ = b // 8, (b // 4) % 2, (b // 2) % 2, b % 2
+        arrive(dop.at[z_, x_, c_, y_], r_do.at[b], jnp.logical_and(active, own_block != b))
+
+    @pl.when(active)
+    def _():
+        pair = turned(dop[...].reshape(1024, 128))
+        dot_t[...] = jnp.where(c == 0, pair[0:64], pair[64:128]).astype(LOW)
 
     for part in range(4):
         cols = pl.ds(part * 256, 256)
@@ -783,7 +826,10 @@
             b1, b2 = back[0:32], back[32:64]
             dqt[0:64, cols] = jnp.concatenate([b1 * cosine + b2 * sine, b2 * cosine - b1 * sine], axis=0).astype(LOW)
 
-        sum_x(part, gf, gf_x, gf_s, s_gf, r_gf, gf_z)
+        if part == 0:
+            out_share()
+        if part < 3:
+            sum_x(2 - part, gf, gf_x, gf_s, s_gf, r_gf, gf_z)
 
     @pl.when(active)
     def _():
@@ -807,7 +853,7 @@
             d1.at[part // 2, part % 2, 1 - c], d1_c.at[part // 2, part % 2],
             s_d1.at[0, part], r_d1.at[0, part], partner("c"), active,
         )
-    for part in range(4):
+    for part in (3, 2, 1, 0):
         sum_x(part, go, go_x, go_s, s_go, r_go, go_z)
 
     @pl.when(jnp.logical_not(active))
@@ -883,33 +929,51 @@
         step_push(t, 2)
     sum_z(go_s, go_z, go_f, go_b, s_go, r_go, go_c)
     arrive(gf_c, r_gf.at[2, 0])
-    ffg_ref[c] = gf_f[c]
-    ffg_ref[1 - c] = gf_c[...].astype(FULL)
+    def by_core(own, other):
+        return jnp.where(c == 0, own, other), jnp.where(c == 0, other, own)
+
     mlp_terms = jnp.zeros((48, 1), FULL)
-    for c_ in range(2):
-        terms = ffg_ref[c_, :, 0:576] * ffp_ref[c_, :, 0:576].astype(FULL)
+    for c_, grads in enumerate(by_core(gf_f[c], gf_c[...].astype(FULL))):
+        lanes = slice(c_ * 288, c_ * 288 + 288)
+        for g in range(2):
+            ing_ref[:, g, lanes] = grads[:, g * 288 : g * 288 + 288]
+        downg_ref[:, lanes] = grads[:, 576:864]
+        terms = grads[:, 0:576] * ffp_ref[c_, :, 0:576].astype(FULL)
         mlp_terms = mlp_terms + jnp.sum(terms, axis=1, keepdims=True)
+    deliver(1, ing_ref, ing_out)
+    deliver(2, downg_ref, downg_out)
     for h_ in range(2):
         for j in range(6):
             arrive(dw_in.at[h_ * 6 + j], r_dw.at[h_ * 6 + j], jnp.logical_not(jnp.logical_and(active, own_head == h_ * 6 + j)))
     attn_terms = jnp.zeros((48, 1), FULL)
     for j in range(6):
         both = dw_in[j].astype(FULL) + dw_in[6 + j].astype(FULL)
-        qkvg_ref[j] = both
+        for g in range(3):
+            qkvg_ref[g, :, j * 64 : j * 64 + 64] = both[:, g * 64 : g * 64 + 64]
         attn_terms = attn_terms + jnp.sum(both * wq_ref[j].astype(FULL), axis=1, keepdims=True)
+    deliver(3, qkvg_ref, qkvg_out)
     lane = lax.broadcasted_iota(jnp.int32, (48, 128), 1)
     gy[...] = jnp.where(lane == 0, attn_terms, jnp.where(lane == 1, mlp_terms, 0.0))
     push(gy, gy_in, s_gy.at[0], r_gy.at[0], partner("y"))
     arrive(go_c, r_go.at[2, 0])
-    outg_ref[c] = go_f[c]
-    outg_ref[1 - c] = go_c[...].astype(FULL)
+    for c_, grads in enumerate(by_core(go_f[c], go_c[...].astype(FULL))):
+        outg_ref[:, c_ * 192 : c_ * 192 + 192] = grads
+    deliver(4, outg_ref, outg_out)
 
     unit_one, scale_one = centred_norm(tok_ref[...].astype(FULL))
     for t in range(3):
         res[0, 0, :, third(t)] = step_sum(t, 2)
     tgrad_ref[...] = tgrad_ref[...] + norm_back(unit_one, scale_one, res[0, 0] * gn[0:1, :])
+    deliver(5, tgrad_ref, tgrad_out)
     arrive(gy_in, r_gy.at[0])
-    gains_ref[...] = gy[...] + gy_in[...]
+    sums = (gy[...] + gy_in[...]).T
+    count = gain_a.shape[1]
+    sums = jnp.where(y == 0, sums[0:2, :count], sums[0:2, count : 2 * count])
+    gains_ref[...] = jnp.zeros_like(gains_ref)
+    gains_ref[0:2, 0:count] = sums / gain_ref[0:2, 0:count]
+    deliver(6, gains_ref, gains_out)
+    for copy in delivered:
+        copy.wait()
     for when, copy in pending:
         if when is None:
             copy.wait_send()
@@ -917,17 +981,28 @@
             pl.when(when)(copy.wait_send)
 
 
+def hand_on(*refs):
+    sources, results, held, sems = refs[:7], refs[7:15], refs[15:21], refs[21]
+    count = results[6].shape[1]
+    results[6][...] = sources[6][0:1, :count]
+    results[7][...] = sources[6][1:2, :count]
+    inward = [pltpu.make_async_copy(a, b, sems.at[0, k]) for k, (a, b) in enumerate(zip(sources[:6], held))]
+    outward = [pltpu.make_async_copy(a, b, sems.at[1, k]) for k, (a, b) in enumerate(zip(held, results[:6]))]
+    for copy in inward:
+        copy.start()
+    for first, second in zip(inward, outward):
+        first.wait()
+        second.start()
+    for copy in outward:
+        copy.wait()
+
+
 def on_device_fast(tokens, out_grad, short_lengths, attn_gain, qkv_weight, out_weight, mlp_gain, in_weight, down_weight):
     rows, width = tokens.shape
     depth = qkv_weight.shape[0]
     heads_here = qkv_weight.shape[2] // HEAD_DIM
     count = attn_gain.shape[0]
-    gain_tile = jnp.pad(jnp.stack([attn_gain, mlp_gain]), ((0, 14), (0, 128 - count)))
-    projections = qkv_weight.reshape(depth, 3, heads_here, HEAD_DIM).transpose(2, 0, 1, 3)
-    projections = projections.reshape(heads_here, depth, 3 * HEAD_DIM)
-    inner = jnp.concatenate([in_weight, down_weight.T[:, None]], axis=1)
-    inner = inner.reshape(depth, 3, 2, -1).transpose(2, 0, 1, 3).reshape(2, depth, -1)
-    ff = inner.shape[2]
+    ff = in_weight.shape[2] // 2 * 3
     feats = out_weight.shape[0]
 
     def vm(shape, kind=LOW):
@@ -936,8 +1011,13 @@
     def sem(*shape):
         return pltpu.SemaphoreType.DMA(shape)
 
-    scratch = [
-        vm((2, 2, 2, 2, 64, 768)), vm((2, 2, 2, 2, 2, 16, 128)), vm((8, 768), FULL), vm((2, 2, 64, 768)),
+    finals = [
+        ((rows, width), LOW), ((rows, width), FULL), ((8, 128), FULL), ((3, depth, 384), FULL),
+        ((depth, feats), FULL), ((depth, 2, 576), FULL), ((depth, 576), FULL),
+    ]
+    scratch = [vm(*shape) for shape in finals] + [
+        vm((8, 128), FULL), vm((heads_here, depth, 192)), vm((2, depth, ff)), vm((depth, feats)),
+        vm((2, 2, 2, 2, 64, 768)), vm((2, 2, 2, 2, 2, 8, 128), FULL), vm((8, 768), FULL), vm((2, 2, 64, 768)),
         vm((768, 192)), vm((192, 768)), vm((4, 2, 96, 864)), vm((4, 2, 2, 48, 768)), vm((1024, 768)),
         vm((3, 32, 1024), FULL), vm((128, 1024)), vm((1024, 128)), vm((64, 1024)), vm((64, 1024)), vm((1024, 64)),
         vm((1024, 1024)), vm((4, 64, 256), FULL), vm((4, 64, 256)), vm((2, 3, 2, 64, 256)), vm((2, 2, 64, 768), FULL),
@@ -953,35 +1033,34 @@
         vm((48, 128), FULL), vm((48, 128), FULL),
         sem(4, 3), sem(4, 3), sem(5), sem(5), sem(16), sem(16), sem(3), sem(3), sem(12), sem(12), sem(7), sem(7),
         sem(5, 2), sem(4, 2), sem(2, 2), sem(2, 2), sem(3), sem(3), sem(12), sem(16), sem(4, 4), sem(4, 4),
-        sem(16), sem(12), sem(3, 4), sem(3, 4), sem(3, 4), sem(3, 4), sem(1), sem(1),
+        sem(16), sem(12), sem(3, 4), sem(3, 4), sem(3, 4), sem(3, 4), sem(1), sem(1), sem(7),
     ]
     vmem = pl.BlockSpec(memory_space=pltpu.VMEM)
-    mixed, tokens_grad, gains, qkv_grad, ff_grad, out_grads = pl.pallas_call(
+    anywhere = pl.BlockSpec(memory_space=pl.ANY)
+    shapes = [jax.ShapeDtypeStruct(*shape) for shape in finals]
+    mixed, tokens_grad, gains, qkv_grad, out_grads, in_grad, down_grad = pl.pallas_call(
         whole_layer,
-        out_shape=[
-            jax.ShapeDtypeStruct((rows, width), LOW),
-            jax.ShapeDtypeStruct((rows, width), FULL),
-            jax.ShapeDtypeStruct((depth, 128), FULL),
-            jax.ShapeDtypeStruct((heads_here, depth, 3 * HEAD_DIM), FULL),
-            jax.ShapeDtypeStruct((2, depth, ff), FULL),
-            jax.ShapeDtypeStruct((2, depth, feats // 2), FULL),
-        ],
-        in_specs=[pl.BlockSpec(memory_space=pltpu.SMEM)] + [vmem] * 6,
-        out_specs=[vmem] * 6,
+        out_shape=shapes,
+        in_specs=[pl.BlockSpec(memory_space=pltpu.SMEM)] + [vmem] * 8,
+        out_specs=[anywhere] * 7,
         scratch_shapes=scratch,
         compiler_params=pltpu.CompilerParams(collective_id=0, has_side_effects=True, vmem_limit_bytes=60 << 20),
-    )(short_lengths, tokens, out_grad, gain_tile, projections, inner, out_weight.T)
-    mine = lax.dynamic_slice_in_dim(gains, lax.axis_index("head") * count, count, 0)
-    attn_gain_grad = mine[:, 0] / attn_gain.astype(FULL)
-    mlp_gain_grad = mine[:, 1] / mlp_gain.astype(FULL)
-    qkv_weight_grad = qkv_grad.reshape(heads_here, depth, 3, HEAD_DIM).transpose(1, 2, 0, 3).reshape(qkv_weight.shape)
-    ff_grad = ff_grad.reshape(2, depth, 3, -1)
-    in_weight_grad = ff_grad[:, :, :2].transpose(1, 2, 0, 3).reshape(in_weight.shape)
-    down_weight_grad = ff_grad[:, :, 2].transpose(0, 2, 1).reshape(down_weight.shape)
-    out_weight_grad = out_grads.transpose(0, 2, 1).reshape(out_weight.shape)
+    )(
+        short_lengths, tokens, out_grad, attn_gain[None], mlp_gain[None],
+        qkv_weight.transpose(1, 0, 2), out_weight.T, in_weight, down_weight.T,
+    )
+    grads = (mixed, tokens_grad, qkv_grad, out_grads, in_grad, down_grad)
+    count = attn_gain.shape[0]
+    mixed, tokens_grad, qkv_grad, out_grads, in_grad, down_grad, attn_gain_grad, mlp_gain_grad = pl.pallas_call(
+        hand_on,
+        out_shape=[jax.ShapeDtypeStruct(a.shape, a.dtype) for a in grads] + [jax.ShapeDtypeStruct((1, count), FULL)] * 2,
+        in_specs=[anywhere] * 6 + [vmem],
+        out_specs=[anywhere] * 6 + [vmem] * 2,
+        scratch_shapes=[vm(a.shape, a.dtype) for a in grads] + [sem(2, 6)],
+    )(*grads, gains)
     return (
-        mixed, tokens_grad, attn_gain_grad, qkv_weight_grad, out_weight_grad, mlp_gain_grad,
-        in_weight_grad, down_weight_grad,
+        mixed, tokens_grad, attn_gain_grad[0], qkv_grad.transpose(1, 0, 2), out_grads.T, mlp_gain_grad[0],
+        in_grad, down_grad.T,
     )
 
 

time: 146 us -> 113 us (0.77)
  Pallas kernels: 129 us -> 112 us
  local copies, waits for them, and re-layouts: 13.5 us -> 0 us
  other arithmetic: 1.47 us -> 0 us
    pallas_call x1 -> x2, Pallas kernels: 129 us -> 112 us  [the longest x1 108 us: on_device_fast(): pl.pallas_call(whole_layer, out_shape=shapes, in_specs=[pl.BlockSpec(memo...]
    reshape x8 -> x0, local copies, waits for them, and re-layouts: 4.82 us -> none  [the longest x2 1.04 us: on_device_fast(): qkv_grad.reshape(heads_here, depth, 3, HEAD_DIM).transpose(1, 2, 0, 3)]
    unnamed x21 -> x0, local copies, waits for them, and re-layouts: 4.5 us -> none
    transpose x5 -> x0, local copies, waits for them, and re-layouts: 1.61 us -> none  [the longest x1 0.97 us: on_device_fast(): out_weight_grad = out_grads.transpose(0, 2, 1).reshape(out_weight.shape)]
where the time goes in v3:
time: 113 us; the launch traced here: 112 us
  Pallas kernels  112 us (99%)
    pallas_call x1, Pallas kernels, on_device_fast(): pl.pallas_call(whole_layer, out_shape=shapes, in_specs=[pl.BlockSpec(memo...  108 us
    pallas_call x1, Pallas kernels, on_device_fast(): pl.pallas_call(hand_on, out_shape=[jax.ShapeDtypeStruct(a.shape, a.dtype)...  3.27 us

profile of v3, /device:TPU:0, one launch (start us, length us, event | category | flops | bytes accessed | tf_op | source)
XLA Modules:
  0.0 112.4 jit_solution(254924027558749044)
XLA Ops:
  0.6 108.4 %shard_map.152 = (bf16[64,768]{1,0:T(8,128)(2,1)}, f32[64,768]{1,0:T(8,128)}, f32[8,128]{1,0:T(8,128)}, f32[3,48,384]{2,1,0:T(8,128)}, f32[48,384]{1,0:T(8,128)}...) custom-call(s32[3]{0:T(128)} %refs_0_.1, bf16[64,768]{1,0:T(8,128)(2,1)} %refs_1_.1, bf16[64,768]{1,0:T(8,128)(2,1)} %refs_2_.1, ...), custom_call_target="tpu_custom_call" | custom-call | tf_op jit(solution)/shard_map/pallas_call | solution.py:1041
  109.0 3.3 %shard_map.153 = (bf16[64,768]{1,0:T(8,128)(2,1)}, f32[64,768]{1,0:T(8,128)}, f32[3,48,384]{2,1,0:T(8,128)}, f32[48,384]{1,0:T(8,128)}, f32[48,2,576]{2,1,0:T(2,...) custom-call(bf16[64,768]{1,0:T(8,128)(2,1)} %get-tuple-element.23.refs_0_, ...), custom_call_target="tpu_custom_call" | custom-call | tf_op jit(solution)/shard_map/pallas_call | solution.py:1054

commit v4 on v3

--- a/solution.py
+++ b/solution.py
@@ -411,7 +411,7 @@
         mixed_ref, tgrad_ref, gains_ref, qkvg_ref, outg_ref, ing_ref, downg_ref,
         gain_ref, wq_ref, ffp_ref, wot_ref, xh, gt, gn, gb, wh, wht, ffw, wo, h1, cs, qa, ka, kt, vt, vr, pt, ot, ol, og, res,
         ms, ms_c, ms_a, ms_y, db, dos, dop, dot_t, ds, dqt, dq, d1, d1_c, d1_a, d1_r1, d1_s1, d1_r2, d1_s2, d1_r3,
-        dw, dw_in, gf, gf_x, gf_s, gf_z, gf_f, gf_b, gf_c, go, go_x, go_s, go_z, go_f, go_b, go_c, gy, gy_in,
+        dw, dw_in, gf, gf_k, gf_s, gf_z, gf_y, gf_f, gf_b, gf_c, go, go_k, go_s, go_z, go_y, go_f, go_b, go_c, gy, gy_in,
         s_tok, r_tok, s_gain, r_gain, s_wq, r_wq, s_g, r_g, s_ff, r_ff, s_wo, r_wo,
         s_o, r_o, s_ms, r_ms, s_db, r_db, s_do, r_do, s_d1, r_d1, s_dw, r_dw, s_gf, r_gf, s_go, r_go, s_gy, r_gy, s_out,
     ) = refs
@@ -490,8 +490,8 @@
         ffp_ref[c_, :, 576:864] = down_ref[:, lanes]
     pl.semaphore_wait(barrier, len(peers))
 
-    xh[zb, x, c, y] = tok_ref[...]
-    orders = (("x", "y", "z"), ("y", "z", "x"), ("z", "x", "y"))
+    xh[zb, c, x, y] = tok_ref[...]
+    orders = (("z", "x", "y"), ("z", "y", "x"), ("z", "x", "y"))
 
     def third(t):
         return pl.ds(t * 256, 256)
@@ -500,7 +500,7 @@
         there = {"z": zb, "x": x, "y": y, "c": c if core is None else core}
         if flipped is not None:
             there[flipped] = 1 - there[flipped]
-        index = tuple(slice(None) if d in opened else there[d] for d in ("z", "x", "c", "y"))
+        index = tuple(slice(None) if d in opened else there[d] for d in ("z", "c", "x", "y"))
         return ref.at[index + (slice(None), lanes)]
 
     for t in range(3):
@@ -508,7 +508,7 @@
         push(view, view, s_tok.at[0, t], r_tok.at[0, t], partner(orders[t][0]))
 
     gt[zh, zb, x, c, y] = gain_ref[...]
-    gain_order = ("x", "y", "z", "h", "c")
+    gain_order = ("c", "h", "x", "y", "z")
 
     def gain_view(opened, flipped=None):
         there = {"h": zh, "z": zb, "x": x, "c": c, "y": y}
@@ -525,21 +525,39 @@
 
     gain_send(0)
 
-    core_rows = pl.ds(pl.multiple_of(c * 48, 16), 48)
     wo_lanes = pl.ds(pl.multiple_of(y * 384, 128), 384)
     wo_others = pl.ds(pl.multiple_of((1 - y) * 384, 128), 384)
 
-    def ff_push(k):
-        c_ = flip(c, k % 2)
-        push(ffp_ref.at[c_], ffw.at[z, x, core_rows, :], s_ff.at[k], r_ff.at[k], at(far_z(k // 2), x, c_, y))
-
-    def ff_forward(kz):
+    def ff_share(src, z_, x_, k, dim):
+        push(src, ffw.at[z_, x_, c], s_ff.at[k], r_ff.at[k], partner(dim))
+
+    def ff_arrive(kz, kx, k):
+        arrive(ffw.at[far_z(kz), flip(x, kx), c], r_ff.at[k])
+
+    def ff_cross():
+        ff_arrive(0, 1, 0)
+        ff_share(ffw.at[z, 1 - x, c], z, 1 - x, 2, "h")
+        ff_share(ffw.at[z, 1 - x, c], z, 1 - x, 4, "z")
+
+    def ff_relay():
+        for kx in range(2):
+            ff_arrive(2, kx, 1 + kx)
+            z_, x_ = far_z(2), flip(x, kx)
+            ff_share(ffw.at[z_, x_, c], z_, x_, 5 + kx, "z")
+
+    def ff_core(kz):
         z_ = far_z(kz)
-        for kc in range(2):
-            if (kz, kc) != (0, 0):
-                rows = pl.ds(pl.multiple_of(flip(c, kc) * 48, 16), 48)
-                arrive(ffw.at[z_, x, rows, :], r_ff.at[kz * 2 + kc])
-        push(ffw.at[z_, x], ffw.at[z_, x], s_ff.at[8 + kz], r_ff.at[8 + kz], partner("x"))
+        push(ffw.at[z_, :, c], ffw.at[z_, :, c], s_ff.at[8 + kz], r_ff.at[8 + kz], partner("c"))
+
+    def ff_near():
+        for kx in range(2):
+            ff_arrive(1, kx, 3 + kx)
+        ff_core(1)
+
+    def ff_last():
+        for kx in range(2):
+            ff_arrive(3, kx, 5 + kx)
+        ff_core(3)
 
     def wo_forward_x():
         for k in range(1, 4):
@@ -556,53 +574,88 @@
         arrive(wo.at[:, :, c, :, wo_others], r_wo.at[5])
         push(wo.at[:, :, c], wo.at[:, :, c], s_wo.at[6], r_wo.at[6], partner("c"))
 
-    ffw[z, x, core_rows, :] = ffp_ref[c]
+    ffw[z, x, c] = ffp_ref[x]
     wo[z, x, c, :, wo_lanes] = wot_ref[...]
-    ff_push(1)
-    for k in range(1, 4):
-        push(wot_ref, wo.at[z, x, c, :, wo_lanes], s_wo.at[k], r_wo.at[k], at(far_z(k), x, c, y))
+    def wo_push():
+        for k in (2, 3, 1):
+            push(wot_ref, wo.at[z, x, c, :, wo_lanes], s_wo.at[k], r_wo.at[k], at(far_z(k), x, c, y))
 
     own_rows = pl.ds(pl.multiple_of(seq * 48, 16), 48)
-    for k in range(16):
-        z_, x_, c_ = far_z(k // 4), flip(x, (k // 2) % 2), flip(c, k % 2)
-        slot_ = (z_ % 2) * 2 + x_
-        piece = wq_ref.at[jnp.minimum(slot_ * 2 + c_, 5)]
-        if k == 0:
-            wh[own_rows, :] = piece[...]
-        else:
+    wh[own_rows, :] = wq_ref[jnp.minimum(slot * 2 + c, 5)]
+
+    def head_push():
+        for k in range(1, 16):
+            z_, x_, c_ = far_z(k // 4), flip(x, (k // 2) % 2), flip(c, k % 2)
+            slot_ = (z_ % 2) * 2 + x_
+            piece = wq_ref.at[jnp.minimum(slot_ * 2 + c_, 5)]
             push(piece, wh.at[own_rows, :], s_wq.at[k], r_wq.at[k], at(z_, x_, c_, y), slot_ < 3)
 
-    for k in range(2, 8):
-        ff_push(k)
-
-    gb[c, y] = gout_ref[...]
+    gb[x, y] = gout_ref[...]
     group = ((0, 1), (1, 0), (1, 1))
-    for k, (kc, ky) in enumerate(group):
-        push(gb.at[c, y], gb.at[c, y], s_g.at[k], r_g.at[k], at(z, x, flip(c, kc), flip(y, ky)))
+
+    def member(kx, ky):
+        return at(z, flip(x, kx), c, flip(y, ky))
+
+    def grad_push():
+        for k, (kx, ky) in enumerate(group):
+            push(gb.at[x, y], gb.at[x, y], s_g.at[k], r_g.at[k], member(kx, ky))
 
     def token_step(step):
         for t in range(3):
             arrive(blocks(xh, orders[t][: step - 1], third(t), orders[t][step - 1]), r_tok.at[step - 1, t])
             view = blocks(xh, orders[t][:step], third(t))
             push(view, view, s_tok.at[step, t], r_tok.at[step, t], partner(orders[t][step]))
-        gain_wait(step - 1)
-        gain_send(step)
-
-    ff_forward(0)
+        gain_wait(step)
+        gain_send(step + 1)
+
+    events = {
+        "fx": lambda: ff_share(ffp_ref.at[1 - x], z, x, 0, "x"),
+        "f2": lambda: ff_share(ffp_ref.at[x], z, x, 1, "h"),
+        "f1": lambda: ff_share(ffp_ref.at[x], z, x, 3, "z"),
+        "fc": ff_cross,
+        "fr": ff_relay,
+        "c0": lambda: ff_core(0),
+        "c1": ff_near,
+        "c2": lambda: ff_core(2),
+        "c3": ff_last,
+        "w": head_push,
+        "g": grad_push,
+        "oz": wo_push,
+        "ox": wo_forward_x,
+        "oy": wo_forward_y,
+        "oc": wo_forward_core,
+    }
+
+    def run(point):
+        for name in plan[point]:
+            events[name]()
+
+    plan = (
+        ("w",),
+        ("f2", "fx", "f1", "oz"),
+        ("fc", "ox", "g"),
+        ("fr", "c0", "c1", "oy"),
+        ("c2",),
+        (),
+        (),
+        (),
+        ("c3", "oc"),
+    )
+    run(0)
+    gain_wait(0)
+    gain_send(1)
     token_step(1)
-    wo_forward_x()
+    run(1)
     token_step(2)
-    ff_forward(1)
-    wo_forward_y()
-    gain_wait(2)
-    gain_send(3)
-    for t in range(3):
-        arrive(blocks(xh, orders[t][:2], third(t), orders[t][2]), r_tok.at[2, t])
-        view = blocks(xh, ("x", "y", "z"), third(t))
-        push(view, view, s_tok.at[3, t], r_tok.at[3, t], partner("c"))
+    run(2)
+    gain_wait(3)
+    gain_send(4)
+    run(3)
 
     half_rows = 1024
-    row = lax.broadcasted_iota(jnp.int32, (32, half_rows), 1) + zh * half_rows
+    lane = lax.broadcasted_iota(jnp.int32, (32, half_rows), 1)
+    row = lane % 64 + (lane // 64 % 2) * 64 + (lane // 256 % 2) * 128 + (lane // 128 % 2) * 256 + (lane // 512) * 512
+    row = row + zh * half_rows
     feature = lax.broadcasted_iota(jnp.int32, (32, half_rows), 0)
     bound = jnp.int32(2 * half_rows)
     for b in range(short_ref.shape[0]):
@@ -623,8 +676,6 @@
     qa[64:96, :] = ((same - 1.0) * 1e30).astype(LOW)
     qa[96:128, :] = jnp.zeros((32, half_rows), LOW)
 
-    gain_wait(3)
-    gain_send(4)
     gain_wait(4)
     tiles = gt[...].reshape(256, 128).astype(LOW)
     width = 24
@@ -635,27 +686,37 @@
     gn[0:1, :] = jnp.sum(jnp.where(source == wanted, spread, 0.0), axis=0, keepdims=True)
     gn[1:2, :] = jnp.sum(jnp.where(source == wanted + 1, spread, 0.0), axis=0, keepdims=True)
 
-    ff_forward(2)
     for t in range(3):
-        arrive(blocks(xh, ("x", "y", "z"), third(t), "c"), r_tok.at[3, t])
+        arrive(blocks(xh, orders[t][:2], third(t), orders[t][2]), r_tok.at[2, t])
+
+    def rows_of(z_, c_):
+        return pl.ds(pl.multiple_of(z_ * 512 + c_ * 256, 256), 256)
+
+    for z_ in range(2):
+        rows = rows_of(z_, c)
+
+        @pl.when(active)
+        def _(z_=z_, rows=rows):
+            unit, _ = centred_norm(xh[z_, c].reshape(256, 768).astype(FULL))
+            h1[rows, :] = (unit * gn[0:1, :]).astype(LOW)
+
+        push(h1.at[rows, :], h1.at[rows, :], s_tok.at[3, z_], r_tok.at[3, z_], partner("c"), active)
     for k in range(1, 16):
         source_seq = far_z(k // 4) * 4 + flip(x, (k // 2) % 2) * 2 + flip(c, k % 2)
         arrive(wh.at[pl.ds(pl.multiple_of(source_seq * 48, 16), 48), :], r_wq.at[k], active)
 
     @pl.when(active)
     def _():
-        gain = gn[0:1, :]
-
-        def normed_block(b, carry):
-            rows = xh[b // 8, (b // 4) % 2, (b // 2) % 2, b % 2].astype(FULL)
-            unit, _ = centred_norm(rows)
-            h1[pl.ds(pl.multiple_of(b * 64, 64), 64), :] = (unit * gain).astype(LOW)
-            return carry
-
-        lax.fori_loop(0, 16, normed_block, 0)
         wht[...] = turned(wh[...]).astype(LOW)
-        for part in range(4):
-            cols = pl.ds(part * 256, 256)
+
+    for part in range(4):
+        z_, c_ = part % 2, flip(c, part // 2)
+        cols = rows_of(z_, c_)
+        if part >= 2:
+            arrive(h1.at[cols, :], r_tok.at[3, z_], active)
+
+        @pl.when(active)
+        def _(cols=cols):
             proj = dot_nt(wht[...], h1[cols, :])
             cosine, sine = cs[0, :, cols], cs[1, :, cols]
             q1, q2, k1, k2 = proj[0:32], proj[32:64], proj[64:96], proj[96:128]
@@ -668,8 +729,7 @@
             ka[cols, :] = jnp.concatenate([kr, cs[2, :, cols], pad], axis=0).T.astype(LOW)
             vr[cols, :] = proj[128:192].T.astype(LOW)
 
-    ff_forward(3)
-    wo_forward_core()
+    run(4)
 
     for part in range(4):
         cols = pl.ds(part * 256, 256)
@@ -684,39 +744,41 @@
             ot[part] = result
             ol[part] = result.astype(LOW)
 
-        for y_ in range(2):
-            mine = jnp.logical_and(slot == part, y == y_)
+        own_group = jnp.logical_and(zb == part // 2, c == part % 2)
+        for k in range(4):
+            x_, y_ = k // 2, k % 2
+            mine = jnp.logical_and(own_group, jnp.logical_and(x == x_, y == y_))
 
             @pl.when(jnp.logical_and(active, mine))
             def _(part=part):
                 og[y, slot3, c] = ol[part]
 
             push(
-                ol.at[part], og.at[y, slot3, c], s_o.at[part, y_], r_o.at[slot3, y],
-                at(zh * 2 + part // 2, part % 2, c, y_), jnp.logical_and(active, jnp.logical_not(mine)),
+                ol.at[part], og.at[y, slot3, c], s_o.at[part, k], r_o.at[slot3, c, y],
+                at(zh * 2 + part // 2, x_, part % 2, y_), jnp.logical_and(active, jnp.logical_not(mine)),
             )
+        run(5 + part)
 
     for slot_ in range(3):
-        for y_ in range(2):
-            mine = jnp.logical_and(slot == slot_, y == y_)
-            arrive(og.at[y_, slot_, c], r_o.at[slot_, y_], jnp.logical_not(mine))
-    push(og.at[:, :, c], og.at[:, :, c], s_o.at[4, 0], r_o.at[3, 0], partner("c"))
-    arrive(og.at[:, :, 1 - c], r_o.at[3, 0])
+        for c_ in range(2):
+            for y_ in range(2):
+                mine = jnp.logical_and(slot == slot_, jnp.logical_and(c == c_, y == y_))
+                arrive(og.at[y_, slot_, c_], r_o.at[slot_, c_, y_], jnp.logical_not(mine))
     arrive(wo.at[:, :, 1 - c], r_wo.at[6])
 
     gain_two = gn[1:2, :]
     branch = dot(wo[...].reshape(768, 768), og[...].reshape(768, 256)).T
-    resid = xh[zb, x].reshape(256, 768).astype(FULL) + branch
+    resid = xh[zb, c].reshape(256, 768).astype(FULL) + branch
     res[...] = resid.reshape(2, 2, 64, 768)
     unit_two, _ = centred_norm(resid)
     h2 = (unit_two * gain_two).astype(LOW)
 
     for kz in range(4):
-        arrive(ffw.at[far_z(kz), 1 - x], r_ff.at[8 + kz])
-    for k, (kc, ky) in enumerate(group):
-        arrive(gb.at[flip(c, kc), flip(y, ky)], r_g.at[k])
-    w_in = ffw[:, :, :, 0:576].reshape(768, 576)
-    w_down = ffw[:, :, :, 576:864].reshape(768, 288)
+        arrive(ffw.at[far_z(kz), :, 1 - c], r_ff.at[8 + kz])
+    for k, (kx, ky) in enumerate(group):
+        arrive(gb.at[flip(x, kx), flip(y, ky)], r_g.at[k])
+    w_in = ffw[:, :, :, :, 0:576].reshape(768, 576)
+    w_down = ffw[:, :, :, :, 576:864].reshape(768, 288)
     gate_up = dot(h2, w_in)
     gate, up = gate_up[:, :288], gate_up[:, 288:]
     grad_out = gb[...].reshape(256, 768)
@@ -728,40 +790,133 @@
     grad_gate = grad_hidden * up * (chance + gate * density)
     grad_gate_up = jnp.concatenate([grad_gate, grad_hidden * curve], axis=1).astype(LOW)
 
+    columns = (slice(0, 384), slice(384, 768))
+
     def halve(kind, part):
         ms[kind] = part.astype(LOW).reshape(2, 2, 64, 768)
-        push(ms.at[kind, 1 - c], ms_c.at[kind], s_ms.at[kind, 0], r_ms.at[kind, 0], partner("c"))
+        push(ms.at[kind, 1 - x, :, :, columns[0]], ms_c.at[kind, 0], s_ms.at[kind, 0, 0], r_ms.at[kind, 0, 0], partner("x"))
+        push(ms.at[kind, :, 1 - y, :, columns[1]], ms_c.at[kind, 1], s_ms.at[kind, 1, 0], r_ms.at[kind, 1, 0], partner("y"))
 
     def quarter(kind):
-        arrive(ms_c.at[kind], r_ms.at[kind, 0])
-        ms_a[kind] = (ms[kind, c, 1 - y].astype(FULL) + ms_c[kind, 1 - y].astype(FULL)).astype(LOW)
-        push(ms_a.at[kind], ms_y.at[kind], s_ms.at[kind, 1], r_ms.at[kind, 1], partner("y"))
+        for t in range(2):
+            arrive(ms_c.at[kind, t], r_ms.at[kind, t, 0])
+            mine = ms[kind, x, 1 - y, :, columns[0]] if t == 0 else ms[kind, 1 - x, y, :, columns[1]]
+            other = ms_c[kind, t, 1 - y] if t == 0 else ms_c[kind, t, 1 - x]
+            ms_a[kind, t] = (mine.astype(FULL) + other.astype(FULL)).astype(LOW)
+            push(ms_a.at[kind, t], ms_y.at[kind, t], s_ms.at[kind, t, 1], r_ms.at[kind, t, 1], partner("yx"[t]))
 
     def quarter_sum(kind):
-        arrive(ms_y.at[kind], r_ms.at[kind, 1])
-        return ms[kind, c, y].astype(FULL) + ms_c[kind, y].astype(FULL) + ms_y[kind].astype(FULL)
+        sums = []
+        for t in range(2):
+            arrive(ms_y.at[kind, t], r_ms.at[kind, t, 1])
+            other = ms_c[kind, t, y] if t == 0 else ms_c[kind, t, x]
+            mine = ms[kind, x, y, :, columns[t]].astype(FULL) + other.astype(FULL)
+            sums.append(mine + ms_y[kind, t].astype(FULL))
+        return jnp.concatenate(sums, axis=1)
 
     halve(0, dot_nt(grad_gate_up, w_in))
+    h2_t = turned(h2).astype(LOW)
+    gf[:, :, :, :, 0:576] = dot(h2_t, grad_gate_up).astype(LOW).reshape(4, 2, 2, 48, 576)
+    g_t = turned(grad_out).astype(LOW)
+    gf[:, :, :, :, 576:864] = dot(g_t, hidden).astype(LOW).reshape(4, 2, 2, 48, 288)
+
+    def sums_of(whole, crossed, low, near, far, wide, last, coming, send, recv):
+        def cross():
+            for kz in (3, 1, 2, 0):
+                z_ = far_z(kz)
+                push(whole.at[z_, :, 1 - c], crossed.at[z_], send.at[0, kz], recv.at[0, kz], partner("c"))
+
+        def pair(kz):
+            z_ = far_z(kz)
+            arrive(crossed.at[z_], recv.at[0, kz])
+            return whole[z_, :, c].astype(FULL) + crossed[z_].astype(FULL)
+
+        def to_near(kz):
+            z_ = far_z(kz)
+            low[z_] = pair(kz).astype(LOW)
+            push(low.at[z_], near.at[kz // 2], send.at[1, kz // 2], recv.at[1, kz // 2], partner("z"))
+
+        def to_far():
+            value = pair(2)
+            arrive(near.at[1], recv.at[1, 1])
+            low[far_z(2)] = (value + near[1].astype(FULL)).astype(LOW)
+            push(low.at[far_z(2)], far, send.at[2, 0], recv.at[2, 0], partner("h"))
+
+        def finish():
+            value = pair(0)
+            arrive(near.at[0], recv.at[1, 0])
+            arrive(far, recv.at[2, 0])
+            wide[...] = value + near[0].astype(FULL) + far[...].astype(FULL)
+            last[...] = wide[1 - x].astype(LOW)
+            push(last, coming, send.at[3, 0], recv.at[3, 0], partner("x"))
+
+        def result():
+            arrive(coming, recv.at[3, 0])
+            own, other = wide[x], coming[...].astype(FULL)
+            return jnp.where(x == 0, own, other), jnp.where(x == 0, other, own)
+
+        return cross, to_near, to_far, finish, result
+
+    ff_sums = sums_of(gf, gf_k, gf_s, gf_z, gf_y, gf_f, gf_b, gf_c, s_gf, r_gf)
+    out_sums = sums_of(go, go_k, go_s, go_z, go_y, go_f, go_b, go_c, s_go, r_go)
+
+    def out_share():
+        for k, (kx, ky) in enumerate(group):
+            arrive(db.at[flip(x, kx), flip(y, ky)], r_db.at[k])
+        db_t = turned(db[...].reshape(256, 768)).astype(LOW)
+        o_part = og[...].reshape(2, 6, 64, 256)
+        o_pick = jnp.where(y == 0, o_part[0], o_part[1])
+        o_pick = jnp.where(x == 0, o_pick[0:3], o_pick[3:6]).reshape(192, 256)
+        go[...] = dot_nt(db_t, o_pick).astype(LOW).reshape(4, 2, 2, 48, 192)
+        out_sums[0]()
+
+    def mixed_done():
+        mixed_ref[...] = (res[x, y] + quarter_sum(1)).astype(LOW)
+        deliver(0, mixed_ref, mixed_out)
+
+    later = {
+        "md": mixed_done,
+        "mx": lambda: quarter(1),
+        "n3": lambda: ff_sums[1](3),
+        "n1": lambda: ff_sums[1](1),
+        "f": ff_sums[2],
+        "e": ff_sums[3],
+        "O": out_share,
+        "O3": lambda: out_sums[1](3),
+        "O1": lambda: out_sums[1](1),
+        "Of": out_sums[2],
+        "Oe": out_sums[3],
+    }
+    then = (
+        ("n3",),
+        ("mx", "n1"),
+        (),
+        ("O", "f"),
+        ("O3", "O1", "md"),
+        (),
+        (),
+        ("Of",),
+        ("Oe", "e"),
+        (),
+    )
+
+    def run_later(point):
+        for name in then[point]:
+            later[name]()
+
+    ff_sums[0]()
+    quarter(0)
     halve(1, dot_nt(hidden, w_down))
-    quarter(0)
-    h2_t = turned(h2).astype(LOW)
-    gf[:, :, :, 0:576] = dot(h2_t, grad_gate_up).astype(LOW).reshape(4, 2, 96, 576)
-    g_t = turned(grad_out).astype(LOW)
-    gf[:, :, :, 576:864] = dot(g_t, hidden).astype(LOW).reshape(4, 2, 96, 288)
-    for kz in (3, 2, 1, 0):
-        z_ = far_z(kz)
-        push(gf.at[z_, 1 - x], gf_x.at[z_], s_gf.at[0, kz], r_gf.at[0, kz], partner("x"))
-    quarter(1)
-
-    own_res = res[c, y]
+    run_later(0)
+    own_res = res[x, y]
     unit_two, scale_two = centred_norm(own_res)
     grad_h2 = quarter_sum(0)
     grad_resid = gout_ref[...].astype(FULL) + norm_back(unit_two, scale_two, grad_h2 * gain_two)
     tgrad_ref[...] = grad_resid
     grad_branch = grad_resid.astype(LOW)
-    db[c, y] = grad_branch
+    db[x, y] = grad_branch
     grad_o = dot(grad_branch, wo[...].reshape(768, 768)).astype(LOW)
-    own_block = zb * 8 + x * 4 + c * 2 + y
+    own_block = zb * 8 + c * 4 + x * 2 + y
     for slot_ in range(3):
         for y_ in range(2):
             lanes = y_ * 384 + slot_ * 128
@@ -771,40 +926,20 @@
 
                 @pl.when(mine)
                 def _(slot_=slot_, y_=y_):
-                    dop[zb, x, c, y] = dos[y_, slot_]
+                    dop[zb, c, x, y] = dos[y_, slot_]
 
                 push(
-                    dos.at[y_, slot_], dop.at[zb, x, c, y], s_do.at[slot_ * 4 + y_ * 2 + c_], r_do.at[own_block],
+                    dos.at[y_, slot_], dop.at[zb, c, x, y], s_do.at[slot_ * 4 + y_ * 2 + c_], r_do.at[own_block],
                     at(zh * 2 + slot_ // 2, slot_ % 2, c_, y_), jnp.logical_not(mine),
                 )
-    for k, (kc, ky) in enumerate(group):
-        push(db.at[c, y], db.at[c, y], s_db.at[k], r_db.at[k], at(z, x, flip(c, kc), flip(y, ky)))
-    mixed_ref[...] = (own_res + quarter_sum(1)).astype(LOW)
-    deliver(0, mixed_ref, mixed_out)
-    def sum_x(kz, mine, other, total, send, recv, landing):
-        z_ = far_z(kz)
-        arrive(other.at[z_], recv.at[0, kz])
-        total[z_] = (mine[z_, x].astype(FULL) + other[z_].astype(FULL)).astype(LOW)
-        if kz:
-            push(total.at[z_], landing.at[kz - 1], send.at[1, kz], recv.at[1, kz], at(z_, x, c, y))
-
-    def out_share():
-        for k, (kc, ky) in enumerate(group):
-            arrive(db.at[flip(c, kc), flip(y, ky)], r_db.at[k])
-        db_t = turned(db[...].reshape(256, 768)).astype(LOW)
-        o_part = og[...].reshape(2, 6, 64, 256)
-        o_pick = jnp.where(y == 0, o_part[0], o_part[1])
-        o_pick = jnp.where(c == 0, o_pick[0:3], o_pick[3:6]).reshape(192, 256)
-        go[...] = dot_nt(db_t, o_pick).astype(LOW).reshape(4, 2, 96, 192)
-        for kz in (3, 2, 1, 0):
-            z_ = far_z(kz)
-            push(go.at[z_, 1 - x], go_x.at[z_], s_go.at[0, kz], r_go.at[0, kz], partner("x"))
-
-    sum_x(3, gf, gf_x, gf_s, s_gf, r_gf, gf_z)
+    run_later(1)
+    for k, (kx, ky) in enumerate(group):
+        push(db.at[x, y], db.at[x, y], s_db.at[k], r_db.at[k], member(kx, ky))
+    run_later(2)
 
     for b in range(16):
-        z_, x_, c_, y_ = b // 8, (b // 4) % 2, (b // 2) % 2, b % 2
-        arrive(dop.at[z_, x_, c_, y_], r_do.at[b], jnp.logical_and(active, own_block != b))
+        z_, c_, x_, y_ = b // 8, (b // 4) % 2, (b // 2) % 2, b % 2
+        arrive(dop.at[z_, c_, x_, y_], r_do.at[b], jnp.logical_and(active, own_block != b))
 
     @pl.when(active)
     def _():
@@ -826,10 +961,7 @@
             b1, b2 = back[0:32], back[32:64]
             dqt[0:64, cols] = jnp.concatenate([b1 * cosine + b2 * sine, b2 * cosine - b1 * sine], axis=0).astype(LOW)
 
-        if part == 0:
-            out_share()
-        if part < 3:
-            sum_x(2 - part, gf, gf_x, gf_s, s_gf, r_gf, gf_z)
+        run_later(3 + part)
 
     @pl.when(active)
     def _():
@@ -843,38 +975,42 @@
             dq[cols, :] = turned(dqt[:, cols]).astype(LOW)
 
     for part in range(4):
-        cols = pl.ds(part * 256, 256)
+        z_, c_ = part % 2, flip(c, 1 - part // 2)
 
         @pl.when(active)
-        def _(part=part, cols=cols):
-            d1[part // 2, part % 2] = dot_nt(dq[cols, :], wh[...]).astype(LOW).reshape(2, 2, 64, 768)
-
-        push(
-            d1.at[part // 2, part % 2, 1 - c], d1_c.at[part // 2, part % 2],
-            s_d1.at[0, part], r_d1.at[0, part], partner("c"), active,
-        )
-    for part in (3, 2, 1, 0):
-        sum_x(part, go, go_x, go_s, s_go, r_go, go_z)
+        def _(z_=z_, c_=c_):
+            rows = pl.ds(pl.multiple_of(z_ * 512 + c_ * 256, 256), 256)
+            d1[z_, c_] = dot_nt(dq[rows, :], wh[...]).astype(LOW).reshape(2, 2, 64, 768)
+
+        if part < 2:
+            push(d1.at[z_, c_], d1_c.at[z_], s_d1.at[0, z_], r_d1.at[0, z_], partner("c"), active)
+    run_later(7)
+
+    @pl.when(active)
+    def _():
+        grad = dot(dqt[...], h1[...])
+        dw[...] = grad.T.astype(LOW).reshape(16, 48, 192)
 
     @pl.when(jnp.logical_not(active))
     def _():
         d1_a[...] = jnp.zeros_like(d1_a)
 
-    for part in range(4):
-        arrive(d1_c.at[part // 2, part % 2], r_d1.at[0, part], active)
+    for z_ in range(2):
+        arrive(d1_c.at[z_], r_d1.at[0, z_], active)
 
         @pl.when(active)
-        def _(part=part):
-            both = d1[part // 2, part % 2, c].astype(FULL) + d1_c[part // 2, part % 2].astype(FULL)
-            d1_a[part // 2, part % 2] = both.astype(LOW)
+        def _(z_=z_):
+            d1_a[z_] = (d1[z_, c].astype(FULL) + d1_c[z_].astype(FULL)).astype(LOW)
+
+    back_orders = (("x", "y", "z"), ("y", "z", "x"), ("z", "x", "y"))
 
     def remaining(t, step):
-        return tuple(d for d in ("z", "x", "y") if d not in orders[t][:step])
+        return tuple(d for d in ("z", "x", "y") if d not in back_orders[t][:step])
 
     landing = (d1_r1, d1_r2, d1_r3)
 
     def step_view(t, step, flipped):
-        dim = orders[t][step]
+        dim = back_orders[t][step]
         place = {"z": zb, "x": x, "y": y}[dim]
         place = 1 - place if flipped else place
         index = tuple(place if d == dim else slice(None) for d in remaining(t, step))
@@ -885,7 +1021,7 @@
     def step_push(t, step):
         push(
             step_view(t, step, True), landing[step].at[t], s_d1.at[1 + step, t], r_d1.at[1 + step, t],
-            partner(orders[t][step]),
+            partner(back_orders[t][step]),
         )
 
     def step_sum(t, step):
@@ -895,11 +1031,6 @@
     for t in range(3):
         step_push(t, 0)
 
-    @pl.when(active)
-    def _():
-        grad = dot(dqt[...], h1[...])
-        dw[...] = grad.T.astype(LOW).reshape(16, 48, 192)
-
     own_head = zh * 6 + slot3 * 2 + c
 
     @pl.when(active)
@@ -914,31 +1045,18 @@
         d1_s1[t] = step_sum(t, 0).astype(LOW)
         step_push(t, 1)
 
-    def sum_z(total, landed, wide, low, send, recv, coming):
-        value = total[z].astype(FULL)
-        for k in range(1, 4):
-            arrive(landed.at[k - 1], recv.at[1, k])
-            value = value + landed[k - 1].astype(FULL)
-        wide[...] = value.reshape(wide.shape)
-        low[...] = wide[1 - c].astype(LOW)
-        push(low, coming, send.at[2, 0], recv.at[2, 0], partner("c"))
-
-    sum_z(gf_s, gf_z, gf_f, gf_b, s_gf, r_gf, gf_c)
+    run_later(8)
     for t in range(3):
         d1_s2[t] = step_sum(t, 1).astype(LOW)
         step_push(t, 2)
-    sum_z(go_s, go_z, go_f, go_b, s_go, r_go, go_c)
-    arrive(gf_c, r_gf.at[2, 0])
-    def by_core(own, other):
-        return jnp.where(c == 0, own, other), jnp.where(c == 0, other, own)
-
+    run_later(9)
     mlp_terms = jnp.zeros((48, 1), FULL)
-    for c_, grads in enumerate(by_core(gf_f[c], gf_c[...].astype(FULL))):
-        lanes = slice(c_ * 288, c_ * 288 + 288)
+    for x_, grads in enumerate(ff_sums[4]()):
+        lanes = slice(x_ * 288, x_ * 288 + 288)
         for g in range(2):
             ing_ref[:, g, lanes] = grads[:, g * 288 : g * 288 + 288]
         downg_ref[:, lanes] = grads[:, 576:864]
-        terms = grads[:, 0:576] * ffp_ref[c_, :, 0:576].astype(FULL)
+        terms = grads[:, 0:576] * ffp_ref[x_, :, 0:576].astype(FULL)
         mlp_terms = mlp_terms + jnp.sum(terms, axis=1, keepdims=True)
     deliver(1, ing_ref, ing_out)
     deliver(2, downg_ref, downg_out)
@@ -955,9 +1073,8 @@
     lane = lax.broadcasted_iota(jnp.int32, (48, 128), 1)
     gy[...] = jnp.where(lane == 0, attn_terms, jnp.where(lane == 1, mlp_terms, 0.0))
     push(gy, gy_in, s_gy.at[0], r_gy.at[0], partner("y"))
-    arrive(go_c, r_go.at[2, 0])
-    for c_, grads in enumerate(by_core(go_f[c], go_c[...].astype(FULL))):
-        outg_ref[:, c_ * 192 : c_ * 192 + 192] = grads
+    for x_, grads in enumerate(out_sums[4]()):
+        outg_ref[:, x_ * 192 : x_ * 192 + 192] = grads
     deliver(4, outg_ref, outg_out)
 
     unit_one, scale_one = centred_norm(tok_ref[...].astype(FULL))
@@ -1018,22 +1135,22 @@
     scratch = [vm(*shape) for shape in finals] + [
         vm((8, 128), FULL), vm((heads_here, depth, 192)), vm((2, depth, ff)), vm((depth, feats)),
         vm((2, 2, 2, 2, 64, 768)), vm((2, 2, 2, 2, 2, 8, 128), FULL), vm((8, 768), FULL), vm((2, 2, 64, 768)),
-        vm((768, 192)), vm((192, 768)), vm((4, 2, 96, 864)), vm((4, 2, 2, 48, 768)), vm((1024, 768)),
+        vm((768, 192)), vm((192, 768)), vm((4, 2, 2, 48, 864)), vm((4, 2, 2, 48, 768)), vm((1024, 768)),
         vm((3, 32, 1024), FULL), vm((128, 1024)), vm((1024, 128)), vm((64, 1024)), vm((64, 1024)), vm((1024, 64)),
         vm((1024, 1024)), vm((4, 64, 256), FULL), vm((4, 64, 256)), vm((2, 3, 2, 64, 256)), vm((2, 2, 64, 768), FULL),
-        vm((2, 2, 2, 64, 768)), vm((2, 2, 64, 768)), vm((2, 64, 768)), vm((2, 64, 768)), vm((2, 2, 64, 768)),
+        vm((2, 2, 2, 64, 768)), vm((2, 2, 2, 64, 384)), vm((2, 2, 64, 384)), vm((2, 2, 64, 384)), vm((2, 2, 64, 768)),
         vm((2, 3, 64, 128)), vm((2, 2, 2, 2, 64, 128)), vm((64, 1024)), vm((1024, 1024)), vm((192, 1024)),
         vm((1024, 192)), vm((2, 2, 2, 2, 64, 768)), vm((2, 2, 2, 64, 768)), vm((2, 2, 2, 64, 768)),
         vm((3, 2, 2, 64, 256)), vm((3, 2, 2, 64, 256)), vm((3, 2, 64, 256)), vm((3, 2, 64, 256)), vm((3, 64, 256)),
         vm((16, 48, 192)), vm((12, 48, 192)),
-        vm((4, 2, 96, 864)), vm((4, 96, 864)), vm((4, 96, 864)), vm((3, 96, 864)), vm((2, 48, 864), FULL),
-        vm((48, 864)), vm((48, 864)),
-        vm((4, 2, 96, 192)), vm((4, 96, 192)), vm((4, 96, 192)), vm((3, 96, 192)), vm((2, 48, 192), FULL),
-        vm((48, 192)), vm((48, 192)),
+        vm((4, 2, 2, 48, 864)), vm((4, 2, 48, 864)), vm((4, 2, 48, 864)), vm((2, 2, 48, 864)), vm((2, 48, 864)),
+        vm((2, 48, 864), FULL), vm((48, 864)), vm((48, 864)),
+        vm((4, 2, 2, 48, 192)), vm((4, 2, 48, 192)), vm((4, 2, 48, 192)), vm((2, 2, 48, 192)), vm((2, 48, 192)),
+        vm((2, 48, 192), FULL), vm((48, 192)), vm((48, 192)),
         vm((48, 128), FULL), vm((48, 128), FULL),
         sem(4, 3), sem(4, 3), sem(5), sem(5), sem(16), sem(16), sem(3), sem(3), sem(12), sem(12), sem(7), sem(7),
-        sem(5, 2), sem(4, 2), sem(2, 2), sem(2, 2), sem(3), sem(3), sem(12), sem(16), sem(4, 4), sem(4, 4),
-        sem(16), sem(12), sem(3, 4), sem(3, 4), sem(3, 4), sem(3, 4), sem(1), sem(1), sem(7),
+        sem(4, 4), sem(3, 2, 2), sem(2, 2, 2), sem(2, 2, 2), sem(3), sem(3), sem(12), sem(16), sem(4, 4), sem(4, 4),
+        sem(16), sem(12), sem(4, 4), sem(4, 4), sem(4, 4), sem(4, 4), sem(1), sem(1), sem(7),
     ]
     vmem = pl.BlockSpec(memory_space=pltpu.VMEM)
     anywhere = pl.BlockSpec(memory_space=pl.ANY)

time: 113 us -> 96.3 us (0.85)
  Pallas kernels: 112 us -> 94.6 us
    pallas_call x1, Pallas kernels: 108 us -> 91.4 us  [on_device_fast(): pl.pallas_call(whole_layer, out_shape=shapes, in_specs=[pl.BlockSpec(memo...]
where the time goes in v4:
time: 96.3 us; the launch traced here: 95.4 us
  Pallas kernels  94.6 us (98%)
    pallas_call x1, Pallas kernels, on_device_fast(): pl.pallas_call(whole_layer, out_shape=shapes, in_specs=[pl.BlockSpec(memo...  91.4 us
    pallas_call x1, Pallas kernels, on_device_fast(): pl.pallas_call(hand_on, out_shape=[jax.ShapeDtypeStruct(a.shape, a.dtype)...  3.27 us

profile of v4, /device:TPU:0, one launch (start us, length us, event | category | flops | bytes accessed | tf_op | source)
XLA Modules:
  0.0 95.4 jit_solution(469539636550705173)
XLA Ops:
  0.6 91.4 %shard_map.152 = (bf16[64,768]{1,0:T(8,128)(2,1)}, f32[64,768]{1,0:T(8,128)}, f32[8,128]{1,0:T(8,128)}, f32[3,48,384]{2,1,0:T(8,128)}, f32[48,384]{1,0:T(8,128)}...) custom-call(s32[3]{0:T(128)} %refs_0_.1, bf16[64,768]{1,0:T(8,128)(2,1)} %refs_1_.1, bf16[64,768]{1,0:T(8,128)(2,1)} %refs_2_.1, ...), custom_call_target="tpu_custom_call" | custom-call | tf_op jit(solution)/shard_map/pallas_call | solution.py:1158
  92.0 3.3 %shard_map.153 = (bf16[64,768]{1,0:T(8,128)(2,1)}, f32[64,768]{1,0:T(8,128)}, f32[3,48,384]{2,1,0:T(8,128)}, f32[48,384]{1,0:T(8,128)}, f32[48,2,576]{2,1,0:T(2,...) custom-call(bf16[64,768]{1,0:T(8,128)(2,1)} %get-tuple-element.23.refs_0_, ...), custom_call_target="tpu_custom_call" | custom-call | tf_op jit(solution)/shard_map/pallas_call | solution.py:1171

commit v5 on v4

--- a/solution.py
+++ b/solution.py
@@ -406,14 +406,14 @@
 
 def whole_layer(*refs):
     (
-        short_ref, tok_ref, gout_ref, gain_a, gain_m, qkv_ref, out_ref, in_ref, down_ref,
+        short_ref, gain_a, gain_m, tok_in, gout_in, qkv_in, out_in, in_in, down_in,
         mixed_out, tgrad_out, gains_out, qkvg_out, outg_out, ing_out, downg_out,
         mixed_ref, tgrad_ref, gains_ref, qkvg_ref, outg_ref, ing_ref, downg_ref,
-        gain_ref, wq_ref, ffp_ref, wot_ref, xh, gt, gn, gb, wh, wht, ffw, wo, h1, cs, qa, ka, kt, vt, vr, pt, ot, ol, og, res,
-        ms, ms_c, ms_a, ms_y, db, dos, dop, dot_t, ds, dqt, dq, d1, d1_c, d1_a, d1_r1, d1_s1, d1_r2, d1_s2, d1_r3,
-        dw, dw_in, gf, gf_k, gf_s, gf_z, gf_y, gf_f, gf_b, gf_c, go, go_k, go_s, go_z, go_y, go_f, go_b, go_c, gy, gy_in,
+        tok_ref, gout_ref, qkv_ref, wot_ref, in_ref, down_ref, gain_ref, wq_ref, ffp_ref, xh, gt, gn, gb, wh_p, wh, wht, ffw, wo, h1, cs, qa, ka, kt, vt, vr, pt, ot, ol, og, res,
+        ms, ms_c, ms_a, ms_y, ms_d, db, dos, dop, dot_t, ds, dqt, dq, d1, d1_c, d1_a, d1_r1, d1_s1, d1_r2, d1_s2, d1_r3,
+        dw, dw_c, dw_p, dw_in, gf, gf_k, gf_s, gf_z, gf_y, gf_f, gf_b, gf_c, go, go_k, go_s, go_z, go_y, go_f, go_b, go_c, gy, gy_in,
         s_tok, r_tok, s_gain, r_gain, s_wq, r_wq, s_g, r_g, s_ff, r_ff, s_wo, r_wo,
-        s_o, r_o, s_ms, r_ms, s_db, r_db, s_do, r_do, s_d1, r_d1, s_dw, r_dw, s_gf, r_gf, s_go, r_go, s_gy, r_gy, s_out,
+        s_o, r_o, s_ms, r_ms, s_db, r_db, s_do, r_do, s_d1, r_d1, s_dw, r_dw, s_gf, r_gf, s_go, r_go, s_gy, r_gy, s_out, s_in,
     ) = refs
     seq, head = lax.axis_index("seq"), lax.axis_index("head")
     z, x, c, y = seq // 4, (seq // 2) % 2, seq % 2, head
@@ -467,6 +467,10 @@
         else:
             pl.when(when)(copy.wait_recv)
 
+    loads = (
+        (tok_in, tok_ref), (qkv_in, qkv_ref), (in_in, in_ref), (down_in, down_ref), (out_in, wot_ref), (gout_in, gout_ref),
+    )
+    loads = [pltpu.make_async_copy(a, b, s_in.at[k]) for k, (a, b) in enumerate(loads)]
     barrier = pltpu.get_barrier_semaphore()
     peers = []
     for k in range(1, 32):
@@ -476,13 +480,17 @@
     for peer in peers:
         pl.semaphore_signal(barrier, inc=1, device_id=peer, device_id_type=pl.DeviceIdType.MESH)
 
+    for load in loads:
+        load.start()
     gain_ref[...] = jnp.zeros_like(gain_ref)
     gain_ref[0:1, 0 : gain_a.shape[1]] = gain_a[...].astype(FULL)
     gain_ref[1:2, 0 : gain_m.shape[1]] = gain_m[...].astype(FULL)
-    wot_ref[...] = out_ref[...]
+    for load in loads:
+        load.wait()
     for g in range(3):
         for j in range(6):
-            wq_ref[j, :, g * 64 : g * 64 + 64] = qkv_ref[g, :, j * 64 : j * 64 + 64]
+            lanes = j % 2 * 192 + g * 64
+            wq_ref[j // 2, :, lanes : lanes + 64] = qkv_ref[g, :, j * 64 : j * 64 + 64]
     for c_ in range(2):
         lanes = slice(c_ * 288, c_ * 288 + 288)
         for g in range(2):
@@ -508,22 +516,28 @@
         push(view, view, s_tok.at[0, t], r_tok.at[0, t], partner(orders[t][0]))
 
     gt[zh, zb, x, c, y] = gain_ref[...]
-    gain_order = ("c", "h", "x", "y", "z")
-
-    def gain_view(opened, flipped=None):
-        there = {"h": zh, "z": zb, "x": x, "c": c, "y": y}
-        if flipped is not None:
-            there[flipped] = 1 - there[flipped]
-        return gt.at[tuple(slice(None) if d in opened else there[d] for d in ("h", "z", "x", "c", "y"))]
-
-    def gain_send(k):
-        view = gain_view(gain_order[:k])
-        push(view, view, s_gain.at[k], r_gain.at[k], partner(gain_order[k]))
-
-    def gain_wait(k):
-        arrive(gain_view(gain_order[:k], gain_order[k]), r_gain.at[k])
-
-    gain_send(0)
+
+    def gain_place(k):
+        return gt.at[flip(zh, k // 2), flip(zb, k % 2), x, c, y]
+
+    for k in range(1, 4):
+        push(gain_place(0), gain_place(0), s_gain.at[k], r_gain.at[k], at(far_z(k), x, c, y))
+
+    def plane(k):
+        return flip(x, k // 4), flip(c, k // 2 % 2), flip(y, k % 2)
+
+    def gain_share():
+        for k in range(1, 4):
+            arrive(gain_place(k), r_gain.at[k])
+        for k in range(1, 8):
+            x_, c_, y_ = plane(k)
+            view = gt.at[:, :, x, c, y]
+            push(view, view, s_gain.at[3 + k], r_gain.at[3 + k], at(z, x_, c_, y_))
+
+    def gain_all():
+        for k in range(1, 8):
+            x_, c_, y_ = plane(k)
+            arrive(gt.at[:, :, x_, c_, y_], r_gain.at[3 + k])
 
     wo_lanes = pl.ds(pl.multiple_of(y * 384, 128), 384)
     wo_others = pl.ds(pl.multiple_of((1 - y) * 384, 128), 384)
@@ -580,15 +594,15 @@
         for k in (2, 3, 1):
             push(wot_ref, wo.at[z, x, c, :, wo_lanes], s_wo.at[k], r_wo.at[k], at(far_z(k), x, c, y))
 
-    own_rows = pl.ds(pl.multiple_of(seq * 48, 16), 48)
-    wh[own_rows, :] = wq_ref[jnp.minimum(slot * 2 + c, 5)]
+    own_pair_at = z * 2 + x
+    wh_p[c, own_pair_at] = wq_ref[slot3]
 
     def head_push():
-        for k in range(1, 16):
-            z_, x_, c_ = far_z(k // 4), flip(x, (k // 2) % 2), flip(c, k % 2)
-            slot_ = (z_ % 2) * 2 + x_
-            piece = wq_ref.at[jnp.minimum(slot_ * 2 + c_, 5)]
-            push(piece, wh.at[own_rows, :], s_wq.at[k], r_wq.at[k], at(z_, x_, c_, y), slot_ < 3)
+        for k in (7, 5, 6, 4, 3, 2, 1):
+            z_, x_ = far_z(k // 2), flip(x, k % 2)
+            slot_ = z_ % 2 * 2 + x_
+            piece = wq_ref.at[jnp.minimum(slot_, 2)]
+            push(piece, wh_p.at[c, own_pair_at], s_wq.at[k], r_wq.at[k], at(z_, x_, c, y), slot_ < 3)
 
     gb[x, y] = gout_ref[...]
     group = ((0, 1), (1, 0), (1, 1))
@@ -605,8 +619,6 @@
             arrive(blocks(xh, orders[t][: step - 1], third(t), orders[t][step - 1]), r_tok.at[step - 1, t])
             view = blocks(xh, orders[t][:step], third(t))
             push(view, view, s_tok.at[step, t], r_tok.at[step, t], partner(orders[t][step]))
-        gain_wait(step)
-        gain_send(step + 1)
 
     events = {
         "fx": lambda: ff_share(ffp_ref.at[1 - x], z, x, 0, "x"),
@@ -642,14 +654,11 @@
         ("c3", "oc"),
     )
     run(0)
-    gain_wait(0)
-    gain_send(1)
     token_step(1)
+    gain_share()
     run(1)
     token_step(2)
     run(2)
-    gain_wait(3)
-    gain_send(4)
     run(3)
 
     half_rows = 1024
@@ -676,7 +685,7 @@
     qa[64:96, :] = ((same - 1.0) * 1e30).astype(LOW)
     qa[96:128, :] = jnp.zeros((32, half_rows), LOW)
 
-    gain_wait(4)
+    gain_all()
     tiles = gt[...].reshape(256, 128).astype(LOW)
     width = 24
     pick = lax.broadcasted_iota(jnp.int32, (128, 768), 1) % width == lax.broadcasted_iota(jnp.int32, (128, 768), 0)
@@ -692,6 +701,10 @@
     def rows_of(z_, c_):
         return pl.ds(pl.multiple_of(z_ * 512 + c_ * 256, 256), 256)
 
+    for k in range(1, 8):
+        arrive(wh_p.at[c, far_z(k // 2) * 2 + flip(x, k % 2)], r_wq.at[k], active)
+    push(wh_p.at[c], wh_p.at[c], s_wq.at[0], r_wq.at[0], partner("c"), active)
+
     for z_ in range(2):
         rows = rows_of(z_, c)
 
@@ -701,13 +714,13 @@
             h1[rows, :] = (unit * gn[0:1, :]).astype(LOW)
 
         push(h1.at[rows, :], h1.at[rows, :], s_tok.at[3, z_], r_tok.at[3, z_], partner("c"), active)
-    for k in range(1, 16):
-        source_seq = far_z(k // 4) * 4 + flip(x, (k // 2) % 2) * 2 + flip(c, k % 2)
-        arrive(wh.at[pl.ds(pl.multiple_of(source_seq * 48, 16), 48), :], r_wq.at[k], active)
+    arrive(wh_p.at[1 - c], r_wq.at[0], active)
 
     @pl.when(active)
     def _():
-        wht[...] = turned(wh[...]).astype(LOW)
+        for c_ in range(2):
+            wh[:, c_] = jnp.where(c == 0, wh_p[c_, :, :, 0:192], wh_p[c_, :, :, 192:384])
+        wht[...] = turned(wh[...].reshape(768, 192)).astype(LOW)
 
     for part in range(4):
         z_, c_ = part % 2, flip(c, part // 2)
@@ -814,7 +827,9 @@
             sums.append(mine + ms_y[kind, t].astype(FULL))
         return jnp.concatenate(sums, axis=1)
 
-    halve(0, dot_nt(grad_gate_up, w_in))
+    ms[0] = dot_nt(grad_gate_up, w_in).astype(LOW).reshape(2, 2, 64, 768)
+    for k, (kx, ky) in enumerate(group):
+        push(ms.at[0, flip(x, kx), flip(y, ky)], ms_d.at[k], s_g.at[3 + k], r_g.at[3 + k], member(kx, ky))
     h2_t = turned(h2).astype(LOW)
     gf[:, :, :, :, 0:576] = dot(h2_t, grad_gate_up).astype(LOW).reshape(4, 2, 2, 48, 576)
     g_t = turned(grad_out).astype(LOW)
@@ -889,15 +904,15 @@
     }
     then = (
         ("n3",),
-        ("mx", "n1"),
-        (),
-        ("O", "f"),
-        ("O3", "O1", "md"),
+        ("n1", "mx"),
         (),
         (),
-        ("Of",),
-        ("Oe", "e"),
+        ("f", "md"),
         (),
+        (),
+        ("O",),
+        ("e", "O3", "O1", "Of"),
+        ("Oe",),
     )
 
     def run_later(point):
@@ -905,12 +920,14 @@
             later[name]()
 
     ff_sums[0]()
-    quarter(0)
     halve(1, dot_nt(hidden, w_down))
     run_later(0)
     own_res = res[x, y]
     unit_two, scale_two = centred_norm(own_res)
-    grad_h2 = quarter_sum(0)
+    grad_h2 = ms[0, x, y].astype(FULL)
+    for k in range(3):
+        arrive(ms_d.at[k], r_g.at[3 + k])
+        grad_h2 = grad_h2 + ms_d[k].astype(FULL)
     grad_resid = gout_ref[...].astype(FULL) + norm_back(unit_two, scale_two, grad_h2 * gain_two)
     tgrad_ref[...] = grad_resid
     grad_branch = grad_resid.astype(LOW)
@@ -980,7 +997,7 @@
         @pl.when(active)
         def _(z_=z_, c_=c_):
             rows = pl.ds(pl.multiple_of(z_ * 512 + c_ * 256, 256), 256)
-            d1[z_, c_] = dot_nt(dq[rows, :], wh[...]).astype(LOW).reshape(2, 2, 64, 768)
+            d1[z_, c_] = dot_nt(dq[rows, :], wh[...].reshape(768, 192)).astype(LOW).reshape(2, 2, 64, 768)
 
         if part < 2:
             push(d1.at[z_, c_], d1_c.at[z_], s_d1.at[0, z_], r_d1.at[0, z_], partner("c"), active)
@@ -989,7 +1006,10 @@
     @pl.when(active)
     def _():
         grad = dot(dqt[...], h1[...])
-        dw[...] = grad.T.astype(LOW).reshape(16, 48, 192)
+        grad = grad.T.astype(LOW).reshape(8, 2, 48, 192)
+        dw[0], dw[1] = grad[:, 0], grad[:, 1]
+
+    push(dw.at[1 - c], dw_c, s_dw.at[0], r_dw.at[6], partner("c"), active)
 
     @pl.when(jnp.logical_not(active))
     def _():
@@ -1031,19 +1051,26 @@
     for t in range(3):
         step_push(t, 0)
 
-    own_head = zh * 6 + slot3 * 2 + c
+    own_pair = zh * 3 + slot3
+    arrive(dw_c, r_dw.at[6], active)
 
     @pl.when(active)
     def _():
-        dw_in[own_head] = dw[seq]
-
-    for k in range(1, 16):
-        z_, x_, c_ = far_z(k // 4), flip(x, (k // 2) % 2), flip(c, k % 2)
-        push(dw.at[z_ * 4 + x_ * 2 + c_], dw_in.at[own_head], s_dw.at[k], r_dw.at[own_head], at(z_, x_, c_, y), active)
-
+        own, other = dw[c], dw_c[...]
+        dw_p[:, :, 0:192] = jnp.where(c == 0, own, other)
+        dw_p[:, :, 192:384] = jnp.where(c == 0, other, own)
+        dw_in[own_pair] = dw_p[z * 2 + x]
+
+    def pair_push(ks):
+        for k in ks:
+            z_, x_ = far_z(k // 2), flip(x, k % 2)
+            push(dw_p.at[z_ * 2 + x_], dw_in.at[own_pair], s_dw.at[k], r_dw.at[own_pair], at(z_, x_, c, y), active)
+
+    pair_push((7, 5, 6, 4))
     for t in range(3):
         d1_s1[t] = step_sum(t, 0).astype(LOW)
         step_push(t, 1)
+    pair_push((3, 2, 1))
 
     run_later(8)
     for t in range(3):
@@ -1061,14 +1088,17 @@
     deliver(1, ing_ref, ing_out)
     deliver(2, downg_ref, downg_out)
     for h_ in range(2):
-        for j in range(6):
-            arrive(dw_in.at[h_ * 6 + j], r_dw.at[h_ * 6 + j], jnp.logical_not(jnp.logical_and(active, own_head == h_ * 6 + j)))
+        for slot_ in range(3):
+            mine = jnp.logical_and(zh == h_, slot == slot_)
+            arrive(dw_in.at[h_ * 3 + slot_], r_dw.at[h_ * 3 + slot_], jnp.logical_not(mine))
     attn_terms = jnp.zeros((48, 1), FULL)
-    for j in range(6):
-        both = dw_in[j].astype(FULL) + dw_in[6 + j].astype(FULL)
-        for g in range(3):
-            qkvg_ref[g, :, j * 64 : j * 64 + 64] = both[:, g * 64 : g * 64 + 64]
-        attn_terms = attn_terms + jnp.sum(both * wq_ref[j].astype(FULL), axis=1, keepdims=True)
+    for slot_ in range(3):
+        both = dw_in[slot_].astype(FULL) + dw_in[3 + slot_].astype(FULL)
+        for c_ in range(2):
+            for g in range(3):
+                lanes, j = c_ * 192 + g * 64, slot_ * 2 + c_
+                qkvg_ref[g, :, j * 64 : j * 64 + 64] = both[:, lanes : lanes + 64]
+        attn_terms = attn_terms + jnp.sum(both * wq_ref[slot_].astype(FULL), axis=1, keepdims=True)
     deliver(3, qkvg_ref, qkvg_out)
     lane = lax.broadcasted_iota(jnp.int32, (48, 128), 1)
     gy[...] = jnp.where(lane == 0, attn_terms, jnp.where(lane == 1, mlp_terms, 0.0))
@@ -1133,24 +1163,25 @@
         ((depth, feats), FULL), ((depth, 2, 576), FULL), ((depth, 576), FULL),
     ]
     scratch = [vm(*shape) for shape in finals] + [
-        vm((8, 128), FULL), vm((heads_here, depth, 192)), vm((2, depth, ff)), vm((depth, feats)),
+        vm((rows, width)), vm((rows, width)), vm((3, depth, 384)), vm((depth, feats)), vm((depth, 2, 576)), vm((depth, 576)),
+        vm((8, 128), FULL), vm((heads_here // 2, depth, 384)), vm((2, depth, ff)),
         vm((2, 2, 2, 2, 64, 768)), vm((2, 2, 2, 2, 2, 8, 128), FULL), vm((8, 768), FULL), vm((2, 2, 64, 768)),
-        vm((768, 192)), vm((192, 768)), vm((4, 2, 2, 48, 864)), vm((4, 2, 2, 48, 768)), vm((1024, 768)),
+        vm((2, 8, 48, 384)), vm((8, 2, 48, 192)), vm((192, 768)), vm((4, 2, 2, 48, 864)), vm((4, 2, 2, 48, 768)), vm((1024, 768)),
         vm((3, 32, 1024), FULL), vm((128, 1024)), vm((1024, 128)), vm((64, 1024)), vm((64, 1024)), vm((1024, 64)),
         vm((1024, 1024)), vm((4, 64, 256), FULL), vm((4, 64, 256)), vm((2, 3, 2, 64, 256)), vm((2, 2, 64, 768), FULL),
-        vm((2, 2, 2, 64, 768)), vm((2, 2, 2, 64, 384)), vm((2, 2, 64, 384)), vm((2, 2, 64, 384)), vm((2, 2, 64, 768)),
+        vm((2, 2, 2, 64, 768)), vm((2, 2, 2, 64, 384)), vm((2, 2, 64, 384)), vm((2, 2, 64, 384)), vm((3, 64, 768)), vm((2, 2, 64, 768)),
         vm((2, 3, 64, 128)), vm((2, 2, 2, 2, 64, 128)), vm((64, 1024)), vm((1024, 1024)), vm((192, 1024)),
         vm((1024, 192)), vm((2, 2, 2, 2, 64, 768)), vm((2, 2, 2, 64, 768)), vm((2, 2, 2, 64, 768)),
         vm((3, 2, 2, 64, 256)), vm((3, 2, 2, 64, 256)), vm((3, 2, 64, 256)), vm((3, 2, 64, 256)), vm((3, 64, 256)),
-        vm((16, 48, 192)), vm((12, 48, 192)),
+        vm((2, 8, 48, 192)), vm((8, 48, 192)), vm((8, 48, 384)), vm((6, 48, 384)),
         vm((4, 2, 2, 48, 864)), vm((4, 2, 48, 864)), vm((4, 2, 48, 864)), vm((2, 2, 48, 864)), vm((2, 48, 864)),
         vm((2, 48, 864), FULL), vm((48, 864)), vm((48, 864)),
         vm((4, 2, 2, 48, 192)), vm((4, 2, 48, 192)), vm((4, 2, 48, 192)), vm((2, 2, 48, 192)), vm((2, 48, 192)),
         vm((2, 48, 192), FULL), vm((48, 192)), vm((48, 192)),
         vm((48, 128), FULL), vm((48, 128), FULL),
-        sem(4, 3), sem(4, 3), sem(5), sem(5), sem(16), sem(16), sem(3), sem(3), sem(12), sem(12), sem(7), sem(7),
+        sem(4, 3), sem(4, 3), sem(11), sem(11), sem(8), sem(8), sem(6), sem(6), sem(12), sem(12), sem(7), sem(7),
         sem(4, 4), sem(3, 2, 2), sem(2, 2, 2), sem(2, 2, 2), sem(3), sem(3), sem(12), sem(16), sem(4, 4), sem(4, 4),
-        sem(16), sem(12), sem(4, 4), sem(4, 4), sem(4, 4), sem(4, 4), sem(1), sem(1), sem(7),
+        sem(8), sem(7), sem(4, 4), sem(4, 4), sem(4, 4), sem(4, 4), sem(1), sem(1), sem(7), sem(6),
     ]
     vmem = pl.BlockSpec(memory_space=pltpu.VMEM)
     anywhere = pl.BlockSpec(memory_space=pl.ANY)
@@ -1158,12 +1189,12 @@
     mixed, tokens_grad, gains, qkv_grad, out_grads, in_grad, down_grad = pl.pallas_call(
         whole_layer,
         out_shape=shapes,
-        in_specs=[pl.BlockSpec(memory_space=pltpu.SMEM)] + [vmem] * 8,
+        in_specs=[pl.BlockSpec(memory_space=pltpu.SMEM)] + [vmem] * 2 + [anywhere] * 6,
         out_specs=[anywhere] * 7,
         scratch_shapes=scratch,
         compiler_params=pltpu.CompilerParams(collective_id=0, has_side_effects=True, vmem_limit_bytes=60 << 20),
     )(
-        short_lengths, tokens, out_grad, attn_gain[None], mlp_gain[None],
+        short_lengths, attn_gain[None], mlp_gain[None], tokens, out_grad,
         qkv_weight.transpose(1, 0, 2), out_weight.T, in_weight, down_weight.T,
     )
     grads = (mixed, tokens_grad, qkv_grad, out_grads, in_grad, down_grad)

time: 96.3 us -> 89.5 us (0.929)
  Pallas kernels: 94.6 us -> 88.5 us
    pallas_call x1, Pallas kernels: 91.4 us -> 85.2 us  [on_device_fast(): pl.pallas_call(whole_layer, out_shape=shapes, in_specs=[pl.BlockSpec(memo...]
where the time goes in v5:
time: 89.5 us; the launch traced here: 89.3 us
  Pallas kernels  88.5 us (99%)
    pallas_call x1, Pallas kernels, on_device_fast(): pl.pallas_call(whole_layer, out_shape=shapes, in_specs=[pl.BlockSpec(memo...  85.2 us
    pallas_call x1, Pallas kernels, on_device_fast(): pl.pallas_call(hand_on, out_shape=[jax.ShapeDtypeStruct(a.shape, a.dtype)...  3.27 us

profile of v5, /device:TPU:0, one launch (start us, length us, event | category | flops | bytes accessed | tf_op | source)
XLA Modules:
  0.0 89.3 jit_solution(11179137653044466613)
XLA Ops:
  0.6 85.2 %shard_map.152 = (bf16[64,768]{1,0:T(8,128)(2,1)}, f32[64,768]{1,0:T(8,128)}, f32[8,128]{1,0:T(8,128)}, f32[3,48,384]{2,1,0:T(8,128)}, f32[48,384]{1,0:T(8,128)}...) custom-call(s32[3]{0:T(128)} %refs_0_.1, bf16[1,24]{1,0:T(2,128)(2,1)} %bitcast.13, bf16[1,24]{1,0:T(2,128)(2,1)} %bitcast.14, ...), custom_call_target="tpu_custom_call" | custom-call | tf_op jit(solution)/shard_map/pallas_call | solution.py:1189
  85.8 3.3 %shard_map.153 = (bf16[64,768]{1,0:T(8,128)(2,1)}, f32[64,768]{1,0:T(8,128)}, f32[3,48,384]{2,1,0:T(8,128)}, f32[48,384]{1,0:T(8,128)}, f32[48,2,576]{2,1,0:T(2,...) custom-call(bf16[64,768]{1,0:T(8,128)(2,1)} %get-tuple-element.23.refs_0_, ...), custom_call_target="tpu_custom_call" | custom-call | tf_op jit(solution)/shard_map/pallas_call | solution.py:1202

commit v6 on v5

--- a/solution.py
+++ b/solution.py
@@ -411,7 +411,7 @@
         mixed_ref, tgrad_ref, gains_ref, qkvg_ref, outg_ref, ing_ref, downg_ref,
         tok_ref, gout_ref, qkv_ref, wot_ref, in_ref, down_ref, gain_ref, wq_ref, ffp_ref, xh, gt, gn, gb, wh_p, wh, wht, ffw, wo, h1, cs, qa, ka, kt, vt, vr, pt, ot, ol, og, res,
         ms, ms_c, ms_a, ms_y, ms_d, db, dos, dop, dot_t, ds, dqt, dq, d1, d1_c, d1_a, d1_r1, d1_s1, d1_r2, d1_s2, d1_r3,
-        dw, dw_c, dw_p, dw_in, gf, gf_k, gf_s, gf_z, gf_y, gf_f, gf_b, gf_c, go, go_k, go_s, go_z, go_y, go_f, go_b, go_c, gy, gy_in,
+        dw, dw_c, dw_p, dw_in, gf, gf_k, gf_s, gf_z, gf_y, gf_f, gf_b, gf_c, go, go_k, go_s, go_z, gy, gy_in,
         s_tok, r_tok, s_gain, r_gain, s_wq, r_wq, s_g, r_g, s_ff, r_ff, s_wo, r_wo,
         s_o, r_o, s_ms, r_ms, s_db, r_db, s_do, r_do, s_d1, r_d1, s_dw, r_dw, s_gf, r_gf, s_go, r_go, s_gy, r_gy, s_out, s_in,
     ) = refs
@@ -644,14 +644,14 @@
 
     plan = (
         ("w",),
-        ("f2", "fx", "f1", "oz"),
-        ("fc", "ox", "g"),
-        ("fr", "c0", "c1", "oy"),
+        ("oz", "fx", "f2", "f1"),
+        ("ox", "fc", "g"),
+        ("oy", "fr", "c0", "c1"),
         ("c2",),
         (),
         (),
         (),
-        ("c3", "oc"),
+        ("oc", "c3"),
     )
     run(0)
     token_step(1)
@@ -873,7 +873,6 @@
         return cross, to_near, to_far, finish, result
 
     ff_sums = sums_of(gf, gf_k, gf_s, gf_z, gf_y, gf_f, gf_b, gf_c, s_gf, r_gf)
-    out_sums = sums_of(go, go_k, go_s, go_z, go_y, go_f, go_b, go_c, s_go, r_go)
 
     def out_share():
         for k, (kx, ky) in enumerate(group):
@@ -883,7 +882,21 @@
         o_pick = jnp.where(y == 0, o_part[0], o_part[1])
         o_pick = jnp.where(x == 0, o_pick[0:3], o_pick[3:6]).reshape(192, 256)
         go[...] = dot_nt(db_t, o_pick).astype(LOW).reshape(4, 2, 2, 48, 192)
-        out_sums[0]()
+        push(go.at[:, :, 1 - c], go_k, s_go.at[0], r_go.at[0], partner("c"))
+
+    def out_send():
+        arrive(go_k, r_go.at[0])
+        go_s[...] = (go[:, :, c].astype(FULL) + go_k[...].astype(FULL)).astype(LOW)
+        for k in (7, 5, 6, 4, 3, 2, 1):
+            z_, x_ = far_z(k // 2), flip(x, k % 2)
+            push(go_s.at[z_, x_], go_z.at[k - 1], s_go.at[k], r_go.at[k], at(z_, x_, c, y))
+
+    def out_result():
+        sums = [go_s[z, x].astype(FULL), jnp.zeros((48, 192), FULL)]
+        for k in range(1, 8):
+            arrive(go_z.at[k - 1], r_go.at[k])
+            sums[k % 2] = sums[k % 2] + go_z[k - 1].astype(FULL)
+        return jnp.where(x == 0, sums[0], sums[1]), jnp.where(x == 0, sums[1], sums[0])
 
     def mixed_done():
         mixed_ref[...] = (res[x, y] + quarter_sum(1)).astype(LOW)
@@ -897,10 +910,7 @@
         "f": ff_sums[2],
         "e": ff_sums[3],
         "O": out_share,
-        "O3": lambda: out_sums[1](3),
-        "O1": lambda: out_sums[1](1),
-        "Of": out_sums[2],
-        "Oe": out_sums[3],
+        "S": out_send,
     }
     then = (
         ("n3",),
@@ -911,8 +921,9 @@
         (),
         (),
         ("O",),
-        ("e", "O3", "O1", "Of"),
-        ("Oe",),
+        ("e", "S"),
+        (),
+        (),
     )
 
     def run_later(point):
@@ -1024,32 +1035,23 @@
 
     back_orders = (("x", "y", "z"), ("y", "z", "x"), ("z", "x", "y"))
 
-    def remaining(t, step):
-        return tuple(d for d in ("z", "x", "y") if d not in back_orders[t][:step])
-
-    landing = (d1_r1, d1_r2, d1_r3)
-
-    def step_view(t, step, flipped):
-        dim = back_orders[t][step]
-        place = {"z": zb, "x": x, "y": y}[dim]
-        place = 1 - place if flipped else place
-        index = tuple(place if d == dim else slice(None) for d in remaining(t, step))
-        if step == 0:
-            return d1_a.at[index + (slice(None), third(t))]
-        return (d1_s1, d1_s2)[step - 1].at[(t,) + index]
-
-    def step_push(t, step):
-        push(
-            step_view(t, step, True), landing[step].at[t], s_d1.at[1 + step, t], r_d1.at[1 + step, t],
-            partner(back_orders[t][step]),
-        )
-
-    def step_sum(t, step):
-        arrive(landing[step].at[t], r_d1.at[1 + step, t])
-        return step_view(t, step, False)[...].astype(FULL) + landing[step][t].astype(FULL)
-
-    for t in range(3):
-        step_push(t, 0)
+    spots = {"z": zb, "x": x, "y": y}
+
+    def halves(t, first, second):
+        a, b, _ = back_orders[t]
+        place = {a: flip(spots[a], first), b: flip(spots[b], second)}
+        return d1_a.at[tuple(place.get(d, slice(None)) for d in ("z", "x", "y")) + (slice(None), third(t))]
+
+    for h in (0, 1):
+        for t in range(3):
+            push(
+                halves(t, 1, 1 - h), d1_r1.at[t, h], s_d1.at[1, t * 2 + h], r_d1.at[1, t * 2 + h],
+                partner(back_orders[t][0]),
+            )
+
+    def first_sum(t, h):
+        arrive(d1_r1.at[t, h], r_d1.at[1, t * 2 + h])
+        d1_s1[t, h] = (halves(t, 0, 1 - h)[...].astype(FULL) + d1_r1[t, h].astype(FULL)).astype(LOW)
 
     own_pair = zh * 3 + slot3
     arrive(dw_c, r_dw.at[6], active)
@@ -1066,16 +1068,25 @@
             z_, x_ = far_z(k // 2), flip(x, k % 2)
             push(dw_p.at[z_ * 2 + x_], dw_in.at[own_pair], s_dw.at[k], r_dw.at[own_pair], at(z_, x_, c, y), active)
 
+    run_later(10)
     pair_push((7, 5, 6, 4))
     for t in range(3):
-        d1_s1[t] = step_sum(t, 0).astype(LOW)
-        step_push(t, 1)
+        first_sum(t, 0)
+        last = spots[back_orders[t][2]]
+        for h in (0, 1):
+            push(
+                d1_s1.at[t, 0, flip(last, 1 - h)], d1_r2.at[t, h], s_d1.at[2, t * 2 + h], r_d1.at[2, t * 2 + h],
+                partner(back_orders[t][1]),
+            )
     pair_push((3, 2, 1))
-
+    for t in range(3):
+        first_sum(t, 1)
     run_later(8)
     for t in range(3):
-        d1_s2[t] = step_sum(t, 1).astype(LOW)
-        step_push(t, 2)
+        last = spots[back_orders[t][2]]
+        arrive(d1_r2.at[t, 0], r_d1.at[2, t * 2])
+        d1_s2[t] = (d1_s1[t, 1, 1 - last].astype(FULL) + d1_r2[t, 0].astype(FULL)).astype(LOW)
+        push(d1_s2.at[t], d1_r3.at[t], s_d1.at[3, t], r_d1.at[3, t], partner(back_orders[t][2]))
     run_later(9)
     mlp_terms = jnp.zeros((48, 1), FULL)
     for x_, grads in enumerate(ff_sums[4]()):
@@ -1103,13 +1114,16 @@
     lane = lax.broadcasted_iota(jnp.int32, (48, 128), 1)
     gy[...] = jnp.where(lane == 0, attn_terms, jnp.where(lane == 1, mlp_terms, 0.0))
     push(gy, gy_in, s_gy.at[0], r_gy.at[0], partner("y"))
-    for x_, grads in enumerate(out_sums[4]()):
+    for x_, grads in enumerate(out_result()):
         outg_ref[:, x_ * 192 : x_ * 192 + 192] = grads
     deliver(4, outg_ref, outg_out)
 
     unit_one, scale_one = centred_norm(tok_ref[...].astype(FULL))
     for t in range(3):
-        res[0, 0, :, third(t)] = step_sum(t, 2)
+        arrive(d1_r2.at[t, 1], r_d1.at[2, t * 2 + 1])
+        arrive(d1_r3.at[t], r_d1.at[3, t])
+        total = d1_s1[t, 1, spots[back_orders[t][2]]].astype(FULL) + d1_r2[t, 1].astype(FULL)
+        res[0, 0, :, third(t)] = total + d1_r3[t].astype(FULL)
     tgrad_ref[...] = tgrad_ref[...] + norm_back(unit_one, scale_one, res[0, 0] * gn[0:1, :])
     deliver(5, tgrad_ref, tgrad_out)
     arrive(gy_in, r_gy.at[0])
@@ -1172,16 +1186,15 @@
         vm((2, 2, 2, 64, 768)), vm((2, 2, 2, 64, 384)), vm((2, 2, 64, 384)), vm((2, 2, 64, 384)), vm((3, 64, 768)), vm((2, 2, 64, 768)),
         vm((2, 3, 64, 128)), vm((2, 2, 2, 2, 64, 128)), vm((64, 1024)), vm((1024, 1024)), vm((192, 1024)),
         vm((1024, 192)), vm((2, 2, 2, 2, 64, 768)), vm((2, 2, 2, 64, 768)), vm((2, 2, 2, 64, 768)),
-        vm((3, 2, 2, 64, 256)), vm((3, 2, 2, 64, 256)), vm((3, 2, 64, 256)), vm((3, 2, 64, 256)), vm((3, 64, 256)),
+        vm((3, 2, 2, 64, 256)), vm((3, 2, 2, 64, 256)), vm((3, 2, 64, 256)), vm((3, 64, 256)), vm((3, 64, 256)),
         vm((2, 8, 48, 192)), vm((8, 48, 192)), vm((8, 48, 384)), vm((6, 48, 384)),
         vm((4, 2, 2, 48, 864)), vm((4, 2, 48, 864)), vm((4, 2, 48, 864)), vm((2, 2, 48, 864)), vm((2, 48, 864)),
         vm((2, 48, 864), FULL), vm((48, 864)), vm((48, 864)),
-        vm((4, 2, 2, 48, 192)), vm((4, 2, 48, 192)), vm((4, 2, 48, 192)), vm((2, 2, 48, 192)), vm((2, 48, 192)),
-        vm((2, 48, 192), FULL), vm((48, 192)), vm((48, 192)),
+        vm((4, 2, 2, 48, 192)), vm((4, 2, 48, 192)), vm((4, 2, 48, 192)), vm((7, 48, 192)),
         vm((48, 128), FULL), vm((48, 128), FULL),
         sem(4, 3), sem(4, 3), sem(11), sem(11), sem(8), sem(8), sem(6), sem(6), sem(12), sem(12), sem(7), sem(7),
-        sem(4, 4), sem(3, 2, 2), sem(2, 2, 2), sem(2, 2, 2), sem(3), sem(3), sem(12), sem(16), sem(4, 4), sem(4, 4),
-        sem(8), sem(7), sem(4, 4), sem(4, 4), sem(4, 4), sem(4, 4), sem(1), sem(1), sem(7), sem(6),
+        sem(4, 4), sem(3, 2, 2), sem(2, 2, 2), sem(2, 2, 2), sem(3), sem(3), sem(12), sem(16), sem(4, 6), sem(4, 6),
+        sem(8), sem(7), sem(4, 4), sem(4, 4), sem(8), sem(8), sem(1), sem(1), sem(7), sem(6),
     ]
     vmem = pl.BlockSpec(memory_space=pltpu.VMEM)
     anywhere = pl.BlockSpec(memory_space=pl.ANY)

time: 89.5 us -> 86.5 us (0.966)
  Pallas kernels: 88.5 us -> 85.5 us
    pallas_call x1, Pallas kernels: 85.2 us -> 82.2 us  [on_device_fast(): pl.pallas_call(whole_layer, out_shape=shapes, in_specs=[pl.BlockSpec(memo...]
where the time goes in v6:
time: 86.5 us; the launch traced here: 86.3 us
  Pallas kernels  85.5 us (99%)
    pallas_call x1, Pallas kernels, on_device_fast(): pl.pallas_call(whole_layer, out_shape=shapes, in_specs=[pl.BlockSpec(memo...  82.2 us
    pallas_call x1, Pallas kernels, on_device_fast(): pl.pallas_call(hand_on, out_shape=[jax.ShapeDtypeStruct(a.shape, a.dtype)...  3.27 us

profile of v6, /device:TPU:0, one launch (start us, length us, event | category | flops | bytes accessed | tf_op | source)
XLA Modules:
  0.0 86.3 jit_solution(7816772337962778582)
XLA Ops:
  0.6 82.2 %shard_map.152 = (bf16[64,768]{1,0:T(8,128)(2,1)}, f32[64,768]{1,0:T(8,128)}, f32[8,128]{1,0:T(8,128)}, f32[3,48,384]{2,1,0:T(8,128)}, f32[48,384]{1,0:T(8,128)}...) custom-call(s32[3]{0:T(128)} %refs_0_.1, bf16[1,24]{1,0:T(2,128)(2,1)} %bitcast.13, bf16[1,24]{1,0:T(2,128)(2,1)} %bitcast.14, ...), custom_call_target="tpu_custom_call" | custom-call | tf_op jit(solution)/shard_map/pallas_call | solution.py:1202
  82.8 3.3 %shard_map.153 = (bf16[64,768]{1,0:T(8,128)(2,1)}, f32[64,768]{1,0:T(8,128)}, f32[3,48,384]{2,1,0:T(8,128)}, f32[48,384]{1,0:T(8,128)}, f32[48,2,576]{2,1,0:T(2,...) custom-call(bf16[64,768]{1,0:T(8,128)(2,1)} %get-tuple-element.23.refs_0_, ...), custom_call_target="tpu_custom_call" | custom-call | tf_op jit(solution)/shard_map/pallas_call | solution.py:1215

commit v7 on v6

--- a/solution.py
+++ b/solution.py
@@ -949,17 +949,20 @@
         for y_ in range(2):
             lanes = y_ * 384 + slot_ * 128
             dos[y_, slot_] = grad_o[:, lanes : lanes + 128]
-            for c_ in range(2):
-                mine = jnp.logical_and(jnp.logical_and(slot == slot_, y == y_), c == c_)
-
-                @pl.when(mine)
-                def _(slot_=slot_, y_=y_):
-                    dop[zb, c, x, y] = dos[y_, slot_]
-
-                push(
-                    dos.at[y_, slot_], dop.at[zb, c, x, y], s_do.at[slot_ * 4 + y_ * 2 + c_], r_do.at[own_block],
-                    at(zh * 2 + slot_ // 2, slot_ % 2, c_, y_), jnp.logical_not(mine),
-                )
+    for turn in (1, 2, 0):
+        slot_ = (slot3 + turn) % 3
+        for k in (3, 2, 1, 0):
+            y_, c_ = flip(y, k // 2), flip(c, k % 2)
+            mine = jnp.logical_and(slot == slot_, k == 0)
+
+            @pl.when(mine)
+            def _(slot_=slot_, y_=y_):
+                dop[zb, c, x, y] = dos[y_, slot_]
+
+            push(
+                dos.at[y_, slot_], dop.at[zb, c, x, y], s_do.at[turn * 4 + k], r_do.at[own_block],
+                at(zh * 2 + slot_ // 2, slot_ % 2, c_, y_), jnp.logical_not(mine),
+            )
     run_later(1)
     for k, (kx, ky) in enumerate(group):
         push(db.at[x, y], db.at[x, y], s_db.at[k], r_db.at[k], member(kx, ky))
@@ -1088,6 +1091,10 @@
         d1_s2[t] = (d1_s1[t, 1, 1 - last].astype(FULL) + d1_r2[t, 0].astype(FULL)).astype(LOW)
         push(d1_s2.at[t], d1_r3.at[t], s_d1.at[3, t], r_d1.at[3, t], partner(back_orders[t][2]))
     run_later(9)
+    def share_terms(which, terms):
+        gy[which] = jnp.broadcast_to(terms, (48, 128))
+        push(gy.at[which], gy_in.at[which], s_gy.at[which], r_gy.at[which], partner("y"))
+
     mlp_terms = jnp.zeros((48, 1), FULL)
     for x_, grads in enumerate(ff_sums[4]()):
         lanes = slice(x_ * 288, x_ * 288 + 288)
@@ -1098,6 +1105,7 @@
         mlp_terms = mlp_terms + jnp.sum(terms, axis=1, keepdims=True)
     deliver(1, ing_ref, ing_out)
     deliver(2, downg_ref, downg_out)
+    share_terms(1, mlp_terms)
     for h_ in range(2):
         for slot_ in range(3):
             mine = jnp.logical_and(zh == h_, slot == slot_)
@@ -1111,9 +1119,7 @@
                 qkvg_ref[g, :, j * 64 : j * 64 + 64] = both[:, lanes : lanes + 64]
         attn_terms = attn_terms + jnp.sum(both * wq_ref[slot_].astype(FULL), axis=1, keepdims=True)
     deliver(3, qkvg_ref, qkvg_out)
-    lane = lax.broadcasted_iota(jnp.int32, (48, 128), 1)
-    gy[...] = jnp.where(lane == 0, attn_terms, jnp.where(lane == 1, mlp_terms, 0.0))
-    push(gy, gy_in, s_gy.at[0], r_gy.at[0], partner("y"))
+    share_terms(0, attn_terms)
     for x_, grads in enumerate(out_result()):
         outg_ref[:, x_ * 192 : x_ * 192 + 192] = grads
     deliver(4, outg_ref, outg_out)
@@ -1126,8 +1132,11 @@
         res[0, 0, :, third(t)] = total + d1_r3[t].astype(FULL)
     tgrad_ref[...] = tgrad_ref[...] + norm_back(unit_one, scale_one, res[0, 0] * gn[0:1, :])
     deliver(5, tgrad_ref, tgrad_out)
-    arrive(gy_in, r_gy.at[0])
-    sums = (gy[...] + gy_in[...]).T
+    for which in range(2):
+        arrive(gy_in.at[which], r_gy.at[which])
+    lane = lax.broadcasted_iota(jnp.int32, (48, 128), 1)
+    sums = gy[...] + gy_in[...]
+    sums = jnp.where(lane == 0, sums[0], sums[1]).T
     count = gain_a.shape[1]
     sums = jnp.where(y == 0, sums[0:2, :count], sums[0:2, count : 2 * count])
     gains_ref[...] = jnp.zeros_like(gains_ref)
@@ -1191,10 +1200,10 @@
         vm((4, 2, 2, 48, 864)), vm((4, 2, 48, 864)), vm((4, 2, 48, 864)), vm((2, 2, 48, 864)), vm((2, 48, 864)),
         vm((2, 48, 864), FULL), vm((48, 864)), vm((48, 864)),
         vm((4, 2, 2, 48, 192)), vm((4, 2, 48, 192)), vm((4, 2, 48, 192)), vm((7, 48, 192)),
-        vm((48, 128), FULL), vm((48, 128), FULL),
+        vm((2, 48, 128), FULL), vm((2, 48, 128), FULL),
         sem(4, 3), sem(4, 3), sem(11), sem(11), sem(8), sem(8), sem(6), sem(6), sem(12), sem(12), sem(7), sem(7),
         sem(4, 4), sem(3, 2, 2), sem(2, 2, 2), sem(2, 2, 2), sem(3), sem(3), sem(12), sem(16), sem(4, 6), sem(4, 6),
-        sem(8), sem(7), sem(4, 4), sem(4, 4), sem(8), sem(8), sem(1), sem(1), sem(7), sem(6),
+        sem(8), sem(7), sem(4, 4), sem(4, 4), sem(8), sem(8), sem(2), sem(2), sem(7), sem(6),
     ]
     vmem = pl.BlockSpec(memory_space=pltpu.VMEM)
     anywhere = pl.BlockSpec(memory_space=pl.ANY)

time: 86.5 us -> 86.3 us (level)
  no operation moved by 1% of the time
where the time goes in v7:
time: 86.3 us; the launch traced here: 86.1 us
  Pallas kernels  85.3 us (99%)
    pallas_call x1, Pallas kernels, on_device_fast(): pl.pallas_call(whole_layer, out_shape=shapes, in_specs=[pl.BlockSpec(memo...  82 us
    pallas_call x1, Pallas kernels, on_device_fast(): pl.pallas_call(hand_on, out_shape=[jax.ShapeDtypeStruct(a.shape, a.dtype)...  3.27 us

profile of v7, /device:TPU:0, one launch (start us, length us, event | category | flops | bytes accessed | tf_op | source)
XLA Modules:
  0.0 86.1 jit_solution(17413170213452465549)
XLA Ops:
  0.6 82.0 %shard_map.152 = (bf16[64,768]{1,0:T(8,128)(2,1)}, f32[64,768]{1,0:T(8,128)}, f32[8,128]{1,0:T(8,128)}, f32[3,48,384]{2,1,0:T(8,128)}, f32[48,384]{1,0:T(8,128)}...) custom-call(s32[3]{0:T(128)} %refs_0_.1, bf16[1,24]{1,0:T(2,128)(2,1)} %bitcast.13, bf16[1,24]{1,0:T(2,128)(2,1)} %bitcast.14, ...), custom_call_target="tpu_custom_call" | custom-call | tf_op jit(solution)/shard_map/pallas_call | solution.py:1211
  82.7 3.3 %shard_map.153 = (bf16[64,768]{1,0:T(8,128)(2,1)}, f32[64,768]{1,0:T(8,128)}, f32[3,48,384]{2,1,0:T(8,128)}, f32[48,384]{1,0:T(8,128)}, f32[48,2,576]{2,1,0:T(2,...) custom-call(bf16[64,768]{1,0:T(8,128)(2,1)} %get-tuple-element.23.refs_0_, ...), custom_call_target="tpu_custom_call" | custom-call | tf_op jit(solution)/shard_map/pallas_call | solution.py:1224

commit v8 on v7

--- a/solution.py
+++ b/solution.py
@@ -830,6 +830,7 @@
     ms[0] = dot_nt(grad_gate_up, w_in).astype(LOW).reshape(2, 2, 64, 768)
     for k, (kx, ky) in enumerate(group):
         push(ms.at[0, flip(x, kx), flip(y, ky)], ms_d.at[k], s_g.at[3 + k], r_g.at[3 + k], member(kx, ky))
+    halve(1, dot_nt(hidden, w_down))
     h2_t = turned(h2).astype(LOW)
     gf[:, :, :, :, 0:576] = dot(h2_t, grad_gate_up).astype(LOW).reshape(4, 2, 2, 48, 576)
     g_t = turned(grad_out).astype(LOW)
@@ -931,7 +932,6 @@
             later[name]()
 
     ff_sums[0]()
-    halve(1, dot_nt(hidden, w_down))
     run_later(0)
     own_res = res[x, y]
     unit_two, scale_two = centred_norm(own_res)

time: 86.3 us -> 86.3 us (level)
  no operation moved by 1% of the time
where the time goes in v8:
time: 86.3 us; the launch traced here: 86.1 us
  Pallas kernels  85.3 us (99%)
    pallas_call x1, Pallas kernels, on_device_fast(): pl.pallas_call(whole_layer, out_shape=shapes, in_specs=[pl.BlockSpec(memo...  82 us
    pallas_call x1, Pallas kernels, on_device_fast(): pl.pallas_call(hand_on, out_shape=[jax.ShapeDtypeStruct(a.shape, a.dtype)...  3.27 us

profile of v8, /device:TPU:0, one launch (start us, length us, event | category | flops | bytes accessed | tf_op | source)
XLA Modules:
  0.0 86.1 jit_solution(14586411652842058713)
XLA Ops:
  0.6 82.0 %shard_map.152 = (bf16[64,768]{1,0:T(8,128)(2,1)}, f32[64,768]{1,0:T(8,128)}, f32[8,128]{1,0:T(8,128)}, f32[3,48,384]{2,1,0:T(8,128)}, f32[48,384]{1,0:T(8,128)}...) custom-call(s32[3]{0:T(128)} %refs_0_.1, bf16[1,24]{1,0:T(2,128)(2,1)} %bitcast.13, bf16[1,24]{1,0:T(2,128)(2,1)} %bitcast.14, ...), custom_call_target="tpu_custom_call" | custom-call | tf_op jit(solution)/shard_map/pallas_call | solution.py:1211
  82.7 3.3 %shard_map.153 = (bf16[64,768]{1,0:T(8,128)(2,1)}, f32[64,768]{1,0:T(8,128)}, f32[3,48,384]{2,1,0:T(8,128)}, f32[48,384]{1,0:T(8,128)}, f32[48,2,576]{2,1,0:T(2,...) custom-call(bf16[64,768]{1,0:T(8,128)(2,1)} %get-tuple-element.23.refs_0_, ...), custom_call_target="tpu_custom_call" | custom-call | tf_op jit(solution)/shard_map/pallas_call | solution.py:1224
